TPU v7x, 32 devices: a whole 2x2x4 slice. The times are simulated.
32 devices in a mesh: across: 2 (over y), along: 16 (over z, x, core).
Axes of the slice: x: 2, y: 2, z: 4, core: 2. Of those that a mesh axis runs over, the one named last changes fastest.
Arguments:
- retard: bfloat16 [256, 2048], P('across', 'along'), may hold values from -0.0078125 to 0.0078125
- cotangent: bfloat16 [8, 256, 2048], P(None, 'across', 'along'), may hold values from -6 to 6
- filters: bfloat16 [8, 128, 128], replicated, may hold values from -0.015625 to 0.015625
Outputs:
- grad_input: float32 [256, 2048], P('across', 'along')
- grad_filters: float32 [8, 128, 128], replicated
All inputs are finite; a program needn't handle non-finite values.
Results may differ from a plain program's by a relative error of at most 0.0003.
Values may be sent and summed in bfloat16 or wider, within the bound.
No kernel may reach another device: no remote copies, remote signals or barrier semaphores. Data moves between devices by JAX's collectives and lax.ppermute only.
A program may use at most 64 MiB of HBM per device.

v0:
```python
import functools
import math

import jax
import jax.numpy as jnp
import numpy as np
from jax import lax
from jax.experimental import pallas as pl
from jax.experimental.pallas import tpu as pltpu
from jax.sharding import PartitionSpec as P

AXES = ("across", "along")
f32 = jnp.float32
bf16 = jnp.bfloat16


def halves(table):
    upper = table.astype(np.float32).astype(jnp.bfloat16)
    lower = (table - upper.astype(np.float64)).astype(np.float32).astype(jnp.bfloat16)
    return upper, lower


def tables(radius):
    period = 2 * radius
    freq = np.arange(radius)[:, None] + 0.5

    def turn(position):
        angle = 2.0 * math.pi / period * freq * position[None, :]
        return np.cos(angle), np.sin(angle)

    near = np.arange(radius)
    wide = (np.arange(period) + radius // 2) % period
    out = {}
    cos_n, sin_n = turn(near)
    cos_w, sin_w = turn(wide)
    hi, lo = halves(np.concatenate([cos_n, sin_n], axis=0))
    out["rows_near"] = np.concatenate([hi, lo], axis=1)
    hi, lo = halves(np.concatenate([cos_n, -sin_n], axis=0).T)
    out["cols_near"] = np.concatenate([hi, hi, lo], axis=0)
    hi, lo = halves(np.concatenate([cos_w, sin_w], axis=0))
    out["rows_wide"] = np.concatenate([hi, lo], axis=1)
    hi, lo = halves(np.concatenate([cos_w, -sin_w], axis=0).T)
    out["cols_wide"] = np.concatenate([hi, hi, lo], axis=0)
    scale = 2.0 / period**2
    hi, lo = halves(np.concatenate([cos_n, sin_n], axis=0).T)
    out["back_rows_near"] = np.concatenate([hi, lo], axis=0)
    hi, lo = halves(np.concatenate([cos_n, -sin_n], axis=0) * scale)
    out["back_cols_near"] = np.concatenate([hi, lo], axis=1)
    hi, lo = halves(np.concatenate([cos_w, sin_w], axis=0).T)
    out["back_rows_wide"] = np.concatenate([hi, lo], axis=0)
    hi, lo = halves(np.concatenate([cos_w, -sin_w], axis=0) * scale)
    out["back_cols_wide"] = np.concatenate([hi, lo], axis=1)
    return out


def dot(a, b):
    return jnp.dot(a, b, preferred_element_type=f32)


def split(x):
    upper = x.astype(bf16)
    return upper, (x - upper.astype(f32)).astype(bf16)


def butterfly(mixed, radius):
    cr, ci = mixed[:radius, :radius], mixed[:radius, radius:]
    sr, si = mixed[radius:, :radius], mixed[radius:, radius:]
    return (cr + si, ci - sr), (cr - si, ci + sr)


def near_spectra(first, second, rows, cols, radius):
    pair = jnp.concatenate([first, second], axis=1)
    mixed = dot(rows, jnp.concatenate([pair, pair], axis=0))
    result = []
    for part in (mixed[:, :radius], mixed[:, radius:]):
        hi, lo = split(part)
        result.append(butterfly(dot(jnp.concatenate([hi, lo, hi], axis=1), cols), radius))
    return result


def inverse(plus, minus, rows, cols):
    (pr, pi), (mr, mi) = plus, minus
    mixed = jnp.concatenate(
        [
            jnp.concatenate([pr + mr, pi + mi], axis=1),
            jnp.concatenate([mi - pi, pr - mr], axis=1),
        ],
        axis=0,
    )
    count = rows.shape[0] // 2
    hi, lo = split(mixed)
    both = dot(rows, hi)
    part = both[:count] + both[count:] + dot(rows[:count], lo)
    width = cols.shape[1] // 2
    hi, lo = split(part)
    both = dot(hi, cols)
    return both[:, :width] + both[:, width:] + dot(lo, cols[:, :width])


def cotangent_kernel(cot_ref, rows_ref, cols_ref, out_ref):
    count, radius = cot_ref.shape[0], cot_ref.shape[1]
    for f in range(0, count, 2):
        spectra = near_spectra(cot_ref[f], cot_ref[f + 1], rows_ref[...], cols_ref[...], radius)
        for g, (plus, minus) in enumerate(spectra):
            out_ref[f + g, 0] = plus[0]
            out_ref[f + g, 1] = plus[1]
            out_ref[f + g, 2] = minus[0]
            out_ref[f + g, 3] = minus[1]


def row_pick(shape, start):
    row = lax.broadcasted_iota(jnp.int32, shape, 0)
    return row < shape[0] // 2 if start else row >= shape[0] // 2


def filters_kernel(two, place_ref, spec_ref, own_ref, *rest):
    pieces, (rows_w, cols_w, rows_b, cols_b, keep_ref, send_ref) = rest[:-6], rest[-6:]
    radius = own_ref.shape[0]
    shape = (radius, radius)
    low_row = lax.broadcasted_iota(jnp.int32, shape, 0) < radius // 2
    low_col = lax.broadcasted_iota(jnp.int32, shape, 1) < radius // 2
    zero = jnp.zeros(shape, f32)
    got = [p[...].astype(f32) for p in pieces]
    left, right = got[:2]
    side = jnp.where(low_col, right, left)
    if two:
        mid, diag_left, diag_right = got[2:]
        use = low_row == (place_ref[2] == 0)
        below = jnp.where(use, mid, zero)
        corner = jnp.where(use, jnp.where(low_col, diag_right, diag_left), zero)
    else:
        up, up_left, up_right, down, down_left, down_right = got[2:]
        below = jnp.where(low_row, down, up)
        corner = jnp.where(
            low_row,
            jnp.where(low_col, down_right, down_left),
            jnp.where(low_col, up_right, up_left),
        )
    window = jnp.concatenate(
        [
            jnp.concatenate([own_ref[...], side.astype(bf16)], axis=1),
            jnp.concatenate([below.astype(bf16), corner.astype(bf16)], axis=1),
        ],
        axis=0,
    )
    mixed = dot(rows_w[...], jnp.concatenate([window, window], axis=0))
    hi, lo = split(mixed)
    mixed = dot(jnp.concatenate([hi, lo, hi], axis=1), cols_w[...])
    (ar, ai), (br, bi) = butterfly(mixed, radius)
    core, quarter = place_ref[0], place_ref[1]
    for slot in range(8):
        half = core if slot < 4 else 1 - core
        f = 4 * half + (quarter ^ (slot % 4))
        pr, pi, mr, mi = spec_ref[f, 0], spec_ref[f, 1], spec_ref[f, 2], spec_ref[f, 3]
        plus = (pr * ar + pi * ai, pr * ai - pi * ar)
        minus = (mr * br + mi * bi, mr * bi - mi * br)
        value = inverse(plus, minus, rows_b[...], cols_b[...])
        if slot < 4:
            keep_ref[slot] = value
        else:
            send_ref[slot - 4] = value


def input_kernel(two, place_ref, spec_ref, filt_ref, rows_ref, cols_ref, rows_b, cols_b, *outs):
    count, radius = filt_ref.shape[0], filt_ref.shape[1]
    total = None
    for f in range(0, count, 2):
        spectra = near_spectra(filt_ref[f], filt_ref[f + 1], rows_ref[...], cols_ref[...], radius)
        for g, ((ar, ai), (br, bi)) in enumerate(spectra):
            pr, pi, mr, mi = (spec_ref[f + g, c] for c in range(4))
            term = (pr * ar - pi * ai, pr * ai + pi * ar, mr * br - mi * bi, mr * bi + mi * br)
            total = term if total is None else tuple(t + u for t, u in zip(total, term))
    full = inverse(total[:2], total[2:], rows_b[...], cols_b[...])
    own_ref, side_ref, below_ref, corner_ref = outs
    own_ref[...] = full[:radius, :radius]
    side_ref[...] = full[:radius, radius:]
    below, corner = full[radius:, :radius], full[radius:, radius:]
    if two:
        half = radius // 2
        first = place_ref[2] == 0
        below_ref[...] = jnp.where(first, below[:half], below[half:])
        corner_ref[...] = jnp.where(first, corner[:half], corner[half:])
    else:
        below_ref[...] = below
        corner_ref[...] = corner


def gather_kernel(place_ref, *refs):
    pieces, out_ref = refs[:8], refs[8]
    core, quarter = place_ref[0], place_ref[1]
    for slot in range(8):
        half = core if slot < 4 else 1 - core
        out_ref[4 * half + (quarter ^ (slot % 4))] = pieces[slot][...]


VMEM = pl.BlockSpec(memory_space=pltpu.VMEM)
SMEM = pl.BlockSpec(memory_space=pltpu.SMEM)
LIMIT = pltpu.CompilerParams(vmem_limit_bytes=32 * 1024 * 1024)


def local(table, across, along, retard, cotangent, filters):
    count, radius = filters.shape[0], filters.shape[1]
    two = across == 2
    block = jax.ShapeDtypeStruct((radius, radius), f32)
    row_index, col_index = lax.axis_index("across"), lax.axis_index("along")
    core = col_index & 1
    quarter = ((col_index >> 1) & 1) + 2 * (row_index & 1)
    place = jnp.stack([core, quarter, row_index]).astype(jnp.int32)

    def move(value, change):
        pairs = []
        for a in range(across):
            for b in range(along):
                c, d = change(a, b)
                if 0 <= c < across and 0 <= d < along:
                    pairs.append((a * along + b, c * along + d))
        return lax.ppermute(value, AXES, pairs)

    def around(side, below, corner):
        result = [move(side, lambda a, b: (a, b + 1)), move(side, lambda a, b: (a, b - 1))]
        if two:
            result.append(move(below, lambda a, b: (1 - a, b)))
            result.append(move(corner, lambda a, b: (1 - a, b + 1)))
            result.append(move(corner, lambda a, b: (1 - a, b - 1)))
        else:
            for s in (1, -1):
                result.append(move(below, lambda a, b: (a + s, b)))
                result.append(move(corner, lambda a, b: (a + s, b + 1)))
                result.append(move(corner, lambda a, b: (a + s, b - 1)))
        return result

    pieces = around(retard, retard, retard)
    spectra = pl.pallas_call(
        cotangent_kernel,
        out_shape=jax.ShapeDtypeStruct((count, 4, radius, radius), f32),
        in_specs=[VMEM] * 3,
        out_specs=VMEM,
        compiler_params=LIMIT,
        name="cotangent_spectra",
    )(cotangent, table["rows_near"], table["cols_near"])
    half = jax.ShapeDtypeStruct((count // 2, radius, radius), f32)
    keep, send = pl.pallas_call(
        functools.partial(filters_kernel, two),
        out_shape=(half, half),
        in_specs=[SMEM] + [VMEM] * (6 + len(pieces)),
        out_specs=(VMEM, VMEM),
        compiler_params=LIMIT,
        name="grad_filters",
    )(
        place,
        spectra,
        retard,
        *pieces,
        table["rows_wide"],
        table["cols_wide"],
        table["back_rows_near"],
        table["back_cols_near"],
    )
    strip = jax.ShapeDtypeStruct((radius // 2, radius), f32) if two else block
    own, side, below, corner = pl.pallas_call(
        functools.partial(input_kernel, two),
        out_shape=(block, block, strip, strip),
        in_specs=[SMEM] + [VMEM] * 6,
        out_specs=(VMEM,) * 4,
        compiler_params=LIMIT,
        name="grad_input",
    )(
        place,
        spectra,
        filters,
        table["rows_near"],
        table["cols_near"],
        table["back_rows_wide"],
        table["back_cols_wide"],
    )

    got = move(send, lambda a, b: (a, b ^ 1))
    mine = [keep[n] + got[n] for n in range(4)]
    flips = [lambda a, b, n=n: (a ^ (n >> 1), b ^ ((n & 1) << 1)) for n in range(4)]
    value = mine[0] + sum(move(mine[n], flips[n]) for n in range(1, 4))
    bits = [(0, 1 << s) for s in range(2, (along - 1).bit_length())]
    bits += [(1 << s, 0) for s in range(1, (across - 1).bit_length())]
    for start in range(0, len(bits), 2):
        group = bits[start : start + 2]
        masks = group + ([tuple(p ^ q for p, q in zip(*group))] if len(group) == 2 else [])
        value = value + sum(
            move(value, lambda a, b, m=m: (a ^ m[0], b ^ m[1])) for m in masks
        )
    parts = [value] + [move(value, flips[n]) for n in range(1, 4)]
    parts += [move(part, lambda a, b: (a, b ^ 1)) for part in parts]
    grad_filters = pl.pallas_call(
        gather_kernel,
        out_shape=jax.ShapeDtypeStruct((count, radius, radius), f32),
        in_specs=[SMEM] + [VMEM] * 8,
        out_specs=VMEM,
        compiler_params=LIMIT,
        name="gather_filters",
    )(place, *parts)

    low_row = lax.broadcasted_iota(jnp.int32, (radius, radius), 0) < radius // 2
    low_col = lax.broadcasted_iota(jnp.int32, (radius, radius), 1) < radius // 2
    got = around(side, below, corner)
    grad_input = own + jnp.where(low_col, got[0], got[1])
    if two:
        strip = got[2] + jnp.where(low_col[: radius // 2], got[3], got[4])
        strip = jnp.concatenate([strip, strip], axis=0)
        grad_input = grad_input + jnp.where(low_row == (row_index == 1), strip, 0.0)
    else:
        above = got[2] + jnp.where(low_col, got[3], got[4])
        under = got[5] + jnp.where(low_col, got[6], got[7])
        grad_input = grad_input + jnp.where(low_row, above, under)
    return grad_input, grad_filters


def solution(mesh):
    across, along = mesh.shape["across"], mesh.shape["along"]

    def whole(retard, cotangent, filters):
        table = {k: jnp.asarray(v) for k, v in tables(filters.shape[1]).items()}
        return jax.shard_map(
            functools.partial(local, table, across, along),
            mesh=mesh,
            in_specs=(P("across", "along"), P(None, "across", "along"), P()),
            out_specs=(P("across", "along"), P()),
            check_vma=False,
        )(retard, cotangent, filters)

    return whole
```

profile of v0, /device:TPU:0, one launch (start us, length us, event | category | flops | bytes accessed | tf_op | source)
XLA Modules:
  0.0 65.4 jit_solution(6900251016389487485)
XLA Ops:
  0.6 2.4 %collective-permute-start.5 = (bf16[128,128]{1,0:T(8,128)(2,1)}, bf16[128,128]{1,0:T(8,128)(2,1)S(1)}, u32[]{:S(2)}, u32[]{:S(2)}) collective-permute-start(bf16[128,128]{1,0:T(8,128)(2,1)} %own_ref.1), channel_id=1, source_target_pairs={{0,1},{1,2},{2,3},{3,4},{4,5},{5,6},{6,7},{7,8},{8,9},{9,10},{10,1... | collective-permute-start | bytes 98312 | tf_op jit(solution)/shard_map/ppermute | solution.py:217
  3.0 1.3 %collective-permute-start.6 = (bf16[128,128]{1,0:T(8,128)(2,1)}, bf16[128,128]{1,0:T(8,128)(2,1)S(1)}, u32[]{:S(2)}, u32[]{:S(2)}) collective-permute-start(bf16[128,128]{1,0:T(8,128)(2,1)} %own_ref.1), channel_id=1, source_target_pairs={{1,0},{2,1},{3,2},{4,3},{5,4},{6,5},{7,6},{8,7},{9,8},{10,9},{11,1... | collective-permute-start | bytes 98312 | tf_op jit(solution)/shard_map/ppermute | solution.py:217
  4.3 2.4 %collective-permute-start.7 = (bf16[128,128]{1,0:T(8,128)(2,1)}, bf16[128,128]{1,0:T(8,128)(2,1)S(1)}, u32[]{:S(2)}, u32[]{:S(2)}) collective-permute-start(bf16[128,128]{1,0:T(8,128)(2,1)} %own_ref.1), channel_id=1, source_target_pairs={{0,16},{1,17},{2,18},{3,19},{4,20},{5,21},{6,22},{7,23},{8,24},{9,... | collective-permute-start | bytes 98312 | tf_op jit(solution)/shard_map/ppermute | solution.py:217
  6.7 4.1 %collective-permute-start.8 = (bf16[128,128]{1,0:T(8,128)(2,1)}, bf16[128,128]{1,0:T(8,128)(2,1)S(1)}, u32[]{:S(2)}, u32[]{:S(2)}) collective-permute-start(bf16[128,128]{1,0:T(8,128)(2,1)} %own_ref.1), channel_id=1, source_target_pairs={{0,17},{1,18},{2,19},{3,20},{4,21},{5,22},{6,23},{7,24},{8,25},{9,... | collective-permute-start | bytes 98312 | tf_op jit(solution)/shard_map/ppermute | solution.py:217
  10.9 1.3 %collective-permute-start.9 = (bf16[128,128]{1,0:T(8,128)(2,1)}, bf16[128,128]{1,0:T(8,128)(2,1)S(1)}, u32[]{:S(2)}, u32[]{:S(2)}) collective-permute-start(bf16[128,128]{1,0:T(8,128)(2,1)} %own_ref.1), channel_id=1, source_target_pairs={{1,16},{2,17},{3,18},{4,19},{5,20},{6,21},{7,22},{8,23},{9,24},{10... | collective-permute-start | bytes 98312 | tf_op jit(solution)/shard_map/ppermute | solution.py:217
  15.0 1.3 %cotangent_spectra.1.spec_ref = f32[8,4,128,128]{3,2,1,0:T(8,128)S(1)} custom-call(bf16[8,128,128]{2,1,0:T(8,128)(2,1)S(1)} %copy-done.3, bf16[256,256]{1,0:T(8,128)(2,1)S(1)} %copy-done.1, bf16[384,256]{1,0:T(8,128)(2,1)S(1)} %copy-done), custom_call_target="tpu_custom_call" | custom-call | tf_op jit(solution)/shard_map/cotangent_spectra/pallas_call | solution.py:233
  16.4 1.1 %collective-permute-done.9.rest_4_ = bf16[128,128]{1,0:T(8,128)(2,1)S(1)} collective-permute-done((bf16[128,128]{1,0:T(8,128)(2,1)}, bf16[128,128]{1,0:T(8,128)(2,1)S(1)}, u32[]{:S(2)}, u32[]{:S(2)}) %collective-permute-start.9) | collective-permute-done | bytes 32800 | tf_op jit(solution)/shard_map/ppermute | solution.py:217
  17.6 3.3 %grad_filters.1 = (f32[4,128,128]{2,1,0:T(8,128)S(1)}, f32[4,128,128]{2,1,0:T(8,128)S(1)}) custom-call(s32[3]{0:T(128)S(1)} %pad_add_fusion.place_ref, f32[8,4,128,128]{3,2,1,0:T(8,128)S(1)} %cotangent_spectra.1.spec_ref, bf16[128,128]{1,0:T(8,128)(2,1)S(1)} %copy-done.10, bf16[128,128]{1,0:T(8,128)(2,1)S(1)} %collective-permute-done.5.rest_0_, ...), custom_call_target="tpu_custom_call" | custom-call | tf_op jit(solution)/shard_map/grad_filters/pallas_call | solution.py:242
  20.9 1.6 %collective-permute-start.10 = (f32[4,128,128]{2,1,0:T(8,128)S(1)}, f32[4,128,128]{2,1,0:T(8,128)S(1)}, u32[]{:S(2)}, u32[]{:S(2)}) collective-permute-start(f32[4,128,128]{2,1,0:T(8,128)S(1)} %get-tuple-element.13), channel_id=1, source_target_pairs={{0,1},{1,0},{2,3},{3,2},{4,5},{5,4},{6,7},{7,6},{8,9},{9,8},{10,11... | collective-permute-start | bytes 786440 | tf_op jit(solution)/shard_map/ppermute | solution.py:217
  22.5 1.2 %collective-permute-done.10 = f32[4,128,128]{2,1,0:T(8,128)S(1)} collective-permute-done((f32[4,128,128]{2,1,0:T(8,128)S(1)}, f32[4,128,128]{2,1,0:T(8,128)S(1)}, u32[]{:S(2)}, u32[]{:S(2)}) %collective-permute-start.10) | collective-permute-done | bytes 262176 | tf_op jit(solution)/shard_map/ppermute | solution.py:217
  23.7 4.4 %collective-permute-start.13 = (f32[128,128]{1,0:T(8,128)S(1)}, f32[128,128]{1,0:T(8,128)S(1)}, u32[]{:S(2)}, u32[]{:S(2)}) collective-permute-start(f32[128,128]{1,0:T(8,128)S(1)} %get-tuple-element.15), channel_id=1, source_target_pairs={{0,18},{1,19},{2,16},{3,17},{4,22},{5,23},{6,20},{7,21},{8,26},{9,... | collective-permute-start | bytes 196616 | tf_op jit(solution)/shard_map/ppermute | solution.py:217
  28.7 2.6 %grad_input.1 = (f32[128,128]{1,0:T(8,128)S(1)}, f32[128,128]{1,0:T(8,128)S(1)}, f32[64,128]{1,0:T(8,128)S(1)}, f32[64,128]{1,0:T(8,128)S(1)}) custom-call(s32[3]{0:T(128)S(1)} %pad_add_fusion.place_ref, f32[8,4,128,128]{3,2,1,0:T(8,128)S(1)} %cotangent_spectra.1.spec_ref, bf16[8,128,128]{2,1,0:T(8,128)(2,1)S(1)} %copy-done.4, ...), custom_call_target="tpu_custom_call" | custom-call | tf_op jit(solution)/shard_map/grad_input/pallas_call | solution.py:260
  31.3 2.7 %collective-permute-start.3 = (f32[64,128]{1,0:T(8,128)S(1)}, f32[64,128]{1,0:T(8,128)S(1)}, u32[]{:S(2)}, u32[]{:S(2)}) collective-permute-start(f32[64,128]{1,0:T(8,128)S(1)} %get-tuple-element.11), channel_id=1, source_target_pairs={{0,17},{1,18},{2,19},{3,20},{4,21},{5,22},{6,23},{7,24},{8,25},{9,... | collective-permute-start | bytes 98312 | tf_op jit(solution)/shard_map/ppermute | solution.py:217
  34.0 1.3 %collective-permute-start.4 = (f32[64,128]{1,0:T(8,128)S(1)}, f32[64,128]{1,0:T(8,128)S(1)}, u32[]{:S(2)}, u32[]{:S(2)}) collective-permute-start(f32[64,128]{1,0:T(8,128)S(1)} %get-tuple-element.11), channel_id=1, source_target_pairs={{1,16},{2,17},{3,18},{4,19},{5,20},{6,21},{7,22},{8,23},{9,24},{10... | collective-permute-start | bytes 98312 | tf_op jit(solution)/shard_map/ppermute | solution.py:217
  35.4 8.7 %collective-permute-start.16 = (f32[128,128]{1,0:T(8,128)S(1)}, f32[128,128]{1,0:T(8,128)S(1)}, u32[]{:S(2)}, u32[]{:S(2)}) collective-permute-start(f32[128,128]{1,0:T(8,128)S(1)} %fusion.4), channel_id=1, source_target_pairs={{0,12},{1,13},{2,14},{3,15},{4,8},{5,9},{6,10},{7,11},{8,4},{9,5},... | collective-permute-start | bytes 196616 | tf_op jit(solution)/shard_map/ppermute | solution.py:217
  44.8 2.5 %collective-permute-done.16 = f32[128,128]{1,0:T(8,128)S(1)} collective-permute-done((f32[128,128]{1,0:T(8,128)S(1)}, f32[128,128]{1,0:T(8,128)S(1)}, u32[]{:S(2)}, u32[]{:S(2)}) %collective-permute-start.16) | collective-permute-done | bytes 65568 | tf_op jit(solution)/shard_map/ppermute | solution.py:217
  47.3 1.3 %collective-permute-start = (f32[128,128]{1,0:T(8,128)S(1)}, f32[128,128]{1,0:T(8,128)S(1)}, u32[]{:S(2)}, u32[]{:S(2)}) collective-permute-start(f32[128,128]{1,0:T(8,128)S(1)} %get-tuple-element.9), channel_id=1, source_target_pairs={{0,1},{1,2},{2,3},{3,4},{4,5},{5,6},{6,7},{7,8},{8,9},{9,10},{10,1... | collective-permute-start | bytes 196616 | tf_op jit(solution)/shard_map/ppermute | solution.py:217
  48.6 1.3 %collective-permute-start.1 = (f32[128,128]{1,0:T(8,128)S(1)}, f32[128,128]{1,0:T(8,128)S(1)}, u32[]{:S(2)}, u32[]{:S(2)}) collective-permute-start(f32[128,128]{1,0:T(8,128)S(1)} %get-tuple-element.9), channel_id=1, source_target_pairs={{1,0},{2,1},{3,2},{4,3},{5,4},{6,5},{7,6},{8,7},{9,8},{10,9},{11,1... | collective-permute-start | bytes 196616 | tf_op jit(solution)/shard_map/ppermute | solution.py:217
  50.3 3.8 %collective-permute-done.2 = f32[64,128]{1,0:T(8,128)S(1)} collective-permute-done((f32[64,128]{1,0:T(8,128)S(1)}, f32[64,128]{1,0:T(8,128)S(1)}, u32[]{:S(2)}, u32[]{:S(2)}) %collective-permute-start.2) | collective-permute-done | bytes 32800 | tf_op jit(solution)/shard_map/ppermute | solution.py:217
  54.1 2.1 %collective-permute-start.17 = (f32[128,128]{1,0:T(8,128)S(1)}, f32[128,128]{1,0:T(8,128)S(1)}, u32[]{:S(2)}, u32[]{:S(2)}) collective-permute-start(f32[128,128]{1,0:T(8,128)S(1)} %add_add_fusion.refs_0_), channel_id=1, source_target_pairs={{0,2},{1,3},{2,0},{3,1},{4,6},{5,7},{6,4},{7,5},{8,10},{9,11},{10,... | collective-permute-start | bytes 196616 | tf_op jit(solution)/shard_map/ppermute | solution.py:217
  56.1 1.5 %collective-permute-start.18 = (f32[128,128]{1,0:T(8,128)S(1)}, f32[128,128]{1,0:T(8,128)S(1)}, u32[]{:S(2)}, u32[]{:S(2)}) collective-permute-start(f32[128,128]{1,0:T(8,128)S(1)} %add_add_fusion.refs_0_), channel_id=1, source_target_pairs={{0,16},{1,17},{2,18},{3,19},{4,20},{5,21},{6,22},{7,23},{8,24},{9,... | collective-permute-start | bytes 196616 | tf_op jit(solution)/shard_map/ppermute | solution.py:217
  58.7 2.4 %collective-permute-done.18.refs_2_ = f32[128,128]{1,0:T(8,128)S(1)} collective-permute-done((f32[128,128]{1,0:T(8,128)S(1)}, f32[128,128]{1,0:T(8,128)S(1)}, u32[]{:S(2)}, u32[]{:S(2)}) %collective-permute-start.18) | collective-permute-done | bytes 65568 | tf_op jit(solution)/shard_map/ppermute | solution.py:217
  61.1 1.7 %collective-permute-done.19.refs_3_ = f32[128,128]{1,0:T(8,128)S(1)} collective-permute-done((f32[128,128]{1,0:T(8,128)S(1)}, f32[128,128]{1,0:T(8,128)S(1)}, u32[]{:S(2)}, u32[]{:S(2)}) %collective-permute-start.19) | collective-permute-done | bytes 65568 | tf_op jit(solution)/shard_map/ppermute | solution.py:217
  64.1 1.4 %gather_filters.1 = f32[8,128,128]{2,1,0:T(8,128)} custom-call(s32[3]{0:T(128)S(1)} %pad_add_fusion.place_ref, f32[128,128]{1,0:T(8,128)S(1)} %add_add_fusion.refs_0_, f32[128,128]{1,0:T(8,128)S(1)} %collective-permute-done.17.refs_1_, f32[128,128]{1,0:T(8,128)S(1)} %collective-permute-done.18.refs_2_, f32[128,128]{1,0:T(8,128)S(1)} %collective-permute-done.19.refs_3_, ...), custom_call_target="tpu_custom_call" | custom-call | tf_op jit(solution)/shard_map/gather_filters/pallas_call | solution.py:291
  (57 shorter events, 7.0 us)
Async XLA Ops:
  0.6 15.7 %collective-permute-start.5 = (bf16[128,128]{1,0:T(8,128)(2,1)}, bf16[128,128]{1,0:T(8,128)(2,1)S(1)}, u32[]{:S(2)}, u32[]{:S(2)}) collective-permute-start(bf16[128,128]{1,0:T(8,128)(2,1)} %own_ref.1), channel_id=1, source_target_pairs={{0,1},{1,2},{2,3},{3,4},{4,5},{5,6},{6,7},{7,8},{8,9},{9,10},{10,1... | collective-permute-start | bytes 98312 | tf_op jit(solution)/shard_map/ppermute | solution.py:217
  3.0 13.4 %collective-permute-start.6 = (bf16[128,128]{1,0:T(8,128)(2,1)}, bf16[128,128]{1,0:T(8,128)(2,1)S(1)}, u32[]{:S(2)}, u32[]{:S(2)}) collective-permute-start(bf16[128,128]{1,0:T(8,128)(2,1)} %own_ref.1), channel_id=1, source_target_pairs={{1,0},{2,1},{3,2},{4,3},{5,4},{6,5},{7,6},{8,7},{9,8},{10,9},{11,1... | collective-permute-start | bytes 98312 | tf_op jit(solution)/shard_map/ppermute | solution.py:217
  4.3 12.1 %collective-permute-start.7 = (bf16[128,128]{1,0:T(8,128)(2,1)}, bf16[128,128]{1,0:T(8,128)(2,1)S(1)}, u32[]{:S(2)}, u32[]{:S(2)}) collective-permute-start(bf16[128,128]{1,0:T(8,128)(2,1)} %own_ref.1), channel_id=1, source_target_pairs={{0,16},{1,17},{2,18},{3,19},{4,20},{5,21},{6,22},{7,23},{8,24},{9,... | collective-permute-start | bytes 98312 | tf_op jit(solution)/shard_map/ppermute | solution.py:217
  6.7 9.7 %collective-permute-start.8 = (bf16[128,128]{1,0:T(8,128)(2,1)}, bf16[128,128]{1,0:T(8,128)(2,1)S(1)}, u32[]{:S(2)}, u32[]{:S(2)}) collective-permute-start(bf16[128,128]{1,0:T(8,128)(2,1)} %own_ref.1), channel_id=1, source_target_pairs={{0,17},{1,18},{2,19},{3,20},{4,21},{5,22},{6,23},{7,24},{8,25},{9,... | collective-permute-start | bytes 98312 | tf_op jit(solution)/shard_map/ppermute | solution.py:217
  10.9 6.7 %collective-permute-start.9 = (bf16[128,128]{1,0:T(8,128)(2,1)}, bf16[128,128]{1,0:T(8,128)(2,1)S(1)}, u32[]{:S(2)}, u32[]{:S(2)}) collective-permute-start(bf16[128,128]{1,0:T(8,128)(2,1)} %own_ref.1), channel_id=1, source_target_pairs={{1,16},{2,17},{3,18},{4,19},{5,20},{6,21},{7,22},{8,23},{9,24},{10... | collective-permute-start | bytes 98312 | tf_op jit(solution)/shard_map/ppermute | solution.py:217
  20.9 2.7 %collective-permute-start.10 = (f32[4,128,128]{2,1,0:T(8,128)S(1)}, f32[4,128,128]{2,1,0:T(8,128)S(1)}, u32[]{:S(2)}, u32[]{:S(2)}) collective-permute-start(f32[4,128,128]{2,1,0:T(8,128)S(1)} %get-tuple-element.13), channel_id=1, source_target_pairs={{0,1},{1,0},{2,3},{3,2},{4,5},{5,4},{6,7},{7,6},{8,9},{9,8},{10,11... | collective-permute-start | bytes 786440 | tf_op jit(solution)/shard_map/ppermute | solution.py:217
  23.7 11.7 %collective-permute-start.13 = (f32[128,128]{1,0:T(8,128)S(1)}, f32[128,128]{1,0:T(8,128)S(1)}, u32[]{:S(2)}, u32[]{:S(2)}) collective-permute-start(f32[128,128]{1,0:T(8,128)S(1)} %get-tuple-element.15), channel_id=1, source_target_pairs={{0,18},{1,19},{2,16},{3,17},{4,22},{5,23},{6,20},{7,21},{8,26},{9,... | collective-permute-start | bytes 196616 | tf_op jit(solution)/shard_map/ppermute | solution.py:217
  28.1 7.3 %collective-permute-start.11 = (f32[128,128]{1,0:T(8,128)S(1)}, f32[128,128]{1,0:T(8,128)S(1)}, u32[]{:S(2)}, u32[]{:S(2)}) collective-permute-start(f32[128,128]{1,0:T(8,128)S(1)} %get-tuple-element.16), channel_id=1, source_target_pairs={{0,2},{1,3},{2,0},{3,1},{4,6},{5,7},{6,4},{7,5},{8,10},{9,11},{10,... | collective-permute-start | bytes 196616 | tf_op jit(solution)/shard_map/ppermute | solution.py:217
  28.1 7.3 %collective-permute-start.12 = (f32[128,128]{1,0:T(8,128)S(1)}, f32[128,128]{1,0:T(8,128)S(1)}, u32[]{:S(2)}, u32[]{:S(2)}) collective-permute-start(f32[128,128]{1,0:T(8,128)S(1)} %get-tuple-element.14), channel_id=1, source_target_pairs={{0,16},{1,17},{2,18},{3,19},{4,20},{5,21},{6,22},{7,23},{8,24},{9,... | collective-permute-start | bytes 196616 | tf_op jit(solution)/shard_map/ppermute | solution.py:217
  31.3 24.8 %collective-permute-start.3 = (f32[64,128]{1,0:T(8,128)S(1)}, f32[64,128]{1,0:T(8,128)S(1)}, u32[]{:S(2)}, u32[]{:S(2)}) collective-permute-start(f32[64,128]{1,0:T(8,128)S(1)} %get-tuple-element.11), channel_id=1, source_target_pairs={{0,17},{1,18},{2,19},{3,20},{4,21},{5,22},{6,23},{7,24},{8,25},{9,... | collective-permute-start | bytes 98312 | tf_op jit(solution)/shard_map/ppermute | solution.py:217
  34.0 23.6 %collective-permute-start.4 = (f32[64,128]{1,0:T(8,128)S(1)}, f32[64,128]{1,0:T(8,128)S(1)}, u32[]{:S(2)}, u32[]{:S(2)}) collective-permute-start(f32[64,128]{1,0:T(8,128)S(1)} %get-tuple-element.11), channel_id=1, source_target_pairs={{1,16},{2,17},{3,18},{4,19},{5,20},{6,21},{7,22},{8,23},{9,24},{10... | collective-permute-start | bytes 98312 | tf_op jit(solution)/shard_map/ppermute | solution.py:217
  35.4 11.9 %collective-permute-start.16 = (f32[128,128]{1,0:T(8,128)S(1)}, f32[128,128]{1,0:T(8,128)S(1)}, u32[]{:S(2)}, u32[]{:S(2)}) collective-permute-start(f32[128,128]{1,0:T(8,128)S(1)} %fusion.4), channel_id=1, source_target_pairs={{0,12},{1,13},{2,14},{3,15},{4,8},{5,9},{6,10},{7,11},{8,4},{9,5},... | collective-permute-start | bytes 196616 | tf_op jit(solution)/shard_map/ppermute | solution.py:217
  44.1 4.5 %collective-permute-start.14 = (f32[128,128]{1,0:T(8,128)S(1)}, f32[128,128]{1,0:T(8,128)S(1)}, u32[]{:S(2)}, u32[]{:S(2)}) collective-permute-start(f32[128,128]{1,0:T(8,128)S(1)} %fusion.4), channel_id=1, source_target_pairs={{0,4},{1,5},{2,6},{3,7},{4,0},{5,1},{6,2},{7,3},{8,12},{9,13},{10,... | collective-permute-start | bytes 196616 | tf_op jit(solution)/shard_map/ppermute | solution.py:217
  44.1 5.8 %collective-permute-start.15 = (f32[128,128]{1,0:T(8,128)S(1)}, f32[128,128]{1,0:T(8,128)S(1)}, u32[]{:S(2)}, u32[]{:S(2)}) collective-permute-start(f32[128,128]{1,0:T(8,128)S(1)} %fusion.4), channel_id=1, source_target_pairs={{0,8},{1,9},{2,10},{3,11},{4,12},{5,13},{6,14},{7,15},{8,0},{9,1},... | collective-permute-start | bytes 196616 | tf_op jit(solution)/shard_map/ppermute | solution.py:217
  47.3 10.4 %collective-permute-start = (f32[128,128]{1,0:T(8,128)S(1)}, f32[128,128]{1,0:T(8,128)S(1)}, u32[]{:S(2)}, u32[]{:S(2)}) collective-permute-start(f32[128,128]{1,0:T(8,128)S(1)} %get-tuple-element.9), channel_id=1, source_target_pairs={{0,1},{1,2},{2,3},{3,4},{4,5},{5,6},{6,7},{7,8},{8,9},{9,10},{10,1... | collective-permute-start | bytes 196616 | tf_op jit(solution)/shard_map/ppermute | solution.py:217
  48.6 14.2 %collective-permute-start.1 = (f32[128,128]{1,0:T(8,128)S(1)}, f32[128,128]{1,0:T(8,128)S(1)}, u32[]{:S(2)}, u32[]{:S(2)}) collective-permute-start(f32[128,128]{1,0:T(8,128)S(1)} %get-tuple-element.9), channel_id=1, source_target_pairs={{1,0},{2,1},{3,2},{4,3},{5,4},{6,5},{7,6},{8,7},{9,8},{10,9},{11,1... | collective-permute-start | bytes 196616 | tf_op jit(solution)/shard_map/ppermute | solution.py:217
  49.9 4.2 %collective-permute-start.2 = (f32[64,128]{1,0:T(8,128)S(1)}, f32[64,128]{1,0:T(8,128)S(1)}, u32[]{:S(2)}, u32[]{:S(2)}) collective-permute-start(f32[64,128]{1,0:T(8,128)S(1)} %get-tuple-element.10), channel_id=1, source_target_pairs={{0,16},{1,17},{2,18},{3,19},{4,20},{5,21},{6,22},{7,23},{8,24},{9,... | collective-permute-start | bytes 98312 | tf_op jit(solution)/shard_map/ppermute | solution.py:217
  54.1 4.7 %collective-permute-start.17 = (f32[128,128]{1,0:T(8,128)S(1)}, f32[128,128]{1,0:T(8,128)S(1)}, u32[]{:S(2)}, u32[]{:S(2)}) collective-permute-start(f32[128,128]{1,0:T(8,128)S(1)} %add_add_fusion.refs_0_), channel_id=1, source_target_pairs={{0,2},{1,3},{2,0},{3,1},{4,6},{5,7},{6,4},{7,5},{8,10},{9,11},{10,... | collective-permute-start | bytes 196616 | tf_op jit(solution)/shard_map/ppermute | solution.py:217
  56.1 5.0 %collective-permute-start.18 = (f32[128,128]{1,0:T(8,128)S(1)}, f32[128,128]{1,0:T(8,128)S(1)}, u32[]{:S(2)}, u32[]{:S(2)}) collective-permute-start(f32[128,128]{1,0:T(8,128)S(1)} %add_add_fusion.refs_0_), channel_id=1, source_target_pairs={{0,16},{1,17},{2,18},{3,19},{4,20},{5,21},{6,22},{7,23},{8,24},{9,... | collective-permute-start | bytes 196616 | tf_op jit(solution)/shard_map/ppermute | solution.py:217
  57.6 5.2 %collective-permute-start.19 = (f32[128,128]{1,0:T(8,128)S(1)}, f32[128,128]{1,0:T(8,128)S(1)}, u32[]{:S(2)}, u32[]{:S(2)}) collective-permute-start(f32[128,128]{1,0:T(8,128)S(1)} %add_add_fusion.refs_0_), channel_id=1, source_target_pairs={{0,18},{1,19},{2,16},{3,17},{4,22},{5,23},{6,20},{7,21},{8,26},{9,... | collective-permute-start | bytes 196616 | tf_op jit(solution)/shard_map/ppermute | solution.py:217
  57.7 5.9 %collective-permute-start.20 = (f32[128,128]{1,0:T(8,128)S(1)}, f32[128,128]{1,0:T(8,128)S(1)}, u32[]{:S(2)}, u32[]{:S(2)}) collective-permute-start(f32[128,128]{1,0:T(8,128)S(1)} %add_add_fusion.refs_0_), channel_id=1, source_target_pairs={{0,1},{1,0},{2,3},{3,2},{4,5},{5,4},{6,7},{7,6},{8,9},{9,8},{10,11... | collective-permute-start | bytes 196616 | tf_op jit(solution)/shard_map/ppermute | solution.py:217
  58.7 4.8 %collective-permute-start.21 = (f32[128,128]{1,0:T(8,128)S(1)}, f32[128,128]{1,0:T(8,128)S(1)}, u32[]{:S(2)}, u32[]{:S(2)}) collective-permute-start(f32[128,128]{1,0:T(8,128)S(1)} %collective-permute-done.17.refs_1_), channel_id=1, source_target_pairs={{0,1},{1,0},{2,3},{3,2},{4,5},{5,4},{6,7},{7,6},{8,9},{9,8},{10,11... | collective-permute-start | bytes 196616 | tf_op jit(solution)/shard_map/ppermute | solution.py:217
  61.1 2.5 %collective-permute-start.22 = (f32[128,128]{1,0:T(8,128)S(1)}, f32[128,128]{1,0:T(8,128)S(1)}, u32[]{:S(2)}, u32[]{:S(2)}) collective-permute-start(f32[128,128]{1,0:T(8,128)S(1)} %collective-permute-done.18.refs_2_), channel_id=1, source_target_pairs={{0,1},{1,0},{2,3},{3,2},{4,5},{5,4},{6,7},{7,6},{8,9},{9,8},{10,11... | collective-permute-start | bytes 196616 | tf_op jit(solution)/shard_map/ppermute | solution.py:217
  62.8 1.3 %collective-permute-start.23 = (f32[128,128]{1,0:T(8,128)S(1)}, f32[128,128]{1,0:T(8,128)S(1)}, u32[]{:S(2)}, u32[]{:S(2)}) collective-permute-start(f32[128,128]{1,0:T(8,128)S(1)} %collective-permute-done.19.refs_3_), channel_id=1, source_target_pairs={{0,1},{1,0},{2,3},{3,2},{4,5},{5,4},{6,7},{7,6},{8,9},{9,8},{10,11... | collective-permute-start | bytes 196616 | tf_op jit(solution)/shard_map/ppermute | solution.py:217
  (11 other events, 52.5 us)
where the time goes:
time: 65.8 us; the launch traced here: 65.4 us
  starting transfers between devices  38 us (58%)
  waiting for transfers between devices  14.2 us (22%)
  Pallas kernels  8.61 us (13%)
  local copies, waits for them, and re-layouts  2.82 us (4%)
  between operations  0.9 us (1%)
  other arithmetic  0.88 us (1%)
    ppermute x24, starting transfers between devices, move(): return lax.ppermute(value, AXES, pairs)  38 us
    ppermute x24, waiting for transfers between devices, move(): return lax.ppermute(value, AXES, pairs)  14.2 us
    pallas_call x1, Pallas kernels, local(): pl.pallas_call(functools.partial(filters_kernel, two), out_shape=(half, h...  3.34 us
    unnamed x22, local copies, waits for them, and re-layouts  2.82 us
    pallas_call x1, Pallas kernels, local(): pl.pallas_call(functools.partial(input_kernel, two), out_shape=(block, bl...  2.62 us
    pallas_call x1, Pallas kernels, local(): pl.pallas_call(gather_kernel, out_shape=jax.ShapeDtypeStruct((count, radi...  1.37 us
  transfers between devices with their start and end apart: 24, of which 8 were waited for; matrix products, arithmetic and copies ran while one was open for 1% of the time, Pallas kernels for 6%

commit v1 on v0

--- a/solution.py
+++ b/solution.py
@@ -97,7 +97,16 @@
     return both[:, :width] + both[:, width:] + dot(lo, cols[:, :width])
 
 
-def cotangent_kernel(cot_ref, rows_ref, cols_ref, out_ref):
+def cotangent_kernel(cot_hbm, rows_hbm, cols_hbm, out_ref, cot_ref, rows_ref, cols_ref, sems):
+    sources, targets = (cot_hbm, rows_hbm, cols_hbm), (cot_ref, rows_ref, cols_ref)
+    copies = [
+        pltpu.make_async_copy(source, target, sems.at[n])
+        for n, (source, target) in enumerate(zip(sources, targets))
+    ]
+    for copy in copies:
+        copy.start()
+    for copy in copies:
+        copy.wait()
     count, radius = cot_ref.shape[0], cot_ref.shape[1]
     for f in range(0, count, 2):
         spectra = near_spectra(cot_ref[f], cot_ref[f + 1], rows_ref[...], cols_ref[...], radius)
@@ -108,41 +117,39 @@
             out_ref[f + g, 3] = minus[1]
 
 
-def row_pick(shape, start):
-    row = lax.broadcasted_iota(jnp.int32, shape, 0)
-    return row < shape[0] // 2 if start else row >= shape[0] // 2
-
-
-def filters_kernel(two, place_ref, spec_ref, own_ref, *rest):
-    pieces, (rows_w, cols_w, rows_b, cols_b, keep_ref, send_ref) = rest[:-6], rest[-6:]
-    radius = own_ref.shape[0]
-    shape = (radius, radius)
-    low_row = lax.broadcasted_iota(jnp.int32, shape, 0) < radius // 2
-    low_col = lax.broadcasted_iota(jnp.int32, shape, 1) < radius // 2
+def window_of(own, pieces, place_ref):
+    shape = own.shape
+    row_edge, row_odd, col_edge, col_odd = (place_ref[n] for n in range(2, 6))
+    low_row = lax.broadcasted_iota(jnp.int32, shape, 0) < shape[0] // 2
+    low_col = lax.broadcasted_iota(jnp.int32, shape, 1) < shape[1] // 2
     zero = jnp.zeros(shape, f32)
     got = [p[...].astype(f32) for p in pieces]
-    left, right = got[:2]
-    side = jnp.where(low_col, right, left)
-    if two:
-        mid, diag_left, diag_right = got[2:]
-        use = low_row == (place_ref[2] == 0)
-        below = jnp.where(use, mid, zero)
-        corner = jnp.where(use, jnp.where(low_col, diag_right, diag_left), zero)
-    else:
-        up, up_left, up_right, down, down_left, down_right = got[2:]
-        below = jnp.where(low_row, down, up)
-        corner = jnp.where(
-            low_row,
-            jnp.where(low_col, down_right, down_left),
-            jnp.where(low_col, up_right, up_left),
-        )
-    window = jnp.concatenate(
+
+    def pick(near, far, low, odd, edge):
+        return jnp.where(low == (odd == 0), near, jnp.where(edge == 1, zero, far))
+
+    side = pick(got[0], got[1], low_col, col_odd, col_edge)
+    rows = []
+    for n in range(2, len(got), 3):
+        rows.append((got[n], pick(got[n + 1], got[n + 2], low_col, col_odd, col_edge)))
+    if len(rows) == 1:
+        rows.append((zero, zero))
+    below, corner = (
+        pick(near, far, low_row, row_odd, row_edge) for near, far in zip(rows[0], rows[1])
+    )
+    return jnp.concatenate(
         [
-            jnp.concatenate([own_ref[...], side.astype(bf16)], axis=1),
+            jnp.concatenate([own, side.astype(bf16)], axis=1),
             jnp.concatenate([below.astype(bf16), corner.astype(bf16)], axis=1),
         ],
         axis=0,
     )
+
+
+def filters_kernel(place_ref, spec_ref, own_ref, *rest):
+    pieces, (rows_w, cols_w, rows_b, cols_b, keep_ref, send_ref) = rest[:-6], rest[-6:]
+    radius = own_ref.shape[0]
+    window = window_of(own_ref[...], pieces, place_ref)
     mixed = dot(rows_w[...], jnp.concatenate([window, window], axis=0))
     hi, lo = split(mixed)
     mixed = dot(jnp.concatenate([hi, lo, hi], axis=1), cols_w[...])
@@ -161,7 +168,7 @@
             send_ref[slot - 4] = value
 
 
-def input_kernel(two, place_ref, spec_ref, filt_ref, rows_ref, cols_ref, rows_b, cols_b, *outs):
+def input_kernel(two, place_ref, spec_ref, filt_ref, rows_ref, cols_ref, rows_b, cols_b, own_ref, side_ref):
     count, radius = filt_ref.shape[0], filt_ref.shape[1]
     total = None
     for f in range(0, count, 2):
@@ -171,29 +178,33 @@
             term = (pr * ar - pi * ai, pr * ai + pi * ar, mr * br - mi * bi, mr * bi + mi * br)
             total = term if total is None else tuple(t + u for t, u in zip(total, term))
     full = inverse(total[:2], total[2:], rows_b[...], cols_b[...])
-    own_ref, side_ref, below_ref, corner_ref = outs
-    own_ref[...] = full[:radius, :radius]
-    side_ref[...] = full[:radius, radius:]
-    below, corner = full[radius:, :radius], full[radius:, radius:]
     if two:
         half = radius // 2
-        first = place_ref[2] == 0
-        below_ref[...] = jnp.where(first, below[:half], below[half:])
-        corner_ref[...] = jnp.where(first, corner[:half], corner[half:])
-    else:
-        below_ref[...] = below
-        corner_ref[...] = corner
-
-
-def gather_kernel(place_ref, *refs):
-    pieces, out_ref = refs[:8], refs[8]
-    core, quarter = place_ref[0], place_ref[1]
+        far = jnp.where(place_ref[3] == 0, full[radius : radius + half], full[radius + half :])
+        full = jnp.concatenate([full[:radius], far], axis=0)
+    own_ref[...] = full[:, :radius]
+    side_ref[...] = full[:, radius:]
+
+
+def gather_kernel(place_ref, own_ref, *refs):
+    pieces, strips, input_ref, out_ref = refs[:8], refs[8:-2], refs[-2], refs[-1]
+    core, quarter, row_edge, row_odd = (place_ref[n] for n in range(4))
     for slot in range(8):
         half = core if slot < 4 else 1 - core
         out_ref[4 * half + (quarter ^ (slot % 4))] = pieces[slot][...]
+    shape = own_ref.shape
+    low_row = lax.broadcasted_iota(jnp.int32, shape, 0) < shape[0] // 2
+    zero = jnp.zeros(shape, f32)
+    if len(strips) == 1:
+        strip = strips[0][...]
+        near, far = jnp.concatenate([strip, strip], axis=0), zero
+    else:
+        near, far = strips[0][...], jnp.where(row_edge == 1, zero, strips[1][...])
+    input_ref[...] = own_ref[...] + jnp.where(low_row == (row_odd == 1), near, far)
 
 
 VMEM = pl.BlockSpec(memory_space=pltpu.VMEM)
+HBM = pl.BlockSpec(memory_space=pltpu.HBM)
 SMEM = pl.BlockSpec(memory_space=pltpu.SMEM)
 LIMIT = pltpu.CompilerParams(vmem_limit_bytes=32 * 1024 * 1024)
 
@@ -203,44 +214,58 @@
     two = across == 2
     block = jax.ShapeDtypeStruct((radius, radius), f32)
     row_index, col_index = lax.axis_index("across"), lax.axis_index("along")
-    core = col_index & 1
-    quarter = ((col_index >> 1) & 1) + 2 * (row_index & 1)
-    place = jnp.stack([core, quarter, row_index]).astype(jnp.int32)
+    place = jnp.stack(
+        [
+            col_index & 1,
+            ((col_index >> 1) & 1) + 2 * (row_index & 1),
+            ((row_index == 0) | (row_index == across - 1)).astype(jnp.int32),
+            row_index & 1,
+            ((col_index == 0) | (col_index == along - 1)).astype(jnp.int32),
+            col_index & 1,
+        ]
+    ).astype(jnp.int32)
 
     def move(value, change):
         pairs = []
         for a in range(across):
             for b in range(along):
                 c, d = change(a, b)
-                if 0 <= c < across and 0 <= d < along:
-                    pairs.append((a * along + b, c * along + d))
+                pairs.append((a * along + b, c * along + d))
         return lax.ppermute(value, AXES, pairs)
 
-    def around(side, below, corner):
-        result = [move(side, lambda a, b: (a, b + 1)), move(side, lambda a, b: (a, b - 1))]
-        if two:
-            result.append(move(below, lambda a, b: (1 - a, b)))
-            result.append(move(corner, lambda a, b: (1 - a, b + 1)))
-            result.append(move(corner, lambda a, b: (1 - a, b - 1)))
-        else:
-            for s in (1, -1):
-                result.append(move(below, lambda a, b: (a + s, b)))
-                result.append(move(corner, lambda a, b: (a + s, b + 1)))
-                result.append(move(corner, lambda a, b: (a + s, b - 1)))
-        return result
-
-    pieces = around(retard, retard, retard)
+    def near(index, size):
+        return index ^ 1
+
+    def far(index, size):
+        other = ((index + 1) ^ 1) - 1
+        return other if 0 <= other < size else index
+
+    def stay(index, size):
+        return index
+
+    def to(row, col):
+        return lambda a, b: (row(a, across), col(b, along))
+
+    row_moves = (near,) if two else (near, far)
+    pieces = [move(retard, to(stay, near)), move(retard, to(stay, far))]
+    for row in row_moves:
+        pieces += [move(retard, to(row, col)) for col in (stay, near, far)]
     spectra = pl.pallas_call(
         cotangent_kernel,
         out_shape=jax.ShapeDtypeStruct((count, 4, radius, radius), f32),
-        in_specs=[VMEM] * 3,
+        in_specs=[HBM] * 3,
         out_specs=VMEM,
+        scratch_shapes=[
+            pltpu.VMEM(v.shape, bf16)
+            for v in (cotangent, table["rows_near"], table["cols_near"])
+        ]
+        + [pltpu.SemaphoreType.DMA((3,))],
         compiler_params=LIMIT,
         name="cotangent_spectra",
     )(cotangent, table["rows_near"], table["cols_near"])
     half = jax.ShapeDtypeStruct((count // 2, radius, radius), f32)
     keep, send = pl.pallas_call(
-        functools.partial(filters_kernel, two),
+        filters_kernel,
         out_shape=(half, half),
         in_specs=[SMEM] + [VMEM] * (6 + len(pieces)),
         out_specs=(VMEM, VMEM),
@@ -256,12 +281,12 @@
         table["back_rows_near"],
         table["back_cols_near"],
     )
-    strip = jax.ShapeDtypeStruct((radius // 2, radius), f32) if two else block
-    own, side, below, corner = pl.pallas_call(
+    tall = jax.ShapeDtypeStruct((2 * radius - (radius // 2 if two else 0), radius), f32)
+    own, side = pl.pallas_call(
         functools.partial(input_kernel, two),
-        out_shape=(block, block, strip, strip),
+        out_shape=(tall, tall),
         in_specs=[SMEM] + [VMEM] * 6,
-        out_specs=(VMEM,) * 4,
+        out_specs=(VMEM, VMEM),
         compiler_params=LIMIT,
         name="grad_input",
     )(
@@ -283,33 +308,26 @@
     for start in range(0, len(bits), 2):
         group = bits[start : start + 2]
         masks = group + ([tuple(p ^ q for p, q in zip(*group))] if len(group) == 2 else [])
+        if start == 0:
+            value, side = lax.optimization_barrier((value, side))
+            beside = [move(side, to(stay, col)) for col in (near, far)]
         value = value + sum(
             move(value, lambda a, b, m=m: (a ^ m[0], b ^ m[1])) for m in masks
         )
+    low_col = lax.broadcasted_iota(jnp.int32, tall.shape, 1) < radius // 2
+    other = jnp.where((col_index == 0) | (col_index == along - 1), 0.0, beside[1])
+    own = own + jnp.where(low_col == (col_index & 1 == 1), beside[0], other)
+    strips = [move(own[radius:], to(row, stay)) for row in row_moves]
     parts = [value] + [move(value, flips[n]) for n in range(1, 4)]
     parts += [move(part, lambda a, b: (a, b ^ 1)) for part in parts]
-    grad_filters = pl.pallas_call(
+    return pl.pallas_call(
         gather_kernel,
-        out_shape=jax.ShapeDtypeStruct((count, radius, radius), f32),
-        in_specs=[SMEM] + [VMEM] * 8,
-        out_specs=VMEM,
+        out_shape=(block, jax.ShapeDtypeStruct((count, radius, radius), f32)),
+        in_specs=[SMEM] + [VMEM] * (9 + len(strips)),
+        out_specs=(VMEM, VMEM),
         compiler_params=LIMIT,
         name="gather_filters",
-    )(place, *parts)
-
-    low_row = lax.broadcasted_iota(jnp.int32, (radius, radius), 0) < radius // 2
-    low_col = lax.broadcasted_iota(jnp.int32, (radius, radius), 1) < radius // 2
-    got = around(side, below, corner)
-    grad_input = own + jnp.where(low_col, got[0], got[1])
-    if two:
-        strip = got[2] + jnp.where(low_col[: radius // 2], got[3], got[4])
-        strip = jnp.concatenate([strip, strip], axis=0)
-        grad_input = grad_input + jnp.where(low_row == (row_index == 1), strip, 0.0)
-    else:
-        above = got[2] + jnp.where(low_col, got[3], got[4])
-        under = got[5] + jnp.where(low_col, got[6], got[7])
-        grad_input = grad_input + jnp.where(low_row, above, under)
-    return grad_input, grad_filters
+    )(place, own[:radius], *parts, *strips)
 
 
 def solution(mesh):

time: 65.8 us -> 51.5 us (0.78)
  starting transfers between devices: 38 us -> 24.1 us
  waiting for transfers between devices: 14.2 us -> 11.9 us
  local copies, waits for them, and re-layouts: 2.82 us -> 4.93 us
  other arithmetic: 0.88 us -> 0.08 us
  Pallas kernels: 8.61 us -> 9.28 us
    ppermute x24 -> x22, starting transfers between devices: 38 us -> 24.1 us  [move(): return lax.ppermute(value, AXES, pairs)]
    ppermute x24 -> x22, waiting for transfers between devices: 14.2 us -> 11.9 us  [move(): return lax.ppermute(value, AXES, pairs)]
    unnamed x22 -> x26, local copies, waits for them, and re-layouts: 2.82 us -> 4.83 us
    add x2 -> x1, other arithmetic: 0.73 us -> 0.02 us  [local(): own = own + jnp.where(low_col == (col_index & 1 == 1), beside[0], other)]
  transfers between devices with their start and end apart: 24 -> 22, of which waited for: 8 -> 9; matrix products, arithmetic and copies ran while one was open for 1% -> 0% of each run, Pallas kernels for 6% -> 8%
where the time goes in v1:
time: 51.5 us; the launch traced here: 51.1 us
  starting transfers between devices  24.1 us (47%)
  waiting for transfers between devices  11.9 us (23%)
  Pallas kernels  9.28 us (18%)
  local copies, waits for them, and re-layouts  4.93 us (10%)
  between operations  0.85 us (2%)
    ppermute x22, starting transfers between devices, move(): return lax.ppermute(value, AXES, pairs)  24.1 us
    ppermute x22, waiting for transfers between devices, move(): return lax.ppermute(value, AXES, pairs)  11.9 us
    unnamed x26, local copies, waits for them, and re-layouts  4.83 us
    pallas_call x1, Pallas kernels, local(): pl.pallas_call(filters_kernel, out_shape=(half, half), in_specs=[SMEM] +...  3.57 us
    pallas_call x1, Pallas kernels, local(): pl.pallas_call(functools.partial(input_kernel, two), out_shape=(tall, tal...  2.58 us
    pallas_call x1, Pallas kernels, local(): pl.pallas_call(cotangent_kernel, out_shape=jax.ShapeDtypeStruct((count, 4...  1.74 us
    pallas_call x1, Pallas kernels, local(): pl.pallas_call(gather_kernel, out_shape=(block, jax.ShapeDtypeStruct((cou...  1.39 us
  transfers between devices with their start and end apart: 22, of which 9 were waited for; matrix products, arithmetic and copies ran while one was open for 0% of the time, Pallas kernels for 8%

profile of v1, /device:TPU:0, one launch (start us, length us, event | category | flops | bytes accessed | tf_op | source)
XLA Modules:
  0.0 51.1 jit_solution(14236773671696304919)
XLA Ops:
  1.2 2.0 %collective-permute-start.1 = (bf16[128,128]{1,0:T(8,128)(2,1)}, bf16[128,128]{1,0:T(8,128)(2,1)}, u32[]{:S(2)}, u32[]{:S(2)}) collective-permute-start(bf16[128,128]{1,0:T(8,128)(2,1)} %own_ref.1), channel_id=1, source_target_pairs={{0,0},{1,2},{2,1},{3,4},{4,3},{5,6},{6,5},{7,8},{8,7},{9,10},{10,9... | collective-permute-start | bytes 98312 | tf_op jit(solution)/shard_map/ppermute | solution.py:234
  3.2 2.5 %collective-permute-start.2 = (bf16[128,128]{1,0:T(8,128)(2,1)}, bf16[128,128]{1,0:T(8,128)(2,1)}, u32[]{:S(2)}, u32[]{:S(2)}) collective-permute-start(bf16[128,128]{1,0:T(8,128)(2,1)} %own_ref.1), channel_id=1, source_target_pairs={{0,16},{1,17},{2,18},{3,19},{4,20},{5,21},{6,22},{7,23},{8,24},{9,... | collective-permute-start | bytes 98312 | tf_op jit(solution)/shard_map/ppermute | solution.py:234
  5.7 1.4 %collective-permute-start.3 = (bf16[128,128]{1,0:T(8,128)(2,1)}, bf16[128,128]{1,0:T(8,128)(2,1)}, u32[]{:S(2)}, u32[]{:S(2)}) collective-permute-start(bf16[128,128]{1,0:T(8,128)(2,1)} %own_ref.1), channel_id=1, source_target_pairs={{0,17},{1,16},{2,19},{3,18},{4,21},{5,20},{6,23},{7,22},{8,25},{9,... | collective-permute-start | bytes 98312 | tf_op jit(solution)/shard_map/ppermute | solution.py:234
  7.1 1.5 %collective-permute-start.4 = (bf16[128,128]{1,0:T(8,128)(2,1)}, bf16[128,128]{1,0:T(8,128)(2,1)}, u32[]{:S(2)}, u32[]{:S(2)}) collective-permute-start(bf16[128,128]{1,0:T(8,128)(2,1)} %own_ref.1), channel_id=1, source_target_pairs={{0,16},{1,18},{2,17},{3,20},{4,19},{5,22},{6,21},{7,24},{8,23},{9,... | collective-permute-start | bytes 98312 | tf_op jit(solution)/shard_map/ppermute | solution.py:234
  8.6 0.9 %copy-done = bf16[384,256]{1,0:T(8,128)(2,1)S(1)} copy-done((bf16[384,256]{1,0:T(8,128)(2,1)S(1)}, bf16[384,256]{1,0:T(8,128)(2,1)}, u32[]{:S(2)}) %copy-start) | copy-done | bytes 196632
  10.5 0.9 %copy-done.5 = bf16[8,128,128]{2,1,0:T(8,128)(2,1)S(1)} copy-done((bf16[8,128,128]{2,1,0:T(8,128)(2,1)S(1)}, bf16[8,128,128]{2,1,0:T(8,128)(2,1)}, u32[]{:S(2)}) %copy-start.5) | copy-done | bytes 262168
  11.4 1.7 %cotangent_spectra.1.spec_ref = f32[8,4,128,128]{3,2,1,0:T(8,128)S(1)} custom-call(bf16[8,128,128]{2,1,0:T(8,128)(2,1)S(1)} %copy-done.5, bf16[256,256]{1,0:T(8,128)(2,1)S(1)} %copy-done.2, bf16[384,256]{1,0:T(8,128)(2,1)S(1)} %copy-done), custom_call_target="tpu_custom_call" | custom-call | tf_op jit(solution)/shard_map/cotangent_spectra/pallas_call | solution.py:253
  13.4 1.1 %copy-done.9 = bf16[256,512]{1,0:T(8,128)(2,1)S(1)} copy-done((bf16[256,512]{1,0:T(8,128)(2,1)S(1)}, bf16[256,512]{1,0:T(8,128)(2,1)}, u32[]{:S(2)}) %copy-start.9) | copy-done | bytes 262168
  15.4 3.6 %grad_filters.1 = (f32[4,128,128]{2,1,0:T(8,128)S(1)}, f32[4,128,128]{2,1,0:T(8,128)S(1)}) custom-call(s32[6]{0:T(128)S(1)} %stack.32.place_ref, f32[8,4,128,128]{3,2,1,0:T(8,128)S(1)} %cotangent_spectra.1.spec_ref, bf16[128,128]{1,0:T(8,128)(2,1)S(1)} %copy-done.12, bf16[128,128]{1,0:T(8,128)(2,1)S(1)} %collective-permute-done.rest_0_, ...), custom_call_target="tpu_custom_call" | custom-call | tf_op jit(solution)/shard_map/grad_filters/pallas_call | solution.py:267
  19.0 1.2 %collective-permute-start.5 = (f32[4,128,128]{2,1,0:T(8,128)S(1)}, f32[4,128,128]{2,1,0:T(8,128)S(1)}, u32[]{:S(2)}, u32[]{:S(2)}) collective-permute-start(f32[4,128,128]{2,1,0:T(8,128)S(1)} %get-tuple-element.10), channel_id=1, source_target_pairs={{0,1},{1,0},{2,3},{3,2},{4,5},{5,4},{6,7},{7,6},{8,9},{9,8},{10,11... | collective-permute-start | bytes 786440 | tf_op jit(solution)/shard_map/ppermute | solution.py:234
  20.1 1.2 %collective-permute-done.5 = f32[4,128,128]{2,1,0:T(8,128)S(1)} collective-permute-done((f32[4,128,128]{2,1,0:T(8,128)S(1)}, f32[4,128,128]{2,1,0:T(8,128)S(1)}, u32[]{:S(2)}, u32[]{:S(2)}) %collective-permute-start.5) | collective-permute-done | bytes 262176 | tf_op jit(solution)/shard_map/ppermute | solution.py:234
  21.3 1.6 %collective-permute-start.6 = (f32[128,128]{1,0:T(8,128)S(1)}, f32[128,128]{1,0:T(8,128)S(1)}, u32[]{:S(2)}, u32[]{:S(2)}) collective-permute-start(f32[128,128]{1,0:T(8,128)S(1)} %get-tuple-element.16), channel_id=1, source_target_pairs={{0,2},{1,3},{2,0},{3,1},{4,6},{5,7},{6,4},{7,5},{8,10},{9,11},{10,... | collective-permute-start | bytes 196616 | tf_op jit(solution)/shard_map/ppermute | solution.py:234
  23.5 1.4 %collective-permute-start.8 = (f32[128,128]{1,0:T(8,128)S(1)}, f32[128,128]{1,0:T(8,128)S(1)}, u32[]{:S(2)}, u32[]{:S(2)}) collective-permute-start(f32[128,128]{1,0:T(8,128)S(1)} %get-tuple-element.15), channel_id=1, source_target_pairs={{0,18},{1,19},{2,16},{3,17},{4,22},{5,23},{6,20},{7,21},{8,26},{9,... | collective-permute-start | bytes 196616 | tf_op jit(solution)/shard_map/ppermute | solution.py:234
  24.9 2.6 %grad_input.1 = (f32[192,128]{1,0:T(8,128)S(1)}, f32[192,128]{1,0:T(8,128)S(1)}) custom-call(s32[6]{0:T(128)S(1)} %stack.32.place_ref, f32[8,4,128,128]{3,2,1,0:T(8,128)S(1)} %cotangent_spectra.1.spec_ref, bf16[8,128,128]{2,1,0:T(8,128)(2,1)S(1)} %copy-done.6, bf16[256,256]{1,0:T(8,128)(2,1)S(1)} %copy-done.3, bf16[384,256]{1,0:T(8,128)(2,1)S(1)} %copy-done.1, ...), custom_call_target="tpu_custom_call" | custom-call | tf_op jit(solution)/shard_map/grad_input/pallas_call | solution.py:285
  28.6 1.6 %collective-permute-start.11 = (f32[128,128]{1,0:T(8,128)S(1)}, f32[128,128]{1,0:T(8,128)S(1)}, u32[]{:S(2)}, u32[]{:S(2)}) collective-permute-start(f32[128,128]{1,0:T(8,128)S(1)} %fusion.4), channel_id=1, source_target_pairs={{0,4},{1,5},{2,6},{3,7},{4,0},{5,1},{6,2},{7,3},{8,12},{9,13},{10,... | collective-permute-start | bytes 196616 | tf_op jit(solution)/shard_map/ppermute | solution.py:234
  30.3 2.0 %collective-permute-start.12 = (f32[128,128]{1,0:T(8,128)S(1)}, f32[128,128]{1,0:T(8,128)S(1)}, u32[]{:S(2)}, u32[]{:S(2)}) collective-permute-start(f32[128,128]{1,0:T(8,128)S(1)} %fusion.4), channel_id=1, source_target_pairs={{0,8},{1,9},{2,10},{3,11},{4,12},{5,13},{6,14},{7,15},{8,0},{9,1},... | collective-permute-start | bytes 196616 | tf_op jit(solution)/shard_map/ppermute | solution.py:234
  33.8 1.9 %collective-permute-start.9 = (f32[192,128]{1,0:T(8,128)S(1)}, f32[192,128]{1,0:T(8,128)S(1)}, u32[]{:S(2)}, u32[]{:S(2)}) collective-permute-start(f32[192,128]{1,0:T(8,128)S(1)} %get-tuple-element.12), channel_id=1, source_target_pairs={{0,1},{1,0},{2,3},{3,2},{4,5},{5,4},{6,7},{7,6},{8,9},{9,8},{10,11... | collective-permute-start | bytes 294920 | tf_op jit(solution)/shard_map/ppermute | solution.py:234
  35.7 1.1 %collective-permute-done.12 = f32[128,128]{1,0:T(8,128)S(1)} collective-permute-done((f32[128,128]{1,0:T(8,128)S(1)}, f32[128,128]{1,0:T(8,128)S(1)}, u32[]{:S(2)}, u32[]{:S(2)}) %collective-permute-start.12) | collective-permute-done | bytes 65568 | tf_op jit(solution)/shard_map/ppermute | solution.py:234
  36.7 1.7 %collective-permute-done.13 = f32[128,128]{1,0:T(8,128)S(1)} collective-permute-done((f32[128,128]{1,0:T(8,128)S(1)}, f32[128,128]{1,0:T(8,128)S(1)}, u32[]{:S(2)}, u32[]{:S(2)}) %collective-permute-start.13) | collective-permute-done | bytes 65568 | tf_op jit(solution)/shard_map/ppermute | solution.py:234
  39.1 1.4 %collective-permute-start.15 = (f32[128,128]{1,0:T(8,128)S(1)}, f32[128,128]{1,0:T(8,128)S(1)}, u32[]{:S(2)}, u32[]{:S(2)}) collective-permute-start(f32[128,128]{1,0:T(8,128)S(1)} %add_add_fusion.refs_0_), channel_id=1, source_target_pairs={{0,16},{1,17},{2,18},{3,19},{4,20},{5,21},{6,22},{7,23},{8,24},{9,... | collective-permute-start | bytes 196616 | tf_op jit(solution)/shard_map/ppermute | solution.py:234
  40.5 1.5 %collective-permute-start.16 = (f32[128,128]{1,0:T(8,128)S(1)}, f32[128,128]{1,0:T(8,128)S(1)}, u32[]{:S(2)}, u32[]{:S(2)}) collective-permute-start(f32[128,128]{1,0:T(8,128)S(1)} %add_add_fusion.refs_0_), channel_id=1, source_target_pairs={{0,18},{1,19},{2,16},{3,17},{4,22},{5,23},{6,20},{7,21},{8,26},{9,... | collective-permute-start | bytes 196616 | tf_op jit(solution)/shard_map/ppermute | solution.py:234
  43.4 2.3 %collective-permute-done.16.refs_3_ = f32[128,128]{1,0:T(8,128)S(1)} collective-permute-done((f32[128,128]{1,0:T(8,128)S(1)}, f32[128,128]{1,0:T(8,128)S(1)}, u32[]{:S(2)}, u32[]{:S(2)}) %collective-permute-start.16) | collective-permute-done | bytes 65568 | tf_op jit(solution)/shard_map/ppermute | solution.py:234
  46.4 3.3 %collective-permute-done.21.refs_8_ = f32[64,128]{1,0:T(8,128)S(1)} collective-permute-done((f32[64,128]{1,0:T(8,128)S(1)}, f32[64,128]{1,0:T(8,128)S(1)}, u32[]{:S(2)}, u32[]{:S(2)}) %collective-permute-start.21) | collective-permute-done | bytes 32800 | tf_op jit(solution)/shard_map/ppermute | solution.py:234
  49.7 1.4 %gather_filters.1 = (f32[128,128]{1,0:T(8,128)}, f32[8,128,128]{2,1,0:T(8,128)}) custom-call(s32[6]{0:T(128)S(1)} %stack.32.place_ref, f32[128,128]{1,0:T(8,128)S(1)} %slice.44.own_ref, f32[128,128]{1,0:T(8,128)S(1)} %add_add_fusion.refs_0_, f32[128,128]{1,0:T(8,128)S(1)} %collective-permute-done.14.refs_1_, f32[128,128]{1,0:T(8,128)S(1)} %collective-permute-done.15.refs_2_, ...), custom_call_target="tpu_custom_call" | custom-call | tf_op jit(solution)/shard_map/gather_filters/pallas_call | solution.py:323
  (58 shorter events, 8.3 us)
Async XLA Ops:
  0.6 12.7 %copy-start.12 = (bf16[128,128]{1,0:T(8,128)(2,1)S(1)}, bf16[128,128]{1,0:T(8,128)(2,1)}, u32[]{:S(2)}) copy-start(bf16[128,128]{1,0:T(8,128)(2,1)} %own_ref.1) | copy-start | bytes 98308
  0.6 12.7 %collective-permute-start = (bf16[128,128]{1,0:T(8,128)(2,1)}, bf16[128,128]{1,0:T(8,128)(2,1)S(1)}, u32[]{:S(2)}, u32[]{:S(2)}) collective-permute-start(bf16[128,128]{1,0:T(8,128)(2,1)} %own_ref.1), channel_id=1, source_target_pairs={{0,1},{1,0},{2,3},{3,2},{4,5},{5,4},{6,7},{7,6},{8,9},{9,8},{10,11... | collective-permute-start | bytes 98312 | tf_op jit(solution)/shard_map/ppermute | solution.py:234
  1.2 12.1 %collective-permute-start.1 = (bf16[128,128]{1,0:T(8,128)(2,1)}, bf16[128,128]{1,0:T(8,128)(2,1)}, u32[]{:S(2)}, u32[]{:S(2)}) collective-permute-start(bf16[128,128]{1,0:T(8,128)(2,1)} %own_ref.1), channel_id=1, source_target_pairs={{0,0},{1,2},{2,1},{3,4},{4,3},{5,6},{6,5},{7,8},{8,7},{9,10},{10,9... | collective-permute-start | bytes 98312 | tf_op jit(solution)/shard_map/ppermute | solution.py:234
  3.2 10.1 %collective-permute-start.2 = (bf16[128,128]{1,0:T(8,128)(2,1)}, bf16[128,128]{1,0:T(8,128)(2,1)}, u32[]{:S(2)}, u32[]{:S(2)}) collective-permute-start(bf16[128,128]{1,0:T(8,128)(2,1)} %own_ref.1), channel_id=1, source_target_pairs={{0,16},{1,17},{2,18},{3,19},{4,20},{5,21},{6,22},{7,23},{8,24},{9,... | collective-permute-start | bytes 98312 | tf_op jit(solution)/shard_map/ppermute | solution.py:234
  5.7 7.6 %collective-permute-start.3 = (bf16[128,128]{1,0:T(8,128)(2,1)}, bf16[128,128]{1,0:T(8,128)(2,1)}, u32[]{:S(2)}, u32[]{:S(2)}) collective-permute-start(bf16[128,128]{1,0:T(8,128)(2,1)} %own_ref.1), channel_id=1, source_target_pairs={{0,17},{1,16},{2,19},{3,18},{4,21},{5,20},{6,23},{7,22},{8,25},{9,... | collective-permute-start | bytes 98312 | tf_op jit(solution)/shard_map/ppermute | solution.py:234
  7.1 6.2 %collective-permute-start.4 = (bf16[128,128]{1,0:T(8,128)(2,1)}, bf16[128,128]{1,0:T(8,128)(2,1)}, u32[]{:S(2)}, u32[]{:S(2)}) collective-permute-start(bf16[128,128]{1,0:T(8,128)(2,1)} %own_ref.1), channel_id=1, source_target_pairs={{0,16},{1,18},{2,17},{3,20},{4,19},{5,22},{6,21},{7,24},{8,23},{9,... | collective-permute-start | bytes 98312 | tf_op jit(solution)/shard_map/ppermute | solution.py:234
  13.2 11.7 %copy-start.1 = (bf16[384,256]{1,0:T(8,128)(2,1)S(1)}, bf16[384,256]{1,0:T(8,128)(2,1)}, u32[]{:S(2)}) copy-start(bf16[384,256]{1,0:T(8,128)(2,1)} %constant.38.clone.cols_hbm.cols_ref) | copy-start | bytes 589828
  19.0 2.3 %collective-permute-start.5 = (f32[4,128,128]{2,1,0:T(8,128)S(1)}, f32[4,128,128]{2,1,0:T(8,128)S(1)}, u32[]{:S(2)}, u32[]{:S(2)}) collective-permute-start(f32[4,128,128]{2,1,0:T(8,128)S(1)} %get-tuple-element.10), channel_id=1, source_target_pairs={{0,1},{1,0},{2,3},{3,2},{4,5},{5,4},{6,7},{7,6},{8,9},{9,8},{10,11... | collective-permute-start | bytes 786440 | tf_op jit(solution)/shard_map/ppermute | solution.py:234
  21.3 6.2 %collective-permute-start.6 = (f32[128,128]{1,0:T(8,128)S(1)}, f32[128,128]{1,0:T(8,128)S(1)}, u32[]{:S(2)}, u32[]{:S(2)}) collective-permute-start(f32[128,128]{1,0:T(8,128)S(1)} %get-tuple-element.16), channel_id=1, source_target_pairs={{0,2},{1,3},{2,0},{3,1},{4,6},{5,7},{6,4},{7,5},{8,10},{9,11},{10,... | collective-permute-start | bytes 196616 | tf_op jit(solution)/shard_map/ppermute | solution.py:234
  22.9 5.0 %collective-permute-start.7 = (f32[128,128]{1,0:T(8,128)S(1)}, f32[128,128]{1,0:T(8,128)S(1)}, u32[]{:S(2)}, u32[]{:S(2)}) collective-permute-start(f32[128,128]{1,0:T(8,128)S(1)} %get-tuple-element.14), channel_id=1, source_target_pairs={{0,16},{1,17},{2,18},{3,19},{4,20},{5,21},{6,22},{7,23},{8,24},{9,... | collective-permute-start | bytes 196616 | tf_op jit(solution)/shard_map/ppermute | solution.py:234
  23.5 5.2 %collective-permute-start.8 = (f32[128,128]{1,0:T(8,128)S(1)}, f32[128,128]{1,0:T(8,128)S(1)}, u32[]{:S(2)}, u32[]{:S(2)}) collective-permute-start(f32[128,128]{1,0:T(8,128)S(1)} %get-tuple-element.15), channel_id=1, source_target_pairs={{0,18},{1,19},{2,16},{3,17},{4,22},{5,23},{6,20},{7,21},{8,26},{9,... | collective-permute-start | bytes 196616 | tf_op jit(solution)/shard_map/ppermute | solution.py:234
  28.6 7.0 %collective-permute-start.11 = (f32[128,128]{1,0:T(8,128)S(1)}, f32[128,128]{1,0:T(8,128)S(1)}, u32[]{:S(2)}, u32[]{:S(2)}) collective-permute-start(f32[128,128]{1,0:T(8,128)S(1)} %fusion.4), channel_id=1, source_target_pairs={{0,4},{1,5},{2,6},{3,7},{4,0},{5,1},{6,2},{7,3},{8,12},{9,13},{10,... | collective-permute-start | bytes 196616 | tf_op jit(solution)/shard_map/ppermute | solution.py:234
  30.3 6.5 %collective-permute-start.12 = (f32[128,128]{1,0:T(8,128)S(1)}, f32[128,128]{1,0:T(8,128)S(1)}, u32[]{:S(2)}, u32[]{:S(2)}) collective-permute-start(f32[128,128]{1,0:T(8,128)S(1)} %fusion.4), channel_id=1, source_target_pairs={{0,8},{1,9},{2,10},{3,11},{4,12},{5,13},{6,14},{7,15},{8,0},{9,1},... | collective-permute-start | bytes 196616 | tf_op jit(solution)/shard_map/ppermute | solution.py:234
  32.3 6.2 %collective-permute-start.13 = (f32[128,128]{1,0:T(8,128)S(1)}, f32[128,128]{1,0:T(8,128)S(1)}, u32[]{:S(2)}, u32[]{:S(2)}) collective-permute-start(f32[128,128]{1,0:T(8,128)S(1)} %fusion.4), channel_id=1, source_target_pairs={{0,12},{1,13},{2,14},{3,15},{4,8},{5,9},{6,10},{7,11},{8,4},{9,5},... | collective-permute-start | bytes 196616 | tf_op jit(solution)/shard_map/ppermute | solution.py:234
  33.1 9.0 %collective-permute-start.10 = (f32[192,128]{1,0:T(8,128)S(1)}, f32[192,128]{1,0:T(8,128)S(1)}, u32[]{:S(2)}, u32[]{:S(2)}) collective-permute-start(f32[192,128]{1,0:T(8,128)S(1)} %get-tuple-element.12), channel_id=1, source_target_pairs={{0,0},{1,2},{2,1},{3,4},{4,3},{5,6},{6,5},{7,8},{8,7},{9,10},{10,9... | collective-permute-start | bytes 294920 | tf_op jit(solution)/shard_map/ppermute | solution.py:234
  33.8 11.9 %collective-permute-start.9 = (f32[192,128]{1,0:T(8,128)S(1)}, f32[192,128]{1,0:T(8,128)S(1)}, u32[]{:S(2)}, u32[]{:S(2)}) collective-permute-start(f32[192,128]{1,0:T(8,128)S(1)} %get-tuple-element.12), channel_id=1, source_target_pairs={{0,1},{1,0},{2,3},{3,2},{4,5},{5,4},{6,7},{7,6},{8,9},{9,8},{10,11... | collective-permute-start | bytes 294920 | tf_op jit(solution)/shard_map/ppermute | solution.py:234
  38.5 4.3 %collective-permute-start.14 = (f32[128,128]{1,0:T(8,128)S(1)}, f32[128,128]{1,0:T(8,128)S(1)}, u32[]{:S(2)}, u32[]{:S(2)}) collective-permute-start(f32[128,128]{1,0:T(8,128)S(1)} %add_add_fusion.refs_0_), channel_id=1, source_target_pairs={{0,2},{1,3},{2,0},{3,1},{4,6},{5,7},{6,4},{7,5},{8,10},{9,11},{10,... | collective-permute-start | bytes 196616 | tf_op jit(solution)/shard_map/ppermute | solution.py:234
  39.1 4.3 %collective-permute-start.15 = (f32[128,128]{1,0:T(8,128)S(1)}, f32[128,128]{1,0:T(8,128)S(1)}, u32[]{:S(2)}, u32[]{:S(2)}) collective-permute-start(f32[128,128]{1,0:T(8,128)S(1)} %add_add_fusion.refs_0_), channel_id=1, source_target_pairs={{0,16},{1,17},{2,18},{3,19},{4,20},{5,21},{6,22},{7,23},{8,24},{9,... | collective-permute-start | bytes 196616 | tf_op jit(solution)/shard_map/ppermute | solution.py:234
  40.5 5.2 %collective-permute-start.16 = (f32[128,128]{1,0:T(8,128)S(1)}, f32[128,128]{1,0:T(8,128)S(1)}, u32[]{:S(2)}, u32[]{:S(2)}) collective-permute-start(f32[128,128]{1,0:T(8,128)S(1)} %add_add_fusion.refs_0_), channel_id=1, source_target_pairs={{0,18},{1,19},{2,16},{3,17},{4,22},{5,23},{6,20},{7,21},{8,26},{9,... | collective-permute-start | bytes 196616 | tf_op jit(solution)/shard_map/ppermute | solution.py:234
  42.1 4.4 %collective-permute-start.17 = (f32[128,128]{1,0:T(8,128)S(1)}, f32[128,128]{1,0:T(8,128)S(1)}, u32[]{:S(2)}, u32[]{:S(2)}) collective-permute-start(f32[128,128]{1,0:T(8,128)S(1)} %add_add_fusion.refs_0_), channel_id=1, source_target_pairs={{0,1},{1,0},{2,3},{3,2},{4,5},{5,4},{6,7},{7,6},{8,9},{9,8},{10,11... | collective-permute-start | bytes 196616 | tf_op jit(solution)/shard_map/ppermute | solution.py:234
  42.8 6.9 %collective-permute-start.18 = (f32[128,128]{1,0:T(8,128)S(1)}, f32[128,128]{1,0:T(8,128)S(1)}, u32[]{:S(2)}, u32[]{:S(2)}) collective-permute-start(f32[128,128]{1,0:T(8,128)S(1)} %collective-permute-done.14.refs_1_), channel_id=1, source_target_pairs={{0,1},{1,0},{2,3},{3,2},{4,5},{5,4},{6,7},{7,6},{8,9},{9,8},{10,11... | collective-permute-start | bytes 196616 | tf_op jit(solution)/shard_map/ppermute | solution.py:234
  43.4 6.3 %collective-permute-start.19 = (f32[128,128]{1,0:T(8,128)S(1)}, f32[128,128]{1,0:T(8,128)S(1)}, u32[]{:S(2)}, u32[]{:S(2)}) collective-permute-start(f32[128,128]{1,0:T(8,128)S(1)} %collective-permute-done.15.refs_2_), channel_id=1, source_target_pairs={{0,1},{1,0},{2,3},{3,2},{4,5},{5,4},{6,7},{7,6},{8,9},{9,8},{10,11... | collective-permute-start | bytes 196616 | tf_op jit(solution)/shard_map/ppermute | solution.py:234
  45.7 4.0 %collective-permute-start.20 = (f32[128,128]{1,0:T(8,128)S(1)}, f32[128,128]{1,0:T(8,128)S(1)}, u32[]{:S(2)}, u32[]{:S(2)}) collective-permute-start(f32[128,128]{1,0:T(8,128)S(1)} %collective-permute-done.16.refs_3_), channel_id=1, source_target_pairs={{0,1},{1,0},{2,3},{3,2},{4,5},{5,4},{6,7},{7,6},{8,9},{9,8},{10,11... | collective-permute-start | bytes 196616 | tf_op jit(solution)/shard_map/ppermute | solution.py:234
  45.7 4.0 %collective-permute-start.21 = (f32[64,128]{1,0:T(8,128)S(1)}, f32[64,128]{1,0:T(8,128)S(1)}, u32[]{:S(2)}, u32[]{:S(2)}) collective-permute-start(f32[64,128]{1,0:T(8,128)S(1)} %slice.45), channel_id=1, source_target_pairs={{0,16},{1,17},{2,18},{3,19},{4,20},{5,21},{6,22},{7,23},{8,24},{9,... | collective-permute-start | bytes 98312 | tf_op jit(solution)/shard_map/ppermute | solution.py:234
  (11 other events, 55.5 us)

commit v2 on v1

v2 whole, which is shorter than its diff:
```python
import functools
import math

import jax
import jax.numpy as jnp
import numpy as np
from jax import lax
from jax.experimental import pallas as pl
from jax.experimental.pallas import tpu as pltpu
from jax.sharding import PartitionSpec as P

AXES = ("across", "along")
f32 = jnp.float32
bf16 = jnp.bfloat16


def halves(table):
    upper = table.astype(np.float32).astype(jnp.bfloat16)
    lower = (table - upper.astype(np.float64)).astype(np.float32).astype(jnp.bfloat16)
    return upper, lower


def tables(radius):
    period = 2 * radius
    freq = np.arange(radius)[:, None] + 0.5

    def turn(position):
        angle = 2.0 * math.pi / period * freq * position[None, :]
        return np.cos(angle), np.sin(angle)

    near = np.arange(radius)
    wide = (np.arange(period) + radius // 2) % period
    def stack(*parts):
        return np.concatenate(parts, axis=0)

    cos_n, sin_n = turn(near)
    cos_w, sin_w = turn(wide)
    scale = 2.0 / period**2
    rows_near = np.concatenate(halves(stack(cos_n, sin_n)), axis=1)
    hi, lo = halves(stack(cos_n, -sin_n).T)
    cols_near = stack(hi, hi, lo)
    rows_wide = stack(*halves(stack(cos_w, sin_w)))
    hi, lo = halves(stack(cos_w, -sin_w).T)
    cols_wide = stack(hi, hi, lo)
    back_rows_near = stack(*halves(stack(cos_n, sin_n).T))
    back_cols_near = np.concatenate(halves(stack(cos_n, -sin_n) * scale), axis=1)
    back_rows_wide = stack(*halves(stack(cos_w, sin_w).T))
    back_cols_wide = stack(*halves(stack(cos_w, -sin_w) * scale))
    return (
        stack(rows_near, cols_near),
        stack(rows_wide, cols_wide, back_rows_near, back_cols_near),
        stack(back_rows_wide, back_cols_wide),
    )


def dot(a, b):
    return jnp.dot(a, b, preferred_element_type=f32)


def split(x):
    upper = x.astype(bf16)
    return upper, (x - upper.astype(f32)).astype(bf16)


def butterfly(mixed, radius):
    cr, ci = mixed[:radius, :radius], mixed[:radius, radius:]
    sr, si = mixed[radius:, :radius], mixed[radius:, radius:]
    return (cr + si, ci - sr), (cr - si, ci + sr)


def near_spectra(first, second, table, radius):
    rows, cols = table[: 2 * radius], table[2 * radius :]
    pair = jnp.concatenate([first, second], axis=1)
    mixed = dot(rows, jnp.concatenate([pair, pair], axis=0))
    result = []
    for part in (mixed[:, :radius], mixed[:, radius:]):
        hi, lo = split(part)
        result.append(butterfly(dot(jnp.concatenate([hi, lo, hi], axis=1), cols), radius))
    return result


def mixed_back(plus, minus):
    (pr, pi), (mr, mi) = plus, minus
    return jnp.concatenate(
        [
            jnp.concatenate([pr + mr, pi + mi], axis=1),
            jnp.concatenate([mi - pi, pr - mr], axis=1),
        ],
        axis=0,
    )


def inverse_rows(mixed, rows):
    count = rows.shape[0] // 2
    hi, lo = split(mixed)
    both = dot(rows, hi)
    return both[:count] + both[count:] + dot(rows[:count], lo)


def inverse_near(plus, minus, rows, cols):
    part = inverse_rows(mixed_back(plus, minus), rows)
    width = cols.shape[1] // 2
    hi, lo = split(part)
    both = dot(hi, cols)
    return both[:, :width] + both[:, width:] + dot(lo, cols[:, :width])


def inverse_wide(plus, minus, rows, cols):
    part = inverse_rows(mixed_back(plus, minus), rows)
    hi, lo = split(part)
    upper, lower = cols[: cols.shape[0] // 2], cols[cols.shape[0] // 2 :]
    return dot(hi, upper) + dot(hi, lower) + dot(lo, upper)


def cotangent_kernel(cot_ref, table_ref, out_ref):
    count, radius = cot_ref.shape[0], cot_ref.shape[1]
    table = table_ref[...]
    for f in range(0, count, 2):
        spectra = near_spectra(cot_ref[f], cot_ref[f + 1], table, radius)
        for g, (plus, minus) in enumerate(spectra):
            out_ref[f + g, 0] = plus[0]
            out_ref[f + g, 1] = plus[1]
            out_ref[f + g, 2] = minus[0]
            out_ref[f + g, 3] = minus[1]


def window_of(own, pieces, place_ref):
    shape = own.shape
    row_edge, row_odd, col_edge, col_odd = (place_ref[n] for n in range(2, 6))
    low_row = lax.broadcasted_iota(jnp.int32, shape, 0) < shape[0] // 2
    low_col = lax.broadcasted_iota(jnp.int32, shape, 1) < shape[1] // 2
    zero = jnp.zeros(shape, f32)
    got = [p[...].astype(f32) for p in pieces]

    def pick(near, far, low, odd, edge):
        return jnp.where(low == (odd == 0), near, jnp.where(edge == 1, zero, far))

    side = pick(got[0], got[1], low_col, col_odd, col_edge)
    rows = []
    for n in range(2, len(got), 3):
        rows.append((got[n], pick(got[n + 1], got[n + 2], low_col, col_odd, col_edge)))
    if len(rows) == 1:
        rows.append((zero, zero))
    below, corner = (
        pick(near, far, low_row, row_odd, row_edge) for near, far in zip(rows[0], rows[1])
    )
    return jnp.concatenate(
        [
            jnp.concatenate([own, side.astype(bf16)], axis=1),
            jnp.concatenate([below.astype(bf16), corner.astype(bf16)], axis=1),
        ],
        axis=0,
    )


def filter_gradients(place_ref, spec_ref, window_spec, back_ref, base, away, out_ref):
    radius = window_spec[0].shape[0]
    ar, ai, br, bi = window_spec
    half, quarter = place_ref[0], place_ref[1]
    if away:
        half = 1 - half
    for slot in range(4):
        f = 4 * half + (quarter ^ slot)
        pr, pi, mr, mi = spec_ref[f, 0], spec_ref[f, 1], spec_ref[f, 2], spec_ref[f, 3]
        plus = (pr * ar + pi * ai, pr * ai - pi * ar)
        minus = (mr * br + mi * bi, mr * bi - mi * br)
        out_ref[slot] = inverse_near(
            plus,
            minus,
            back_ref[base : base + 2 * radius],
            back_ref[base + 2 * radius : base + 4 * radius],
        )


def send_kernel(place_ref, spec_ref, own_ref, *rest):
    pieces, (table_ref, out_ref, window_ref) = rest[:-3], rest[-3:]
    radius = own_ref.shape[0]
    side = 2 * radius
    window = window_of(own_ref[...], pieces, place_ref)
    mixed = dot(table_ref[:side], window) + dot(table_ref[side : 2 * side], window)
    hi, lo = split(mixed)
    mixed = dot(jnp.concatenate([hi, lo, hi], axis=1), table_ref[2 * side : 5 * side])
    plus, minus = butterfly(mixed, radius)
    for n, part in enumerate(plus + minus):
        window_ref[n] = part
    filter_gradients(place_ref, spec_ref, plus + minus, table_ref, 5 * side, True, out_ref)


def keep_kernel(place_ref, spec_ref, window_ref, table_ref, out_ref):
    side = table_ref.shape[1]
    spec = tuple(window_ref[n] for n in range(4))
    filter_gradients(place_ref, spec_ref, spec, table_ref, 5 * side, False, out_ref)


def input_kernel(two, place_ref, spec_ref, filt_ref, table_ref, back_ref, own_ref, side_ref):
    count, radius = filt_ref.shape[0], filt_ref.shape[1]
    table = table_ref[...]
    total = None
    for f in range(0, count, 2):
        spectra = near_spectra(filt_ref[f], filt_ref[f + 1], table, radius)
        for g, ((ar, ai), (br, bi)) in enumerate(spectra):
            pr, pi, mr, mi = (spec_ref[f + g, c] for c in range(4))
            term = (pr * ar - pi * ai, pr * ai + pi * ar, mr * br - mi * bi, mr * bi + mi * br)
            total = term if total is None else tuple(t + u for t, u in zip(total, term))
    full = inverse_wide(total[:2], total[2:], back_ref[: 4 * radius], back_ref[4 * radius :])
    if two:
        half = radius // 2
        far = jnp.where(place_ref[3] == 0, full[radius : radius + half], full[radius + half :])
        full = jnp.concatenate([full[:radius], far], axis=0)
    own_ref[...] = full[:, :radius]
    side_ref[...] = full[:, radius:]


def gather_kernel(place_ref, own_ref, *refs):
    pieces, strips, input_ref, out_ref = refs[:8], refs[8:-2], refs[-2], refs[-1]
    core, quarter, row_edge, row_odd = (place_ref[n] for n in range(4))
    for slot in range(8):
        half = core if slot < 4 else 1 - core
        out_ref[4 * half + (quarter ^ (slot % 4))] = pieces[slot][...]
    shape = own_ref.shape
    low_row = lax.broadcasted_iota(jnp.int32, shape, 0) < shape[0] // 2
    zero = jnp.zeros(shape, f32)
    if len(strips) == 1:
        strip = strips[0][...]
        near, far = jnp.concatenate([strip, strip], axis=0), zero
    else:
        near, far = strips[0][...], jnp.where(row_edge == 1, zero, strips[1][...])
    input_ref[...] = own_ref[...] + jnp.where(low_row == (row_odd == 1), near, far)


VMEM = pl.BlockSpec(memory_space=pltpu.VMEM)
SMEM = pl.BlockSpec(memory_space=pltpu.SMEM)
LIMIT = pltpu.CompilerParams(vmem_limit_bytes=12 * 1024 * 1024)


def local(table, across, along, retard, cotangent, filters):
    count, radius = filters.shape[0], filters.shape[1]
    two = across == 2
    row_index, col_index = lax.axis_index("across"), lax.axis_index("along")
    place = jnp.stack(
        [
            col_index & 1,
            ((col_index >> 1) & 1) + 2 * (row_index & 1),
            ((row_index == 0) | (row_index == across - 1)).astype(jnp.int32),
            row_index & 1,
            ((col_index == 0) | (col_index == along - 1)).astype(jnp.int32),
            col_index & 1,
        ]
    ).astype(jnp.int32)

    def move(value, change):
        pairs = []
        for a in range(across):
            for b in range(along):
                c, d = change(a, b)
                pairs.append((a * along + b, c * along + d))
        return lax.ppermute(value, AXES, pairs)

    def near(index, size):
        return index ^ 1

    def far(index, size):
        other = ((index + 1) ^ 1) - 1
        return other if 0 <= other < size else index

    def stay(index, size):
        return index

    def to(row, col):
        return lambda a, b: (row(a, across), col(b, along))

    row_moves = (near,) if two else (near, far)
    pieces = [move(retard, to(stay, near)), move(retard, to(stay, far))]
    for row in row_moves:
        pieces += [move(retard, to(row, col)) for col in (stay, near, far)]
    near_table, filter_table, input_table = table

    def call(kernel, outs, name, work, *operands):
        scalars = operands[0] is place
        return pl.pallas_call(
            kernel,
            out_shape=outs,
            in_specs=[SMEM] * scalars + [VMEM] * (len(operands) - scalars),
            out_specs=jax.tree.map(lambda _: VMEM, outs),
            compiler_params=LIMIT,
            cost_estimate=pl.CostEstimate(
                flops=work * radius**3,
                bytes_accessed=sum(v.size * v.dtype.itemsize for v in operands),
                transcendentals=0,
            ),
            name=name,
        )(*operands)

    def arrays(*shape):
        return jax.ShapeDtypeStruct(shape, f32)

    spectra = call(
        cotangent_kernel,
        arrays(count, 4, radius, radius),
        "cotangent_spectra",
        700,
        cotangent,
        near_table,
    )
    half = arrays(count // 2, radius, radius)
    send, window = call(
        send_kernel,
        (half, arrays(4, radius, radius)),
        "filters_send",
        1100,
        place,
        spectra,
        retard,
        *pieces,
        filter_table,
    )
    keep = call(keep_kernel, half, "filters_keep", 800, place, spectra, window, filter_table)
    tall = arrays(2 * radius - (radius // 2 if two else 0), radius)
    own, side = call(
        functools.partial(input_kernel, two),
        (tall, tall),
        "grad_input",
        1300,
        place,
        spectra,
        filters,
        near_table,
        input_table,
    )

    got = move(send, lambda a, b: (a, b ^ 1))
    mine = lax.optimization_barrier([keep[n] + got[n] for n in range(4)])
    flips = [lambda a, b, n=n: (a ^ (n >> 1), b ^ ((n & 1) << 1)) for n in range(4)]
    value = mine[0] + sum(move(mine[n], flips[n]) for n in range(1, 4))
    bits = [(0, 1 << s) for s in range(2, (along - 1).bit_length())]
    bits += [(1 << s, 0) for s in range(1, (across - 1).bit_length())]
    for start in range(0, len(bits), 2):
        group = bits[start : start + 2]
        masks = group + ([tuple(p ^ q for p, q in zip(*group))] if len(group) == 2 else [])
        if start == 0:
            value, side = lax.optimization_barrier((value, side))
            beside = [move(side, to(stay, col)) for col in (near, far)]
        value = value + sum(
            move(value, lambda a, b, m=m: (a ^ m[0], b ^ m[1])) for m in masks
        )
    low_col = lax.broadcasted_iota(jnp.int32, tall.shape, 1) < radius // 2
    other = jnp.where((col_index == 0) | (col_index == along - 1), 0.0, beside[1])
    own = own + jnp.where(low_col == (col_index & 1 == 1), beside[0], other)
    value, strip = lax.optimization_barrier((value, own[radius:]))
    strips = [move(strip, to(row, stay)) for row in row_moves]
    parts = [value] + [move(value, flips[n]) for n in range(1, 4)]
    parts[3], strips = lax.optimization_barrier((parts[3], strips))
    parts += [move(part, lambda a, b: (a, b ^ 1)) for part in parts]
    return call(
        gather_kernel,
        (arrays(radius, radius), arrays(count, radius, radius)),
        "gather_filters",
        0,
        place,
        own[:radius],
        *parts,
        *strips,
    )


def solution(mesh):
    across, along = mesh.shape["across"], mesh.shape["along"]

    def whole(retard, cotangent, filters):
        table = [jnp.asarray(v) for v in tables(filters.shape[1])]
        return jax.shard_map(
            functools.partial(local, table, across, along),
            mesh=mesh,
            in_specs=(P("across", "along"), P(None, "across", "along"), P()),
            out_specs=(P("across", "along"), P()),
            check_vma=False,
        )(retard, cotangent, filters)

    return whole
```

time: 51.5 us -> 45.7 us (0.89)
  waiting for transfers between devices: 11.9 us -> 7.33 us
  local copies, waits for them, and re-layouts: 4.93 us -> 2.03 us
  starting transfers between devices: 24.1 us -> 25.9 us
    ppermute x22, waiting for transfers between devices: 11.9 us -> 7.33 us  [move(): return lax.ppermute(value, AXES, pairs)]
    unnamed x26 -> x14, local copies, waits for them, and re-layouts: 4.83 us -> 1.94 us
    ppermute x22, starting transfers between devices: 24.1 us -> 25.9 us  [move(): return lax.ppermute(value, AXES, pairs)]
    pallas_call x4 -> x5, Pallas kernels: 9.28 us -> 9.32 us  [call(): pl.pallas_call(kernel, out_shape=outs, in_specs=[SMEM] * scalars + [VMEM]...]
  transfers between devices with their start and end apart: 22 -> 22, of which waited for: 9 -> 8; matrix products, arithmetic and copies ran while one was open for 0% -> 0% of each run, Pallas kernels for 8% -> 12%
where the time goes in v2:
time: 45.7 us; the launch traced here: 45.5 us
  starting transfers between devices  25.9 us (57%)
  Pallas kernels  9.32 us (20%)
  waiting for transfers between devices  7.33 us (16%)
  local copies, waits for them, and re-layouts  2.03 us (4%)
  between operations  0.81 us (2%)
    ppermute x22, starting transfers between devices, move(): return lax.ppermute(value, AXES, pairs)  25.9 us
    pallas_call x5, Pallas kernels, call(): pl.pallas_call(kernel, out_shape=outs, in_specs=[SMEM] * scalars + [VMEM]...  9.32 us
    ppermute x22, waiting for transfers between devices, move(): return lax.ppermute(value, AXES, pairs)  7.33 us
    unnamed x14, local copies, waits for them, and re-layouts  1.94 us
  transfers between devices with their start and end apart: 22, of which 8 were waited for; matrix products, arithmetic and copies ran while one was open for 0% of the time, Pallas kernels for 12%

profile of v2, /device:TPU:0, one launch (start us, length us, event | category | flops | bytes accessed | tf_op | source)
XLA Modules:
  0.0 45.5 jit_solution(3464891796014698601)
XLA Ops:
  1.1 1.4 %collective-permute-start.1 = (bf16[128,128]{1,0:T(8,128)(2,1)}, bf16[128,128]{1,0:T(8,128)(2,1)S(1)}, u32[]{:S(2)}, u32[]{:S(2)}) collective-permute-start(bf16[128,128]{1,0:T(8,128)(2,1)} %own_ref.1), channel_id=1, source_target_pairs={{0,0},{1,2},{2,1},{3,4},{4,3},{5,6},{6,5},{7,8},{8,7},{9,10},{10,9... | collective-permute-start | bytes 98312 | tf_op jit(solution)/shard_map/ppermute | solution.py:257
  2.6 2.5 %collective-permute-start.2 = (bf16[128,128]{1,0:T(8,128)(2,1)}, bf16[128,128]{1,0:T(8,128)(2,1)S(1)}, u32[]{:S(2)}, u32[]{:S(2)}) collective-permute-start(bf16[128,128]{1,0:T(8,128)(2,1)} %own_ref.1), channel_id=1, source_target_pairs={{0,16},{1,17},{2,18},{3,19},{4,20},{5,21},{6,22},{7,23},{8,24},{9,... | collective-permute-start | bytes 98312 | tf_op jit(solution)/shard_map/ppermute | solution.py:257
  5.1 2.0 %collective-permute-start.3 = (bf16[128,128]{1,0:T(8,128)(2,1)}, bf16[128,128]{1,0:T(8,128)(2,1)S(1)}, u32[]{:S(2)}, u32[]{:S(2)}) collective-permute-start(bf16[128,128]{1,0:T(8,128)(2,1)} %own_ref.1), channel_id=1, source_target_pairs={{0,17},{1,16},{2,19},{3,18},{4,21},{5,20},{6,23},{7,22},{8,25},{9,... | collective-permute-start | bytes 98312 | tf_op jit(solution)/shard_map/ppermute | solution.py:257
  7.1 1.5 %collective-permute-start.4 = (bf16[128,128]{1,0:T(8,128)(2,1)}, bf16[128,128]{1,0:T(8,128)(2,1)S(1)}, u32[]{:S(2)}, u32[]{:S(2)}) collective-permute-start(bf16[128,128]{1,0:T(8,128)(2,1)} %own_ref.1), channel_id=1, source_target_pairs={{0,16},{1,18},{2,17},{3,20},{4,19},{5,22},{6,21},{7,24},{8,23},{9,... | collective-permute-start | bytes 98312 | tf_op jit(solution)/shard_map/ppermute | solution.py:257
  8.6 0.9 %copy-done = bf16[8,128,128]{2,1,0:T(8,128)(2,1)S(1)} copy-done((bf16[8,128,128]{2,1,0:T(8,128)(2,1)S(1)}, bf16[8,128,128]{2,1,0:T(8,128)(2,1)}, u32[]{:S(2)}) %copy-start) | copy-done | bytes 262168
  9.6 1.0 %copy-done.5 = bf16[640,256]{1,0:T(8,128)(2,1)S(1)} copy-done((bf16[640,256]{1,0:T(8,128)(2,1)S(1)}, bf16[640,256]{1,0:T(8,128)(2,1)}, u32[]{:S(2)}) %copy-start.5) | copy-done | bytes 327704
  10.5 1.3 %cotangent_spectra.1.spec_ref = f32[8,4,128,128]{3,2,1,0:T(8,128)S(1)} custom-call(bf16[8,128,128]{2,1,0:T(8,128)(2,1)S(1)} %copy-done, bf16[640,256]{1,0:T(8,128)(2,1)S(1)} %copy-done.5), custom_call_target="tpu_custom_call" | custom-call | flops 1468006400 | bytes 589824 | tf_op jit(solution)/shard_map/cotangent_spectra/pallas_call | solution.py:280
  12.0 2.3 %filters_send.1 = (f32[4,128,128]{2,1,0:T(8,128)S(1)}, f32[4,128,128]{2,1,0:T(8,128)S(1)}) custom-call(s32[6]{0:T(128)S(1)} %stack.32.place_ref, f32[8,4,128,128]{3,2,1,0:T(8,128)S(1)} %cotangent_spectra.1.spec_ref, bf16[128,128]{1,0:T(8,128)(2,1)S(1)} %copy-done.2, bf16[128,128]{1,0:T(8,128)(2,1)S(1)} %collective-permute-done.rest_0_, ...), custom_call_target="tpu_custom_call" | custom-call | flops 2306867200 | bytes 3211288 | tf_op jit(solution)/shard_map/filters_send/pallas_call | solution.py:280
  14.3 1.2 %collective-permute-start.5 = (f32[4,128,128]{2,1,0:T(8,128)S(1)}, f32[4,128,128]{2,1,0:T(8,128)S(1)}, u32[]{:S(2)}, u32[]{:S(2)}) collective-permute-start(f32[4,128,128]{2,1,0:T(8,128)S(1)} %get-tuple-element.18), channel_id=1, source_target_pairs={{0,1},{1,0},{2,3},{3,2},{4,5},{5,4},{6,7},{7,6},{8,9},{9,8},{10,11... | collective-permute-start | bytes 786440 | tf_op jit(solution)/shard_map/ppermute | solution.py:257
  15.4 1.8 %filters_keep.1 = f32[4,128,128]{2,1,0:T(8,128)S(1)} custom-call(s32[6]{0:T(128)S(1)} %stack.32.place_ref, f32[8,4,128,128]{3,2,1,0:T(8,128)S(1)} %cotangent_spectra.1.spec_ref, f32[4,128,128]{2,1,0:T(8,128)S(1)} %get-tuple-element.17.window_ref, bf16[1792,256]{1,0:T(8,128)(2,1)S(1)} %copy-done.3), custom_call_target="tpu_custom_call" | custom-call | flops 1677721600 | bytes 3276824 | tf_op jit(solution)/shard_map/filters_keep/pallas_call | solution.py:280
  17.3 1.6 %collective-permute-start.6 = (f32[128,128]{1,0:T(8,128)S(1)}, f32[128,128]{1,0:T(8,128)S(1)}, u32[]{:S(2)}, u32[]{:S(2)}) collective-permute-start(f32[128,128]{1,0:T(8,128)S(1)} %get-tuple-element.20), channel_id=1, source_target_pairs={{0,2},{1,3},{2,0},{3,1},{4,6},{5,7},{6,4},{7,5},{8,10},{9,11},{10,... | collective-permute-start | bytes 196616 | tf_op jit(solution)/shard_map/ppermute | solution.py:257
  19.5 1.3 %collective-permute-start.8 = (f32[128,128]{1,0:T(8,128)S(1)}, f32[128,128]{1,0:T(8,128)S(1)}, u32[]{:S(2)}, u32[]{:S(2)}) collective-permute-start(f32[128,128]{1,0:T(8,128)S(1)} %get-tuple-element.22), channel_id=1, source_target_pairs={{0,18},{1,19},{2,16},{3,17},{4,22},{5,23},{6,20},{7,21},{8,26},{9,... | collective-permute-start | bytes 196616 | tf_op jit(solution)/shard_map/ppermute | solution.py:257
  20.8 2.6 %grad_input.1 = (f32[192,128]{1,0:T(8,128)S(1)}, f32[192,128]{1,0:T(8,128)S(1)}) custom-call(s32[6]{0:T(128)S(1)} %stack.32.place_ref, f32[8,4,128,128]{3,2,1,0:T(8,128)S(1)} %cotangent_spectra.1.spec_ref, bf16[8,128,128]{2,1,0:T(8,128)(2,1)S(1)} %copy-done.1, bf16[640,256]{1,0:T(8,128)(2,1)S(1)} %copy-done.6, bf16[1024,256]{1,0:T(8,128)(2,1)S(1)} %copy-done.4), custom_call_target="tpu_custom_call" | custom-call | flops 2726297600 | bytes 3211288 | tf_op jit(solution)/shard_map/grad_input/pallas_call | solution.py:280
  23.8 0.9 %collective-permute-done.8 = f32[128,128]{1,0:T(8,128)S(1)} collective-permute-done((f32[128,128]{1,0:T(8,128)S(1)}, f32[128,128]{1,0:T(8,128)S(1)}, u32[]{:S(2)}, u32[]{:S(2)}) %collective-permute-start.8) | collective-permute-done | bytes 65568 | tf_op jit(solution)/shard_map/ppermute | solution.py:257
  24.7 1.6 %collective-permute-start.11 = (f32[128,128]{1,0:T(8,128)S(1)}, f32[128,128]{1,0:T(8,128)S(1)}, u32[]{:S(2)}, u32[]{:S(2)}) collective-permute-start(f32[128,128]{1,0:T(8,128)S(1)} %add_add_fusion.1), channel_id=1, source_target_pairs={{0,4},{1,5},{2,6},{3,7},{4,0},{5,1},{6,2},{7,3},{8,12},{9,13},{10,... | collective-permute-start | bytes 196616 | tf_op jit(solution)/shard_map/ppermute | solution.py:257
  26.3 1.6 %collective-permute-start.12 = (f32[128,128]{1,0:T(8,128)S(1)}, f32[128,128]{1,0:T(8,128)S(1)}, u32[]{:S(2)}, u32[]{:S(2)}) collective-permute-start(f32[128,128]{1,0:T(8,128)S(1)} %add_add_fusion.1), channel_id=1, source_target_pairs={{0,8},{1,9},{2,10},{3,11},{4,12},{5,13},{6,14},{7,15},{8,0},{9,1},... | collective-permute-start | bytes 196616 | tf_op jit(solution)/shard_map/ppermute | solution.py:257
  27.9 1.2 %collective-permute-start.13 = (f32[128,128]{1,0:T(8,128)S(1)}, f32[128,128]{1,0:T(8,128)S(1)}, u32[]{:S(2)}, u32[]{:S(2)}) collective-permute-start(f32[128,128]{1,0:T(8,128)S(1)} %add_add_fusion.1), channel_id=1, source_target_pairs={{0,12},{1,13},{2,14},{3,15},{4,8},{5,9},{6,10},{7,11},{8,4},{9,5},... | collective-permute-start | bytes 196616 | tf_op jit(solution)/shard_map/ppermute | solution.py:257
  29.8 2.1 %collective-permute-start.9 = (f32[192,128]{1,0:T(8,128)S(1)}, f32[192,128]{1,0:T(8,128)S(1)}, u32[]{:S(2)}, u32[]{:S(2)}) collective-permute-start(f32[192,128]{1,0:T(8,128)S(1)} %get-tuple-element.24), channel_id=1, source_target_pairs={{0,1},{1,0},{2,3},{3,2},{4,5},{5,4},{6,7},{7,6},{8,9},{9,8},{10,11... | collective-permute-start | bytes 294920 | tf_op jit(solution)/shard_map/ppermute | solution.py:257
  31.9 1.0 %collective-permute-done.12 = f32[128,128]{1,0:T(8,128)S(1)} collective-permute-done((f32[128,128]{1,0:T(8,128)S(1)}, f32[128,128]{1,0:T(8,128)S(1)}, u32[]{:S(2)}, u32[]{:S(2)}) %collective-permute-start.12) | collective-permute-done | bytes 65568 | tf_op jit(solution)/shard_map/ppermute | solution.py:257
  32.9 1.2 %collective-permute-done.13 = f32[128,128]{1,0:T(8,128)S(1)} collective-permute-done((f32[128,128]{1,0:T(8,128)S(1)}, f32[128,128]{1,0:T(8,128)S(1)}, u32[]{:S(2)}, u32[]{:S(2)}) %collective-permute-start.13) | collective-permute-done | bytes 65568 | tf_op jit(solution)/shard_map/ppermute | solution.py:257
  34.2 3.4 %collective-permute-start.16 = (f32[128,128]{1,0:T(8,128)S(1)}, f32[128,128]{1,0:T(8,128)S(1)}, u32[]{:S(2)}, u32[]{:S(2)}) collective-permute-start(f32[128,128]{1,0:T(8,128)S(1)} %add_add_fusion.refs_0_), channel_id=1, source_target_pairs={{0,18},{1,19},{2,16},{3,17},{4,22},{5,23},{6,20},{7,21},{8,26},{9,... | collective-permute-start | bytes 196616 | tf_op jit(solution)/shard_map/ppermute | solution.py:257
  38.4 1.2 %collective-permute-start.17 = (f32[64,128]{1,0:T(8,128)S(1)}, f32[64,128]{1,0:T(8,128)S(1)}, u32[]{:S(2)}, u32[]{:S(2)}) collective-permute-start(f32[64,128]{1,0:T(8,128)S(1)} %slice.49), channel_id=1, source_target_pairs={{0,16},{1,17},{2,18},{3,19},{4,20},{5,21},{6,22},{7,23},{8,24},{9,... | collective-permute-start | bytes 98312 | tf_op jit(solution)/shard_map/ppermute | solution.py:257
  39.6 2.7 %collective-permute-done.17.refs_8_ = f32[64,128]{1,0:T(8,128)S(1)} collective-permute-done((f32[64,128]{1,0:T(8,128)S(1)}, f32[64,128]{1,0:T(8,128)S(1)}, u32[]{:S(2)}, u32[]{:S(2)}) %collective-permute-start.17) | collective-permute-done | bytes 32800 | tf_op jit(solution)/shard_map/ppermute | solution.py:257
  44.1 1.4 %gather_filters.1 = (f32[128,128]{1,0:T(8,128)}, f32[8,128,128]{2,1,0:T(8,128)}) custom-call(s32[6]{0:T(128)S(1)} %stack.32.place_ref, f32[128,128]{1,0:T(8,128)S(1)} %slice.48.own_ref, f32[128,128]{1,0:T(8,128)S(1)} %add_add_fusion.refs_0_, f32[128,128]{1,0:T(8,128)S(1)} %collective-permute-done.14.refs_1_, f32[128,128]{1,0:T(8,128)S(1)} %collective-permute-done.15.refs_2_, ...), custom_call_target="tpu_custom_call" | custom-call | bytes 622616 | tf_op jit(solution)/shard_map/gather_filters/pallas_call | solution.py:280
  (47 shorter events, 5.0 us)
Async XLA Ops:
  0.6 11.3 %collective-permute-start = (bf16[128,128]{1,0:T(8,128)(2,1)}, bf16[128,128]{1,0:T(8,128)(2,1)S(1)}, u32[]{:S(2)}, u32[]{:S(2)}) collective-permute-start(bf16[128,128]{1,0:T(8,128)(2,1)} %own_ref.1), channel_id=1, source_target_pairs={{0,1},{1,0},{2,3},{3,2},{4,5},{5,4},{6,7},{7,6},{8,9},{9,8},{10,11... | collective-permute-start | bytes 98312 | tf_op jit(solution)/shard_map/ppermute | solution.py:257
  1.1 10.8 %collective-permute-start.1 = (bf16[128,128]{1,0:T(8,128)(2,1)}, bf16[128,128]{1,0:T(8,128)(2,1)S(1)}, u32[]{:S(2)}, u32[]{:S(2)}) collective-permute-start(bf16[128,128]{1,0:T(8,128)(2,1)} %own_ref.1), channel_id=1, source_target_pairs={{0,0},{1,2},{2,1},{3,4},{4,3},{5,6},{6,5},{7,8},{8,7},{9,10},{10,9... | collective-permute-start | bytes 98312 | tf_op jit(solution)/shard_map/ppermute | solution.py:257
  2.6 9.4 %collective-permute-start.2 = (bf16[128,128]{1,0:T(8,128)(2,1)}, bf16[128,128]{1,0:T(8,128)(2,1)S(1)}, u32[]{:S(2)}, u32[]{:S(2)}) collective-permute-start(bf16[128,128]{1,0:T(8,128)(2,1)} %own_ref.1), channel_id=1, source_target_pairs={{0,16},{1,17},{2,18},{3,19},{4,20},{5,21},{6,22},{7,23},{8,24},{9,... | collective-permute-start | bytes 98312 | tf_op jit(solution)/shard_map/ppermute | solution.py:257
  5.1 6.9 %collective-permute-start.3 = (bf16[128,128]{1,0:T(8,128)(2,1)}, bf16[128,128]{1,0:T(8,128)(2,1)S(1)}, u32[]{:S(2)}, u32[]{:S(2)}) collective-permute-start(bf16[128,128]{1,0:T(8,128)(2,1)} %own_ref.1), channel_id=1, source_target_pairs={{0,17},{1,16},{2,19},{3,18},{4,21},{5,20},{6,23},{7,22},{8,25},{9,... | collective-permute-start | bytes 98312 | tf_op jit(solution)/shard_map/ppermute | solution.py:257
  7.1 4.9 %collective-permute-start.4 = (bf16[128,128]{1,0:T(8,128)(2,1)}, bf16[128,128]{1,0:T(8,128)(2,1)S(1)}, u32[]{:S(2)}, u32[]{:S(2)}) collective-permute-start(bf16[128,128]{1,0:T(8,128)(2,1)} %own_ref.1), channel_id=1, source_target_pairs={{0,16},{1,18},{2,17},{3,20},{4,19},{5,22},{6,21},{7,24},{8,23},{9,... | collective-permute-start | bytes 98312 | tf_op jit(solution)/shard_map/ppermute | solution.py:257
  14.3 2.9 %collective-permute-start.5 = (f32[4,128,128]{2,1,0:T(8,128)S(1)}, f32[4,128,128]{2,1,0:T(8,128)S(1)}, u32[]{:S(2)}, u32[]{:S(2)}) collective-permute-start(f32[4,128,128]{2,1,0:T(8,128)S(1)} %get-tuple-element.18), channel_id=1, source_target_pairs={{0,1},{1,0},{2,3},{3,2},{4,5},{5,4},{6,7},{7,6},{8,9},{9,8},{10,11... | collective-permute-start | bytes 786440 | tf_op jit(solution)/shard_map/ppermute | solution.py:257
  15.4 5.4 %copy-start.4 = (bf16[1024,256]{1,0:T(8,128)(2,1)S(1)}, bf16[1024,256]{1,0:T(8,128)(2,1)}, u32[]{:S(2)}) copy-start(bf16[1024,256]{1,0:T(8,128)(2,1)} %constant.29.clone.back_ref) | copy-start | bytes 1572868
  15.4 5.4 %copy-start.6 = (bf16[640,256]{1,0:T(8,128)(2,1)S(1)}, bf16[640,256]{1,0:T(8,128)(2,1)}, u32[]{:S(2)}) copy-start(bf16[640,256]{1,0:T(8,128)(2,1)} %constant.27.clone.table_ref) | copy-start | bytes 983044
  17.3 6.2 %collective-permute-start.6 = (f32[128,128]{1,0:T(8,128)S(1)}, f32[128,128]{1,0:T(8,128)S(1)}, u32[]{:S(2)}, u32[]{:S(2)}) collective-permute-start(f32[128,128]{1,0:T(8,128)S(1)} %get-tuple-element.20), channel_id=1, source_target_pairs={{0,2},{1,3},{2,0},{3,1},{4,6},{5,7},{6,4},{7,5},{8,10},{9,11},{10,... | collective-permute-start | bytes 196616 | tf_op jit(solution)/shard_map/ppermute | solution.py:257
  18.8 5.0 %collective-permute-start.7 = (f32[128,128]{1,0:T(8,128)S(1)}, f32[128,128]{1,0:T(8,128)S(1)}, u32[]{:S(2)}, u32[]{:S(2)}) collective-permute-start(f32[128,128]{1,0:T(8,128)S(1)} %get-tuple-element.21), channel_id=1, source_target_pairs={{0,16},{1,17},{2,18},{3,19},{4,20},{5,21},{6,22},{7,23},{8,24},{9,... | collective-permute-start | bytes 196616 | tf_op jit(solution)/shard_map/ppermute | solution.py:257
  19.5 5.2 %collective-permute-start.8 = (f32[128,128]{1,0:T(8,128)S(1)}, f32[128,128]{1,0:T(8,128)S(1)}, u32[]{:S(2)}, u32[]{:S(2)}) collective-permute-start(f32[128,128]{1,0:T(8,128)S(1)} %get-tuple-element.22), channel_id=1, source_target_pairs={{0,18},{1,19},{2,16},{3,17},{4,22},{5,23},{6,20},{7,21},{8,26},{9,... | collective-permute-start | bytes 196616 | tf_op jit(solution)/shard_map/ppermute | solution.py:257
  24.7 7.2 %collective-permute-start.11 = (f32[128,128]{1,0:T(8,128)S(1)}, f32[128,128]{1,0:T(8,128)S(1)}, u32[]{:S(2)}, u32[]{:S(2)}) collective-permute-start(f32[128,128]{1,0:T(8,128)S(1)} %add_add_fusion.1), channel_id=1, source_target_pairs={{0,4},{1,5},{2,6},{3,7},{4,0},{5,1},{6,2},{7,3},{8,12},{9,13},{10,... | collective-permute-start | bytes 196616 | tf_op jit(solution)/shard_map/ppermute | solution.py:257
  26.3 6.6 %collective-permute-start.12 = (f32[128,128]{1,0:T(8,128)S(1)}, f32[128,128]{1,0:T(8,128)S(1)}, u32[]{:S(2)}, u32[]{:S(2)}) collective-permute-start(f32[128,128]{1,0:T(8,128)S(1)} %add_add_fusion.1), channel_id=1, source_target_pairs={{0,8},{1,9},{2,10},{3,11},{4,12},{5,13},{6,14},{7,15},{8,0},{9,1},... | collective-permute-start | bytes 196616 | tf_op jit(solution)/shard_map/ppermute | solution.py:257
  27.9 6.2 %collective-permute-start.13 = (f32[128,128]{1,0:T(8,128)S(1)}, f32[128,128]{1,0:T(8,128)S(1)}, u32[]{:S(2)}, u32[]{:S(2)}) collective-permute-start(f32[128,128]{1,0:T(8,128)S(1)} %add_add_fusion.1), channel_id=1, source_target_pairs={{0,12},{1,13},{2,14},{3,15},{4,8},{5,9},{6,10},{7,11},{8,4},{9,5},... | collective-permute-start | bytes 196616 | tf_op jit(solution)/shard_map/ppermute | solution.py:257
  29.1 5.0 %collective-permute-start.10 = (f32[192,128]{1,0:T(8,128)S(1)}, f32[192,128]{1,0:T(8,128)S(1)}, u32[]{:S(2)}, u32[]{:S(2)}) collective-permute-start(f32[192,128]{1,0:T(8,128)S(1)} %get-tuple-element.24), channel_id=1, source_target_pairs={{0,0},{1,2},{2,1},{3,4},{4,3},{5,6},{6,5},{7,8},{8,7},{9,10},{10,9... | collective-permute-start | bytes 294920 | tf_op jit(solution)/shard_map/ppermute | solution.py:257
  29.8 4.3 %collective-permute-start.9 = (f32[192,128]{1,0:T(8,128)S(1)}, f32[192,128]{1,0:T(8,128)S(1)}, u32[]{:S(2)}, u32[]{:S(2)}) collective-permute-start(f32[192,128]{1,0:T(8,128)S(1)} %get-tuple-element.24), channel_id=1, source_target_pairs={{0,1},{1,0},{2,3},{3,2},{4,5},{5,4},{6,7},{7,6},{8,9},{9,8},{10,11... | collective-permute-start | bytes 294920 | tf_op jit(solution)/shard_map/ppermute | solution.py:257
  34.2 8.1 %collective-permute-start.16 = (f32[128,128]{1,0:T(8,128)S(1)}, f32[128,128]{1,0:T(8,128)S(1)}, u32[]{:S(2)}, u32[]{:S(2)}) collective-permute-start(f32[128,128]{1,0:T(8,128)S(1)} %add_add_fusion.refs_0_), channel_id=1, source_target_pairs={{0,18},{1,19},{2,16},{3,17},{4,22},{5,23},{6,20},{7,21},{8,26},{9,... | collective-permute-start | bytes 196616 | tf_op jit(solution)/shard_map/ppermute | solution.py:257
  37.5 4.8 %collective-permute-start.14 = (f32[128,128]{1,0:T(8,128)S(1)}, f32[128,128]{1,0:T(8,128)S(1)}, u32[]{:S(2)}, u32[]{:S(2)}) collective-permute-start(f32[128,128]{1,0:T(8,128)S(1)} %add_add_fusion.refs_0_), channel_id=1, source_target_pairs={{0,2},{1,3},{2,0},{3,1},{4,6},{5,7},{6,4},{7,5},{8,10},{9,11},{10,... | collective-permute-start | bytes 196616 | tf_op jit(solution)/shard_map/ppermute | solution.py:257
  37.5 5.3 %collective-permute-start.15 = (f32[128,128]{1,0:T(8,128)S(1)}, f32[128,128]{1,0:T(8,128)S(1)}, u32[]{:S(2)}, u32[]{:S(2)}) collective-permute-start(f32[128,128]{1,0:T(8,128)S(1)} %add_add_fusion.refs_0_), channel_id=1, source_target_pairs={{0,16},{1,17},{2,18},{3,19},{4,20},{5,21},{6,22},{7,23},{8,24},{9,... | collective-permute-start | bytes 196616 | tf_op jit(solution)/shard_map/ppermute | solution.py:257
  38.4 3.9 %collective-permute-start.17 = (f32[64,128]{1,0:T(8,128)S(1)}, f32[64,128]{1,0:T(8,128)S(1)}, u32[]{:S(2)}, u32[]{:S(2)}) collective-permute-start(f32[64,128]{1,0:T(8,128)S(1)} %slice.49), channel_id=1, source_target_pairs={{0,16},{1,17},{2,18},{3,19},{4,20},{5,21},{6,22},{7,23},{8,24},{9,... | collective-permute-start | bytes 98312 | tf_op jit(solution)/shard_map/ppermute | solution.py:257
  39.6 3.3 %collective-permute-start.18 = (f32[128,128]{1,0:T(8,128)S(1)}, f32[128,128]{1,0:T(8,128)S(1)}, u32[]{:S(2)}, u32[]{:S(2)}) collective-permute-start(f32[128,128]{1,0:T(8,128)S(1)} %add_add_fusion.refs_0_), channel_id=1, source_target_pairs={{0,1},{1,0},{2,3},{3,2},{4,5},{5,4},{6,7},{7,6},{8,9},{9,8},{10,11... | collective-permute-start | bytes 196616 | tf_op jit(solution)/shard_map/ppermute | solution.py:257
  42.3 1.3 %collective-permute-start.21 = (f32[128,128]{1,0:T(8,128)S(1)}, f32[128,128]{1,0:T(8,128)S(1)}, u32[]{:S(2)}, u32[]{:S(2)}) collective-permute-start(f32[128,128]{1,0:T(8,128)S(1)} %collective-permute-done.16.refs_3_), channel_id=1, source_target_pairs={{0,1},{1,0},{2,3},{3,2},{4,5},{5,4},{6,7},{7,6},{8,9},{9,8},{10,11... | collective-permute-start | bytes 196616 | tf_op jit(solution)/shard_map/ppermute | solution.py:257
  42.3 1.4 %collective-permute-start.19 = (f32[128,128]{1,0:T(8,128)S(1)}, f32[128,128]{1,0:T(8,128)S(1)}, u32[]{:S(2)}, u32[]{:S(2)}) collective-permute-start(f32[128,128]{1,0:T(8,128)S(1)} %collective-permute-done.14.refs_1_), channel_id=1, source_target_pairs={{0,1},{1,0},{2,3},{3,2},{4,5},{5,4},{6,7},{7,6},{8,9},{9,8},{10,11... | collective-permute-start | bytes 196616 | tf_op jit(solution)/shard_map/ppermute | solution.py:257
  42.8 1.3 %collective-permute-start.20 = (f32[128,128]{1,0:T(8,128)S(1)}, f32[128,128]{1,0:T(8,128)S(1)}, u32[]{:S(2)}, u32[]{:S(2)}) collective-permute-start(f32[128,128]{1,0:T(8,128)S(1)} %collective-permute-done.15.refs_2_), channel_id=1, source_target_pairs={{0,1},{1,0},{2,3},{3,2},{4,5},{5,4},{6,7},{7,6},{8,9},{9,8},{10,11... | collective-permute-start | bytes 196616 | tf_op jit(solution)/shard_map/ppermute | solution.py:257
  (5 other events, 10.2 us)

commit v3 on v2

--- a/solution.py
+++ b/solution.py
@@ -97,14 +97,6 @@
     return both[:count] + both[count:] + dot(rows[:count], lo)
 
 
-def inverse_near(plus, minus, rows, cols):
-    part = inverse_rows(mixed_back(plus, minus), rows)
-    width = cols.shape[1] // 2
-    hi, lo = split(part)
-    both = dot(hi, cols)
-    return both[:, :width] + both[:, width:] + dot(lo, cols[:, :width])
-
-
 def inverse_wide(plus, minus, rows, cols):
     part = inverse_rows(mixed_back(plus, minus), rows)
     hi, lo = split(part)
@@ -135,9 +127,9 @@
     def pick(near, far, low, odd, edge):
         return jnp.where(low == (odd == 0), near, jnp.where(edge == 1, zero, far))
 
-    side = pick(got[0], got[1], low_col, col_odd, col_edge)
+    side = pick(got[-1], got[-2], low_col, col_odd, col_edge)
     rows = []
-    for n in range(2, len(got), 3):
+    for n in range(0, len(got) - 2, 3):
         rows.append((got[n], pick(got[n + 1], got[n + 2], low_col, col_odd, col_edge)))
     if len(rows) == 1:
         rows.append((zero, zero))
@@ -159,17 +151,20 @@
     half, quarter = place_ref[0], place_ref[1]
     if away:
         half = 1 - half
+    rows = back_ref[base : base + 2 * radius]
+    cols = back_ref[base + 2 * radius : base + 4 * radius]
+    parts = []
     for slot in range(4):
         f = 4 * half + (quarter ^ slot)
         pr, pi, mr, mi = spec_ref[f, 0], spec_ref[f, 1], spec_ref[f, 2], spec_ref[f, 3]
         plus = (pr * ar + pi * ai, pr * ai - pi * ar)
         minus = (mr * br + mi * bi, mr * bi - mi * br)
-        out_ref[slot] = inverse_near(
-            plus,
-            minus,
-            back_ref[base : base + 2 * radius],
-            back_ref[base + 2 * radius : base + 4 * radius],
-        )
+        parts.append(split(inverse_rows(mixed_back(plus, minus), rows)))
+    hi, lo = (jnp.concatenate(p, axis=0) for p in zip(*parts))
+    both = dot(hi, cols)
+    value = both[:, :radius] + both[:, radius:] + dot(lo, cols[:, :radius])
+    for slot in range(4):
+        out_ref[slot] = value[slot * radius : (slot + 1) * radius]
 
 
 def send_kernel(place_ref, spec_ref, own_ref, *rest):
@@ -270,9 +265,11 @@
         return lambda a, b: (row(a, across), col(b, along))
 
     row_moves = (near,) if two else (near, far)
-    pieces = [move(retard, to(stay, near)), move(retard, to(stay, far))]
-    for row in row_moves:
-        pieces += [move(retard, to(row, col)) for col in (stay, near, far)]
+    corners = [[move(retard, to(row, col)) for col in (near, far)] for row in row_moves]
+    pieces = []
+    for corner in corners:
+        pieces += [move(corner[0], to(stay, near)), *corner]
+    pieces += [move(retard, to(stay, col)) for col in (far, near)]
     near_table, filter_table, input_table = table
 
     def call(kernel, outs, name, work, *operands):

time: 45.7 us -> 43.8 us (0.958)
  starting transfers between devices: 25.9 us -> 23.3 us
  waiting for transfers between devices: 7.33 us -> 9 us
  Pallas kernels: 9.32 us -> 8.25 us
    ppermute x22, starting transfers between devices: 25.9 us -> 23.3 us  [move(): return lax.ppermute(value, AXES, pairs)]
    ppermute x22, waiting for transfers between devices: 7.33 us -> 9 us  [move(): return lax.ppermute(value, AXES, pairs)]
    pallas_call x5, Pallas kernels: 9.32 us -> 8.25 us  [call(): pl.pallas_call(kernel, out_shape=outs, in_specs=[SMEM] * scalars + [VMEM]...]
where the time goes in v3:
time: 43.8 us; the launch traced here: 43.5 us
  starting transfers between devices  23.3 us (53%)
  waiting for transfers between devices  9 us (21%)
  Pallas kernels  8.25 us (19%)
  local copies, waits for them, and re-layouts  2.04 us (5%)
  between operations  0.8 us (2%)
    ppermute x22, starting transfers between devices, move(): return lax.ppermute(value, AXES, pairs)  23.3 us
    ppermute x22, waiting for transfers between devices, move(): return lax.ppermute(value, AXES, pairs)  9 us
    pallas_call x5, Pallas kernels, call(): pl.pallas_call(kernel, out_shape=outs, in_specs=[SMEM] * scalars + [VMEM]...  8.25 us
    unnamed x14, local copies, waits for them, and re-layouts  1.94 us
  transfers between devices with their start and end apart: 22, of which 8 were waited for; matrix products, arithmetic and copies ran while one was open for 0% of the time, Pallas kernels for 12%

profile of v3, /device:TPU:0, one launch (start us, length us, event | category | flops | bytes accessed | tf_op | source)
XLA Modules:
  0.0 43.5 jit_solution(15208660027645912597)
XLA Ops:
  0.6 2.5 %collective-permute-start = (bf16[128,128]{1,0:T(8,128)(2,1)}, bf16[128,128]{1,0:T(8,128)(2,1)S(1)}, u32[]{:S(2)}, u32[]{:S(2)}) collective-permute-start(bf16[128,128]{1,0:T(8,128)(2,1)} %own_ref.1), channel_id=1, source_target_pairs={{0,17},{1,16},{2,19},{3,18},{4,21},{5,20},{6,23},{7,22},{8,25},{9,... | collective-permute-start | bytes 98312 | tf_op jit(solution)/shard_map/ppermute | solution.py:252
  3.7 1.4 %collective-permute-start.3 = (bf16[128,128]{1,0:T(8,128)(2,1)}, bf16[128,128]{1,0:T(8,128)(2,1)S(1)}, u32[]{:S(2)}, u32[]{:S(2)}) collective-permute-start(bf16[128,128]{1,0:T(8,128)(2,1)} %own_ref.1), channel_id=1, source_target_pairs={{0,0},{1,2},{2,1},{3,4},{4,3},{5,6},{6,5},{7,8},{8,7},{9,10},{10,9... | collective-permute-start | bytes 98312 | tf_op jit(solution)/shard_map/ppermute | solution.py:252
  5.1 1.6 %collective-permute-start.4 = (bf16[128,128]{1,0:T(8,128)(2,1)}, bf16[128,128]{1,0:T(8,128)(2,1)S(1)}, u32[]{:S(2)}, u32[]{:S(2)}) collective-permute-start(bf16[128,128]{1,0:T(8,128)(2,1)} %own_ref.1), channel_id=1, source_target_pairs={{0,1},{1,0},{2,3},{3,2},{4,5},{5,4},{6,7},{7,6},{8,9},{9,8},{10,11... | collective-permute-start | bytes 98312 | tf_op jit(solution)/shard_map/ppermute | solution.py:252
  6.9 0.9 %copy-done = bf16[8,128,128]{2,1,0:T(8,128)(2,1)S(1)} copy-done((bf16[8,128,128]{2,1,0:T(8,128)(2,1)S(1)}, bf16[8,128,128]{2,1,0:T(8,128)(2,1)}, u32[]{:S(2)}) %copy-start) | copy-done | bytes 262168
  7.8 1.0 %copy-done.5 = bf16[640,256]{1,0:T(8,128)(2,1)S(1)} copy-done((bf16[640,256]{1,0:T(8,128)(2,1)S(1)}, bf16[640,256]{1,0:T(8,128)(2,1)}, u32[]{:S(2)}) %copy-start.5) | copy-done | bytes 327704
  8.8 1.3 %cotangent_spectra.1.spec_ref = f32[8,4,128,128]{3,2,1,0:T(8,128)S(1)} custom-call(bf16[8,128,128]{2,1,0:T(8,128)(2,1)S(1)} %copy-done, bf16[640,256]{1,0:T(8,128)(2,1)S(1)} %copy-done.5), custom_call_target="tpu_custom_call" | custom-call | flops 1468006400 | bytes 589824 | tf_op jit(solution)/shard_map/cotangent_spectra/pallas_call | solution.py:277
  10.2 1.8 %filters_send.1 = (f32[4,128,128]{2,1,0:T(8,128)S(1)}, f32[4,128,128]{2,1,0:T(8,128)S(1)}) custom-call(s32[6]{0:T(128)S(1)} %stack.32.place_ref, f32[8,4,128,128]{3,2,1,0:T(8,128)S(1)} %cotangent_spectra.1.spec_ref, bf16[128,128]{1,0:T(8,128)(2,1)S(1)} %copy-done.2, bf16[128,128]{1,0:T(8,128)(2,1)S(1)} %collective-permute-done.1.rest_0_, ...), custom_call_target="tpu_custom_call" | custom-call | flops 2306867200 | bytes 3211288 | tf_op jit(solution)/shard_map/filters_send/pallas_call | solution.py:277
  12.5 1.2 %filters_keep.1 = f32[4,128,128]{2,1,0:T(8,128)S(1)} custom-call(s32[6]{0:T(128)S(1)} %stack.32.place_ref, f32[8,4,128,128]{3,2,1,0:T(8,128)S(1)} %cotangent_spectra.1.spec_ref, f32[4,128,128]{2,1,0:T(8,128)S(1)} %get-tuple-element.17.window_ref, bf16[1792,256]{1,0:T(8,128)(2,1)S(1)} %copy-done.3), custom_call_target="tpu_custom_call" | custom-call | flops 1677721600 | bytes 3276824 | tf_op jit(solution)/shard_map/filters_keep/pallas_call | solution.py:277
  13.7 3.1 %collective-permute-start.6 = (f32[128,128]{1,0:T(8,128)S(1)}, f32[128,128]{1,0:T(8,128)S(1)}, u32[]{:S(2)}, u32[]{:S(2)}) collective-permute-start(f32[128,128]{1,0:T(8,128)S(1)} %get-tuple-element.20), channel_id=1, source_target_pairs={{0,2},{1,3},{2,0},{3,1},{4,6},{5,7},{6,4},{7,5},{8,10},{9,11},{10,... | collective-permute-start | bytes 196616 | tf_op jit(solution)/shard_map/ppermute | solution.py:252
  16.9 1.5 %collective-permute-start.7 = (f32[128,128]{1,0:T(8,128)S(1)}, f32[128,128]{1,0:T(8,128)S(1)}, u32[]{:S(2)}, u32[]{:S(2)}) collective-permute-start(f32[128,128]{1,0:T(8,128)S(1)} %get-tuple-element.21), channel_id=1, source_target_pairs={{0,16},{1,17},{2,18},{3,19},{4,20},{5,21},{6,22},{7,23},{8,24},{9,... | collective-permute-start | bytes 196616 | tf_op jit(solution)/shard_map/ppermute | solution.py:252
  18.4 2.6 %grad_input.1 = (f32[192,128]{1,0:T(8,128)S(1)}, f32[192,128]{1,0:T(8,128)S(1)}) custom-call(s32[6]{0:T(128)S(1)} %stack.32.place_ref, f32[8,4,128,128]{3,2,1,0:T(8,128)S(1)} %cotangent_spectra.1.spec_ref, bf16[8,128,128]{2,1,0:T(8,128)(2,1)S(1)} %copy-done.1, bf16[640,256]{1,0:T(8,128)(2,1)S(1)} %copy-done.6, bf16[1024,256]{1,0:T(8,128)(2,1)S(1)} %copy-done.4), custom_call_target="tpu_custom_call" | custom-call | flops 2726297600 | bytes 3211288 | tf_op jit(solution)/shard_map/grad_input/pallas_call | solution.py:277
  21.1 2.4 %collective-permute-done.8 = f32[128,128]{1,0:T(8,128)S(1)} collective-permute-done((f32[128,128]{1,0:T(8,128)S(1)}, f32[128,128]{1,0:T(8,128)S(1)}, u32[]{:S(2)}, u32[]{:S(2)}) %collective-permute-start.8) | collective-permute-done | bytes 65568 | tf_op jit(solution)/shard_map/ppermute | solution.py:252
  23.6 1.6 %collective-permute-start.11 = (f32[128,128]{1,0:T(8,128)S(1)}, f32[128,128]{1,0:T(8,128)S(1)}, u32[]{:S(2)}, u32[]{:S(2)}) collective-permute-start(f32[128,128]{1,0:T(8,128)S(1)} %add_add_fusion.1), channel_id=1, source_target_pairs={{0,4},{1,5},{2,6},{3,7},{4,0},{5,1},{6,2},{7,3},{8,12},{9,13},{10,... | collective-permute-start | bytes 196616 | tf_op jit(solution)/shard_map/ppermute | solution.py:252
  25.2 1.3 %collective-permute-start.12 = (f32[128,128]{1,0:T(8,128)S(1)}, f32[128,128]{1,0:T(8,128)S(1)}, u32[]{:S(2)}, u32[]{:S(2)}) collective-permute-start(f32[128,128]{1,0:T(8,128)S(1)} %add_add_fusion.1), channel_id=1, source_target_pairs={{0,8},{1,9},{2,10},{3,11},{4,12},{5,13},{6,14},{7,15},{8,0},{9,1},... | collective-permute-start | bytes 196616 | tf_op jit(solution)/shard_map/ppermute | solution.py:252
  26.5 1.5 %collective-permute-start.13 = (f32[128,128]{1,0:T(8,128)S(1)}, f32[128,128]{1,0:T(8,128)S(1)}, u32[]{:S(2)}, u32[]{:S(2)}) collective-permute-start(f32[128,128]{1,0:T(8,128)S(1)} %add_add_fusion.1), channel_id=1, source_target_pairs={{0,12},{1,13},{2,14},{3,15},{4,8},{5,9},{6,10},{7,11},{8,4},{9,5},... | collective-permute-start | bytes 196616 | tf_op jit(solution)/shard_map/ppermute | solution.py:252
  28.0 0.7 %collective-permute-start.10 = (f32[192,128]{1,0:T(8,128)S(1)}, f32[192,128]{1,0:T(8,128)S(1)}, u32[]{:S(2)}, u32[]{:S(2)}) collective-permute-start(f32[192,128]{1,0:T(8,128)S(1)} %get-tuple-element.24), channel_id=1, source_target_pairs={{0,0},{1,2},{2,1},{3,4},{4,3},{5,6},{6,5},{7,8},{8,7},{9,10},{10,9... | collective-permute-start | bytes 294920 | tf_op jit(solution)/shard_map/ppermute | solution.py:252
  28.7 1.5 %collective-permute-start.9 = (f32[192,128]{1,0:T(8,128)S(1)}, f32[192,128]{1,0:T(8,128)S(1)}, u32[]{:S(2)}, u32[]{:S(2)}) collective-permute-start(f32[192,128]{1,0:T(8,128)S(1)} %get-tuple-element.24), channel_id=1, source_target_pairs={{0,1},{1,0},{2,3},{3,2},{4,5},{5,4},{6,7},{7,6},{8,9},{9,8},{10,11... | collective-permute-start | bytes 294920 | tf_op jit(solution)/shard_map/ppermute | solution.py:252
  30.2 1.1 %collective-permute-done.12 = f32[128,128]{1,0:T(8,128)S(1)} collective-permute-done((f32[128,128]{1,0:T(8,128)S(1)}, f32[128,128]{1,0:T(8,128)S(1)}, u32[]{:S(2)}, u32[]{:S(2)}) %collective-permute-start.12) | collective-permute-done | bytes 65568 | tf_op jit(solution)/shard_map/ppermute | solution.py:252
  31.3 1.4 %collective-permute-done.13 = f32[128,128]{1,0:T(8,128)S(1)} collective-permute-done((f32[128,128]{1,0:T(8,128)S(1)}, f32[128,128]{1,0:T(8,128)S(1)}, u32[]{:S(2)}, u32[]{:S(2)}) %collective-permute-start.13) | collective-permute-done | bytes 65568 | tf_op jit(solution)/shard_map/ppermute | solution.py:252
  32.8 2.7 %collective-permute-start.16 = (f32[128,128]{1,0:T(8,128)S(1)}, f32[128,128]{1,0:T(8,128)S(1)}, u32[]{:S(2)}, u32[]{:S(2)}) collective-permute-start(f32[128,128]{1,0:T(8,128)S(1)} %add_add_fusion.refs_0_), channel_id=1, source_target_pairs={{0,18},{1,19},{2,16},{3,17},{4,22},{5,23},{6,20},{7,21},{8,26},{9,... | collective-permute-start | bytes 196616 | tf_op jit(solution)/shard_map/ppermute | solution.py:252
  35.6 0.9 %collective-permute-start.15 = (f32[128,128]{1,0:T(8,128)S(1)}, f32[128,128]{1,0:T(8,128)S(1)}, u32[]{:S(2)}, u32[]{:S(2)}) collective-permute-start(f32[128,128]{1,0:T(8,128)S(1)} %add_add_fusion.refs_0_), channel_id=1, source_target_pairs={{0,16},{1,17},{2,18},{3,19},{4,20},{5,21},{6,22},{7,23},{8,24},{9,... | collective-permute-start | bytes 196616 | tf_op jit(solution)/shard_map/ppermute | solution.py:252
  36.4 1.2 %collective-permute-start.17 = (f32[64,128]{1,0:T(8,128)S(1)}, f32[64,128]{1,0:T(8,128)S(1)}, u32[]{:S(2)}, u32[]{:S(2)}) collective-permute-start(f32[64,128]{1,0:T(8,128)S(1)} %slice.49), channel_id=1, source_target_pairs={{0,16},{1,17},{2,18},{3,19},{4,20},{5,21},{6,22},{7,23},{8,24},{9,... | collective-permute-start | bytes 98312 | tf_op jit(solution)/shard_map/ppermute | solution.py:252
  37.6 2.7 %collective-permute-done.17.refs_8_ = f32[64,128]{1,0:T(8,128)S(1)} collective-permute-done((f32[64,128]{1,0:T(8,128)S(1)}, f32[64,128]{1,0:T(8,128)S(1)}, u32[]{:S(2)}, u32[]{:S(2)}) %collective-permute-start.17) | collective-permute-done | bytes 32800 | tf_op jit(solution)/shard_map/ppermute | solution.py:252
  42.1 1.4 %gather_filters.1 = (f32[128,128]{1,0:T(8,128)}, f32[8,128,128]{2,1,0:T(8,128)}) custom-call(s32[6]{0:T(128)S(1)} %stack.32.place_ref, f32[128,128]{1,0:T(8,128)S(1)} %slice.48.own_ref, f32[128,128]{1,0:T(8,128)S(1)} %add_add_fusion.refs_0_, f32[128,128]{1,0:T(8,128)S(1)} %collective-permute-done.14.refs_1_, f32[128,128]{1,0:T(8,128)S(1)} %collective-permute-done.15.refs_2_, ...), custom_call_target="tpu_custom_call" | custom-call | bytes 622616 | tf_op jit(solution)/shard_map/gather_filters/pallas_call | solution.py:277
  (47 shorter events, 3.3 us)
Async XLA Ops:
  0.6 6.1 %collective-permute-start = (bf16[128,128]{1,0:T(8,128)(2,1)}, bf16[128,128]{1,0:T(8,128)(2,1)S(1)}, u32[]{:S(2)}, u32[]{:S(2)}) collective-permute-start(bf16[128,128]{1,0:T(8,128)(2,1)} %own_ref.1), channel_id=1, source_target_pairs={{0,17},{1,16},{2,19},{3,18},{4,21},{5,20},{6,23},{7,22},{8,25},{9,... | collective-permute-start | bytes 98312 | tf_op jit(solution)/shard_map/ppermute | solution.py:252
  3.1 7.1 %collective-permute-start.2 = (bf16[128,128]{1,0:T(8,128)(2,1)}, bf16[128,128]{1,0:T(8,128)(2,1)S(1)}, u32[]{:S(2)}, u32[]{:S(2)}) collective-permute-start(bf16[128,128]{1,0:T(8,128)(2,1)} %own_ref.1), channel_id=1, source_target_pairs={{0,16},{1,18},{2,17},{3,20},{4,19},{5,22},{6,21},{7,24},{8,23},{9,... | collective-permute-start | bytes 98312 | tf_op jit(solution)/shard_map/ppermute | solution.py:252
  3.7 6.4 %collective-permute-start.3 = (bf16[128,128]{1,0:T(8,128)(2,1)}, bf16[128,128]{1,0:T(8,128)(2,1)S(1)}, u32[]{:S(2)}, u32[]{:S(2)}) collective-permute-start(bf16[128,128]{1,0:T(8,128)(2,1)} %own_ref.1), channel_id=1, source_target_pairs={{0,0},{1,2},{2,1},{3,4},{4,3},{5,6},{6,5},{7,8},{8,7},{9,10},{10,9... | collective-permute-start | bytes 98312 | tf_op jit(solution)/shard_map/ppermute | solution.py:252
  5.1 5.0 %collective-permute-start.4 = (bf16[128,128]{1,0:T(8,128)(2,1)}, bf16[128,128]{1,0:T(8,128)(2,1)S(1)}, u32[]{:S(2)}, u32[]{:S(2)}) collective-permute-start(bf16[128,128]{1,0:T(8,128)(2,1)} %own_ref.1), channel_id=1, source_target_pairs={{0,1},{1,0},{2,3},{3,2},{4,5},{5,4},{6,7},{7,6},{8,9},{9,8},{10,11... | collective-permute-start | bytes 98312 | tf_op jit(solution)/shard_map/ppermute | solution.py:252
  6.8 3.4 %collective-permute-start.1 = (bf16[128,128]{1,0:T(8,128)(2,1)S(1)}, bf16[128,128]{1,0:T(8,128)(2,1)S(1)}, u32[]{:S(2)}, u32[]{:S(2)}) collective-permute-start(bf16[128,128]{1,0:T(8,128)(2,1)S(1)} %collective-permute-done.rest_1_), channel_id=1, source_target_pairs={{0,1},{1,0},{2,3},{3,2},{4,5},{5,4},{6,7},{7,6},{8,9},{9,8},{10,11... | collective-permute-start | bytes 98312 | tf_op jit(solution)/shard_map/ppermute | solution.py:252
  12.0 1.7 %collective-permute-start.5 = (f32[4,128,128]{2,1,0:T(8,128)S(1)}, f32[4,128,128]{2,1,0:T(8,128)S(1)}, u32[]{:S(2)}, u32[]{:S(2)}) collective-permute-start(f32[4,128,128]{2,1,0:T(8,128)S(1)} %get-tuple-element.18), channel_id=1, source_target_pairs={{0,1},{1,0},{2,3},{3,2},{4,5},{5,4},{6,7},{7,6},{8,9},{9,8},{10,11... | collective-permute-start | bytes 786440 | tf_op jit(solution)/shard_map/ppermute | solution.py:252
  12.5 6.0 %copy-start.4 = (bf16[1024,256]{1,0:T(8,128)(2,1)S(1)}, bf16[1024,256]{1,0:T(8,128)(2,1)}, u32[]{:S(2)}) copy-start(bf16[1024,256]{1,0:T(8,128)(2,1)} %constant.29.clone.back_ref) | copy-start | bytes 1572868
  12.5 6.0 %copy-start.6 = (bf16[640,256]{1,0:T(8,128)(2,1)S(1)}, bf16[640,256]{1,0:T(8,128)(2,1)}, u32[]{:S(2)}) copy-start(bf16[640,256]{1,0:T(8,128)(2,1)} %constant.27.clone.table_ref) | copy-start | bytes 983044
  13.7 7.3 %collective-permute-start.6 = (f32[128,128]{1,0:T(8,128)S(1)}, f32[128,128]{1,0:T(8,128)S(1)}, u32[]{:S(2)}, u32[]{:S(2)}) collective-permute-start(f32[128,128]{1,0:T(8,128)S(1)} %get-tuple-element.20), channel_id=1, source_target_pairs={{0,2},{1,3},{2,0},{3,1},{4,6},{5,7},{6,4},{7,5},{8,10},{9,11},{10,... | collective-permute-start | bytes 196616 | tf_op jit(solution)/shard_map/ppermute | solution.py:252
  16.9 4.3 %collective-permute-start.7 = (f32[128,128]{1,0:T(8,128)S(1)}, f32[128,128]{1,0:T(8,128)S(1)}, u32[]{:S(2)}, u32[]{:S(2)}) collective-permute-start(f32[128,128]{1,0:T(8,128)S(1)} %get-tuple-element.21), channel_id=1, source_target_pairs={{0,16},{1,17},{2,18},{3,19},{4,20},{5,21},{6,22},{7,23},{8,24},{9,... | collective-permute-start | bytes 196616 | tf_op jit(solution)/shard_map/ppermute | solution.py:252
  18.4 5.2 %collective-permute-start.8 = (f32[128,128]{1,0:T(8,128)S(1)}, f32[128,128]{1,0:T(8,128)S(1)}, u32[]{:S(2)}, u32[]{:S(2)}) collective-permute-start(f32[128,128]{1,0:T(8,128)S(1)} %get-tuple-element.22), channel_id=1, source_target_pairs={{0,18},{1,19},{2,16},{3,17},{4,22},{5,23},{6,20},{7,21},{8,26},{9,... | collective-permute-start | bytes 196616 | tf_op jit(solution)/shard_map/ppermute | solution.py:252
  23.6 6.6 %collective-permute-start.11 = (f32[128,128]{1,0:T(8,128)S(1)}, f32[128,128]{1,0:T(8,128)S(1)}, u32[]{:S(2)}, u32[]{:S(2)}) collective-permute-start(f32[128,128]{1,0:T(8,128)S(1)} %add_add_fusion.1), channel_id=1, source_target_pairs={{0,4},{1,5},{2,6},{3,7},{4,0},{5,1},{6,2},{7,3},{8,12},{9,13},{10,... | collective-permute-start | bytes 196616 | tf_op jit(solution)/shard_map/ppermute | solution.py:252
  25.2 6.1 %collective-permute-start.12 = (f32[128,128]{1,0:T(8,128)S(1)}, f32[128,128]{1,0:T(8,128)S(1)}, u32[]{:S(2)}, u32[]{:S(2)}) collective-permute-start(f32[128,128]{1,0:T(8,128)S(1)} %add_add_fusion.1), channel_id=1, source_target_pairs={{0,8},{1,9},{2,10},{3,11},{4,12},{5,13},{6,14},{7,15},{8,0},{9,1},... | collective-permute-start | bytes 196616 | tf_op jit(solution)/shard_map/ppermute | solution.py:252
  26.5 6.2 %collective-permute-start.13 = (f32[128,128]{1,0:T(8,128)S(1)}, f32[128,128]{1,0:T(8,128)S(1)}, u32[]{:S(2)}, u32[]{:S(2)}) collective-permute-start(f32[128,128]{1,0:T(8,128)S(1)} %add_add_fusion.1), channel_id=1, source_target_pairs={{0,12},{1,13},{2,14},{3,15},{4,8},{5,9},{6,10},{7,11},{8,4},{9,5},... | collective-permute-start | bytes 196616 | tf_op jit(solution)/shard_map/ppermute | solution.py:252
  28.0 4.8 %collective-permute-start.10 = (f32[192,128]{1,0:T(8,128)S(1)}, f32[192,128]{1,0:T(8,128)S(1)}, u32[]{:S(2)}, u32[]{:S(2)}) collective-permute-start(f32[192,128]{1,0:T(8,128)S(1)} %get-tuple-element.24), channel_id=1, source_target_pairs={{0,0},{1,2},{2,1},{3,4},{4,3},{5,6},{6,5},{7,8},{8,7},{9,10},{10,9... | collective-permute-start | bytes 294920 | tf_op jit(solution)/shard_map/ppermute | solution.py:252
  28.7 4.1 %collective-permute-start.9 = (f32[192,128]{1,0:T(8,128)S(1)}, f32[192,128]{1,0:T(8,128)S(1)}, u32[]{:S(2)}, u32[]{:S(2)}) collective-permute-start(f32[192,128]{1,0:T(8,128)S(1)} %get-tuple-element.24), channel_id=1, source_target_pairs={{0,1},{1,0},{2,3},{3,2},{4,5},{5,4},{6,7},{7,6},{8,9},{9,8},{10,11... | collective-permute-start | bytes 294920 | tf_op jit(solution)/shard_map/ppermute | solution.py:252
  32.8 7.5 %collective-permute-start.16 = (f32[128,128]{1,0:T(8,128)S(1)}, f32[128,128]{1,0:T(8,128)S(1)}, u32[]{:S(2)}, u32[]{:S(2)}) collective-permute-start(f32[128,128]{1,0:T(8,128)S(1)} %add_add_fusion.refs_0_), channel_id=1, source_target_pairs={{0,18},{1,19},{2,16},{3,17},{4,22},{5,23},{6,20},{7,21},{8,26},{9,... | collective-permute-start | bytes 196616 | tf_op jit(solution)/shard_map/ppermute | solution.py:252
  35.6 4.8 %collective-permute-start.14 = (f32[128,128]{1,0:T(8,128)S(1)}, f32[128,128]{1,0:T(8,128)S(1)}, u32[]{:S(2)}, u32[]{:S(2)}) collective-permute-start(f32[128,128]{1,0:T(8,128)S(1)} %add_add_fusion.refs_0_), channel_id=1, source_target_pairs={{0,2},{1,3},{2,0},{3,1},{4,6},{5,7},{6,4},{7,5},{8,10},{9,11},{10,... | collective-permute-start | bytes 196616 | tf_op jit(solution)/shard_map/ppermute | solution.py:252
  35.6 5.3 %collective-permute-start.15 = (f32[128,128]{1,0:T(8,128)S(1)}, f32[128,128]{1,0:T(8,128)S(1)}, u32[]{:S(2)}, u32[]{:S(2)}) collective-permute-start(f32[128,128]{1,0:T(8,128)S(1)} %add_add_fusion.refs_0_), channel_id=1, source_target_pairs={{0,16},{1,17},{2,18},{3,19},{4,20},{5,21},{6,22},{7,23},{8,24},{9,... | collective-permute-start | bytes 196616 | tf_op jit(solution)/shard_map/ppermute | solution.py:252
  36.4 3.9 %collective-permute-start.17 = (f32[64,128]{1,0:T(8,128)S(1)}, f32[64,128]{1,0:T(8,128)S(1)}, u32[]{:S(2)}, u32[]{:S(2)}) collective-permute-start(f32[64,128]{1,0:T(8,128)S(1)} %slice.49), channel_id=1, source_target_pairs={{0,16},{1,17},{2,18},{3,19},{4,20},{5,21},{6,22},{7,23},{8,24},{9,... | collective-permute-start | bytes 98312 | tf_op jit(solution)/shard_map/ppermute | solution.py:252
  37.6 3.4 %collective-permute-start.18 = (f32[128,128]{1,0:T(8,128)S(1)}, f32[128,128]{1,0:T(8,128)S(1)}, u32[]{:S(2)}, u32[]{:S(2)}) collective-permute-start(f32[128,128]{1,0:T(8,128)S(1)} %add_add_fusion.refs_0_), channel_id=1, source_target_pairs={{0,1},{1,0},{2,3},{3,2},{4,5},{5,4},{6,7},{7,6},{8,9},{9,8},{10,11... | collective-permute-start | bytes 196616 | tf_op jit(solution)/shard_map/ppermute | solution.py:252
  40.3 1.3 %collective-permute-start.21 = (f32[128,128]{1,0:T(8,128)S(1)}, f32[128,128]{1,0:T(8,128)S(1)}, u32[]{:S(2)}, u32[]{:S(2)}) collective-permute-start(f32[128,128]{1,0:T(8,128)S(1)} %collective-permute-done.16.refs_3_), channel_id=1, source_target_pairs={{0,1},{1,0},{2,3},{3,2},{4,5},{5,4},{6,7},{7,6},{8,9},{9,8},{10,11... | collective-permute-start | bytes 196616 | tf_op jit(solution)/shard_map/ppermute | solution.py:252
  40.4 1.4 %collective-permute-start.19 = (f32[128,128]{1,0:T(8,128)S(1)}, f32[128,128]{1,0:T(8,128)S(1)}, u32[]{:S(2)}, u32[]{:S(2)}) collective-permute-start(f32[128,128]{1,0:T(8,128)S(1)} %collective-permute-done.14.refs_1_), channel_id=1, source_target_pairs={{0,1},{1,0},{2,3},{3,2},{4,5},{5,4},{6,7},{7,6},{8,9},{9,8},{10,11... | collective-permute-start | bytes 196616 | tf_op jit(solution)/shard_map/ppermute | solution.py:252
  40.9 1.3 %collective-permute-start.20 = (f32[128,128]{1,0:T(8,128)S(1)}, f32[128,128]{1,0:T(8,128)S(1)}, u32[]{:S(2)}, u32[]{:S(2)}) collective-permute-start(f32[128,128]{1,0:T(8,128)S(1)} %collective-permute-done.15.refs_2_), channel_id=1, source_target_pairs={{0,1},{1,0},{2,3},{3,2},{4,5},{5,4},{6,7},{7,6},{8,9},{9,8},{10,11... | collective-permute-start | bytes 196616 | tf_op jit(solution)/shard_map/ppermute | solution.py:252
  (5 other events, 10.7 us)

commit v4 on v3

--- a/solution.py
+++ b/solution.py
@@ -206,23 +206,6 @@
     side_ref[...] = full[:, radius:]
 
 
-def gather_kernel(place_ref, own_ref, *refs):
-    pieces, strips, input_ref, out_ref = refs[:8], refs[8:-2], refs[-2], refs[-1]
-    core, quarter, row_edge, row_odd = (place_ref[n] for n in range(4))
-    for slot in range(8):
-        half = core if slot < 4 else 1 - core
-        out_ref[4 * half + (quarter ^ (slot % 4))] = pieces[slot][...]
-    shape = own_ref.shape
-    low_row = lax.broadcasted_iota(jnp.int32, shape, 0) < shape[0] // 2
-    zero = jnp.zeros(shape, f32)
-    if len(strips) == 1:
-        strip = strips[0][...]
-        near, far = jnp.concatenate([strip, strip], axis=0), zero
-    else:
-        near, far = strips[0][...], jnp.where(row_edge == 1, zero, strips[1][...])
-    input_ref[...] = own_ref[...] + jnp.where(low_row == (row_odd == 1), near, far)
-
-
 VMEM = pl.BlockSpec(memory_space=pltpu.VMEM)
 SMEM = pl.BlockSpec(memory_space=pltpu.SMEM)
 LIMIT = pltpu.CompilerParams(vmem_limit_bytes=12 * 1024 * 1024)
@@ -328,7 +311,7 @@
     got = move(send, lambda a, b: (a, b ^ 1))
     mine = lax.optimization_barrier([keep[n] + got[n] for n in range(4)])
     flips = [lambda a, b, n=n: (a ^ (n >> 1), b ^ ((n & 1) << 1)) for n in range(4)]
-    value = mine[0] + sum(move(mine[n], flips[n]) for n in range(1, 4))
+    value = mine[0] + sum(move(mine[n], flips[n]) for n in (3, 2, 1))
     bits = [(0, 1 << s) for s in range(2, (along - 1).bit_length())]
     bits += [(1 << s, 0) for s in range(1, (across - 1).bit_length())]
     for start in range(0, len(bits), 2):
@@ -338,26 +321,25 @@
             value, side = lax.optimization_barrier((value, side))
             beside = [move(side, to(stay, col)) for col in (near, far)]
         value = value + sum(
-            move(value, lambda a, b, m=m: (a ^ m[0], b ^ m[1])) for m in masks
+            move(value, lambda a, b, m=m: (a ^ m[0], b ^ m[1])) for m in masks[::-1]
         )
     low_col = lax.broadcasted_iota(jnp.int32, tall.shape, 1) < radius // 2
     other = jnp.where((col_index == 0) | (col_index == along - 1), 0.0, beside[1])
     own = own + jnp.where(low_col == (col_index & 1 == 1), beside[0], other)
-    value, strip = lax.optimization_barrier((value, own[radius:]))
-    strips = [move(strip, to(row, stay)) for row in row_moves]
+    strips = [move(own[radius:], to(row, stay)) for row in row_moves]
     parts = [value] + [move(value, flips[n]) for n in range(1, 4)]
-    parts[3], strips = lax.optimization_barrier((parts[3], strips))
     parts += [move(part, lambda a, b: (a, b ^ 1)) for part in parts]
-    return call(
-        gather_kernel,
-        (arrays(radius, radius), arrays(count, radius, radius)),
-        "gather_filters",
-        0,
-        place,
-        own[:radius],
-        *parts,
-        *strips,
-    )
+    for bit, flag in enumerate((col_index >> 1, row_index, col_index)):
+        swap = flag & 1 == 1
+        parts = [jnp.where(swap, parts[n ^ (1 << bit)], parts[n]) for n in range(8)]
+    grad_filters = jnp.stack(parts)
+    low_row = lax.broadcasted_iota(jnp.int32, (radius, radius), 0) < radius // 2
+    near_strip = jnp.concatenate([strips[0]] * 2, axis=0) if two else strips[0]
+    far_strip = 0.0
+    if not two:
+        far_strip = jnp.where((row_index == 0) | (row_index == across - 1), 0.0, strips[1])
+    grad_input = own[:radius] + jnp.where(low_row == (row_index & 1 == 1), near_strip, far_strip)
+    return grad_input, grad_filters
 
 
 def solution(mesh):

time: 43.8 us -> 40.9 us (0.934)
  waiting for transfers between devices: 9 us -> 4.82 us
  Pallas kernels: 8.25 us -> 6.88 us
  starting transfers between devices: 23.3 us -> 24.3 us
  other arithmetic: 0.1 us -> 1 us
  local copies, waits for them, and re-layouts: 2.04 us -> 2.82 us
    ppermute x22, waiting for transfers between devices: 9 us -> 4.82 us  [move(): return lax.ppermute(value, AXES, pairs)]
    pallas_call x5 -> x4, Pallas kernels: 8.25 us -> 6.88 us  [call(): pl.pallas_call(kernel, out_shape=outs, in_specs=[SMEM] * scalars + [VMEM]...]
    ppermute x22, starting transfers between devices: 23.3 us -> 24.3 us  [move(): return lax.ppermute(value, AXES, pairs)]
    unnamed x14 -> x16, local copies, waits for them, and re-layouts: 1.94 us -> 2.73 us
    add x1 -> x2, other arithmetic: 0.02 us -> 0.73 us  [the longest x1 0.72 us: local(): own[:radius]]
  transfers between devices with their start and end apart: 22 -> 22, of which waited for: 8 -> 7; matrix products, arithmetic and copies ran while one was open for 0% -> 2% of each run, Pallas kernels for 12% -> 13%
where the time goes in v4:
time: 40.9 us; the launch traced here: 40.7 us
  starting transfers between devices  24.3 us (59%)
  Pallas kernels  6.88 us (17%)
  waiting for transfers between devices  4.82 us (12%)
  local copies, waits for them, and re-layouts  2.82 us (7%)
  other arithmetic  1 us (2%)
  between operations  0.87 us (2%)
    ppermute x22, starting transfers between devices, move(): return lax.ppermute(value, AXES, pairs)  24.3 us
    pallas_call x4, Pallas kernels, call(): pl.pallas_call(kernel, out_shape=outs, in_specs=[SMEM] * scalars + [VMEM]...  6.88 us
    ppermute x22, waiting for transfers between devices, move(): return lax.ppermute(value, AXES, pairs)  4.82 us
    unnamed x16, local copies, waits for them, and re-layouts  2.73 us
  transfers between devices with their start and end apart: 22, of which 7 were waited for; matrix products, arithmetic and copies ran while one was open for 2% of the time, Pallas kernels for 13%

profile of v4, /device:TPU:0, one launch (start us, length us, event | category | flops | bytes accessed | tf_op | source)
XLA Modules:
  0.0 40.7 jit_solution(13679247520924528901)
XLA Ops:
  0.6 2.5 %collective-permute-start = (bf16[128,128]{1,0:T(8,128)(2,1)}, bf16[128,128]{1,0:T(8,128)(2,1)S(1)}, u32[]{:S(2)}, u32[]{:S(2)}) collective-permute-start(bf16[128,128]{1,0:T(8,128)(2,1)} %own_ref.1), channel_id=1, source_target_pairs={{0,17},{1,16},{2,19},{3,18},{4,21},{5,20},{6,23},{7,22},{8,25},{9,... | collective-permute-start | bytes 98312 | tf_op jit(solution)/shard_map/ppermute | solution.py:235
  3.1 0.6 %collective-permute-start.2 = (bf16[128,128]{1,0:T(8,128)(2,1)}, bf16[128,128]{1,0:T(8,128)(2,1)S(1)}, u32[]{:S(2)}, u32[]{:S(2)}) collective-permute-start(bf16[128,128]{1,0:T(8,128)(2,1)} %own_ref.1), channel_id=1, source_target_pairs={{0,16},{1,18},{2,17},{3,20},{4,19},{5,22},{6,21},{7,24},{8,23},{9,... | collective-permute-start | bytes 98312 | tf_op jit(solution)/shard_map/ppermute | solution.py:235
  3.7 1.4 %collective-permute-start.3 = (bf16[128,128]{1,0:T(8,128)(2,1)}, bf16[128,128]{1,0:T(8,128)(2,1)S(1)}, u32[]{:S(2)}, u32[]{:S(2)}) collective-permute-start(bf16[128,128]{1,0:T(8,128)(2,1)} %own_ref.1), channel_id=1, source_target_pairs={{0,0},{1,2},{2,1},{3,4},{4,3},{5,6},{6,5},{7,8},{8,7},{9,10},{10,9... | collective-permute-start | bytes 98312 | tf_op jit(solution)/shard_map/ppermute | solution.py:235
  5.1 1.6 %collective-permute-start.4 = (bf16[128,128]{1,0:T(8,128)(2,1)}, bf16[128,128]{1,0:T(8,128)(2,1)S(1)}, u32[]{:S(2)}, u32[]{:S(2)}) collective-permute-start(bf16[128,128]{1,0:T(8,128)(2,1)} %own_ref.1), channel_id=1, source_target_pairs={{0,1},{1,0},{2,3},{3,2},{4,5},{5,4},{6,7},{7,6},{8,9},{9,8},{10,11... | collective-permute-start | bytes 98312 | tf_op jit(solution)/shard_map/ppermute | solution.py:235
  6.9 0.9 %copy-done = bf16[8,128,128]{2,1,0:T(8,128)(2,1)S(1)} copy-done((bf16[8,128,128]{2,1,0:T(8,128)(2,1)S(1)}, bf16[8,128,128]{2,1,0:T(8,128)(2,1)}, u32[]{:S(2)}) %copy-start) | copy-done | bytes 262168
  7.8 1.0 %copy-done.5 = bf16[640,256]{1,0:T(8,128)(2,1)S(1)} copy-done((bf16[640,256]{1,0:T(8,128)(2,1)S(1)}, bf16[640,256]{1,0:T(8,128)(2,1)}, u32[]{:S(2)}) %copy-start.5) | copy-done | bytes 327704
  8.8 1.3 %cotangent_spectra.1.spec_ref = f32[8,4,128,128]{3,2,1,0:T(8,128)S(1)} custom-call(bf16[8,128,128]{2,1,0:T(8,128)(2,1)S(1)} %copy-done, bf16[640,256]{1,0:T(8,128)(2,1)S(1)} %copy-done.5), custom_call_target="tpu_custom_call" | custom-call | flops 1468006400 | bytes 589824 | tf_op jit(solution)/shard_map/cotangent_spectra/pallas_call | solution.py:260
  10.2 1.8 %filters_send.1 = (f32[4,128,128]{2,1,0:T(8,128)S(1)}, f32[4,128,128]{2,1,0:T(8,128)S(1)}) custom-call(s32[6]{0:T(128)S(1)} %stack.59.place_ref, f32[8,4,128,128]{3,2,1,0:T(8,128)S(1)} %cotangent_spectra.1.spec_ref, bf16[128,128]{1,0:T(8,128)(2,1)S(1)} %copy-done.2, bf16[128,128]{1,0:T(8,128)(2,1)S(1)} %collective-permute-done.1.rest_0_, ...), custom_call_target="tpu_custom_call" | custom-call | flops 2306867200 | bytes 3211288 | tf_op jit(solution)/shard_map/filters_send/pallas_call | solution.py:260
  12.5 1.2 %filters_keep.1 = f32[4,128,128]{2,1,0:T(8,128)S(1)} custom-call(s32[6]{0:T(128)S(1)} %stack.59.place_ref, f32[8,4,128,128]{3,2,1,0:T(8,128)S(1)} %cotangent_spectra.1.spec_ref, f32[4,128,128]{2,1,0:T(8,128)S(1)} %get-tuple-element.13.window_ref, bf16[1792,256]{1,0:T(8,128)(2,1)S(1)} %copy-done.3), custom_call_target="tpu_custom_call" | custom-call | flops 1677721600 | bytes 3276824 | tf_op jit(solution)/shard_map/filters_keep/pallas_call | solution.py:260
  13.8 4.1 %collective-permute-start.6 = (f32[128,128]{1,0:T(8,128)S(1)}, f32[128,128]{1,0:T(8,128)S(1)}, u32[]{:S(2)}, u32[]{:S(2)}) collective-permute-start(f32[128,128]{1,0:T(8,128)S(1)} %get-tuple-element.16), channel_id=1, source_target_pairs={{0,18},{1,19},{2,16},{3,17},{4,22},{5,23},{6,20},{7,21},{8,26},{9,... | collective-permute-start | bytes 196616 | tf_op jit(solution)/shard_map/ppermute | solution.py:235
  18.5 2.6 %grad_input.1 = (f32[192,128]{1,0:T(8,128)S(1)}, f32[192,128]{1,0:T(8,128)S(1)}) custom-call(s32[6]{0:T(128)S(1)} %stack.59.place_ref, f32[8,4,128,128]{3,2,1,0:T(8,128)S(1)} %cotangent_spectra.1.spec_ref, bf16[8,128,128]{2,1,0:T(8,128)(2,1)S(1)} %copy-done.1, bf16[640,256]{1,0:T(8,128)(2,1)S(1)} %copy-done.6, bf16[1024,256]{1,0:T(8,128)(2,1)S(1)} %copy-done.4), custom_call_target="tpu_custom_call" | custom-call | flops 2726297600 | bytes 3211288 | tf_op jit(solution)/shard_map/grad_input/pallas_call | solution.py:260
  21.1 1.0 %collective-permute-done.7 = f32[128,128]{1,0:T(8,128)S(1)} collective-permute-done((f32[128,128]{1,0:T(8,128)S(1)}, f32[128,128]{1,0:T(8,128)S(1)}, u32[]{:S(2)}, u32[]{:S(2)}) %collective-permute-start.7) | collective-permute-done | bytes 65568 | tf_op jit(solution)/shard_map/ppermute | solution.py:235
  22.6 2.7 %collective-permute-start.12 = (f32[128,128]{1,0:T(8,128)S(1)}, f32[128,128]{1,0:T(8,128)S(1)}, u32[]{:S(2)}, u32[]{:S(2)}) collective-permute-start(f32[128,128]{1,0:T(8,128)S(1)} %add_add_fusion.1), channel_id=1, source_target_pairs={{0,12},{1,13},{2,14},{3,15},{4,8},{5,9},{6,10},{7,11},{8,4},{9,5},... | collective-permute-start | bytes 196616 | tf_op jit(solution)/shard_map/ppermute | solution.py:235
  25.7 1.3 %collective-permute-start.14 = (f32[128,128]{1,0:T(8,128)S(1)}, f32[128,128]{1,0:T(8,128)S(1)}, u32[]{:S(2)}, u32[]{:S(2)}) collective-permute-start(f32[128,128]{1,0:T(8,128)S(1)} %add_add_fusion.1), channel_id=1, source_target_pairs={{0,4},{1,5},{2,6},{3,7},{4,0},{5,1},{6,2},{7,3},{8,12},{9,13},{10,... | collective-permute-start | bytes 196616 | tf_op jit(solution)/shard_map/ppermute | solution.py:235
  27.1 0.7 %collective-permute-start.10 = (f32[192,128]{1,0:T(8,128)S(1)}, f32[192,128]{1,0:T(8,128)S(1)}, u32[]{:S(2)}, u32[]{:S(2)}) collective-permute-start(f32[192,128]{1,0:T(8,128)S(1)} %get-tuple-element.20), channel_id=1, source_target_pairs={{0,0},{1,2},{2,1},{3,4},{4,3},{5,6},{6,5},{7,8},{8,7},{9,10},{10,9... | collective-permute-start | bytes 294920 | tf_op jit(solution)/shard_map/ppermute | solution.py:235
  27.8 2.3 %collective-permute-start.9 = (f32[192,128]{1,0:T(8,128)S(1)}, f32[192,128]{1,0:T(8,128)S(1)}, u32[]{:S(2)}, u32[]{:S(2)}) collective-permute-start(f32[192,128]{1,0:T(8,128)S(1)} %get-tuple-element.20), channel_id=1, source_target_pairs={{0,1},{1,0},{2,3},{3,2},{4,5},{5,4},{6,7},{7,6},{8,9},{9,8},{10,11... | collective-permute-start | bytes 294920 | tf_op jit(solution)/shard_map/ppermute | solution.py:235
  30.1 1.2 %collective-permute-done.13 = f32[128,128]{1,0:T(8,128)S(1)} collective-permute-done((f32[128,128]{1,0:T(8,128)S(1)}, f32[128,128]{1,0:T(8,128)S(1)}, u32[]{:S(2)}, u32[]{:S(2)}) %collective-permute-start.13) | collective-permute-done | bytes 65568 | tf_op jit(solution)/shard_map/ppermute | solution.py:235
  31.3 1.7 %collective-permute-start.15 = (f32[128,128]{1,0:T(8,128)S(1)}, f32[128,128]{1,0:T(8,128)S(1)}, u32[]{:S(2)}, u32[]{:S(2)}) collective-permute-start(f32[128,128]{1,0:T(8,128)S(1)} %add_add_fusion), channel_id=1, source_target_pairs={{0,18},{1,19},{2,16},{3,17},{4,22},{5,23},{6,20},{7,21},{8,26},{9,... | collective-permute-start | bytes 196616 | tf_op jit(solution)/shard_map/ppermute | solution.py:235
  33.0 1.1 %collective-permute-start.17 = (f32[128,128]{1,0:T(8,128)S(1)}, f32[128,128]{1,0:T(8,128)S(1)}, u32[]{:S(2)}, u32[]{:S(2)}) collective-permute-start(f32[128,128]{1,0:T(8,128)S(1)} %add_add_fusion), channel_id=1, source_target_pairs={{0,16},{1,17},{2,18},{3,19},{4,20},{5,21},{6,22},{7,23},{8,24},{9,... | collective-permute-start | bytes 196616 | tf_op jit(solution)/shard_map/ppermute | solution.py:235
  34.1 0.8 %collective-permute-start.19 = (f32[128,128]{1,0:T(8,128)S(1)}, f32[128,128]{1,0:T(8,128)S(1)}, u32[]{:S(2)}, u32[]{:S(2)}) collective-permute-start(f32[128,128]{1,0:T(8,128)S(1)} %add_add_fusion), channel_id=1, source_target_pairs={{0,2},{1,3},{2,0},{3,1},{4,6},{5,7},{6,4},{7,5},{8,10},{9,11},{10,... | collective-permute-start | bytes 196616 | tf_op jit(solution)/shard_map/ppermute | solution.py:235
  34.9 1.8 %collective-permute-start.11 = (f32[64,128]{1,0:T(8,128)S(1)}, f32[64,128]{1,0:T(8,128)S(1)}, u32[]{:S(2)}, u32[]{:S(2)}) collective-permute-start(f32[64,128]{1,0:T(8,128)S(1)} %slice.49), channel_id=1, source_target_pairs={{0,16},{1,17},{2,18},{3,19},{4,20},{5,21},{6,22},{7,23},{8,24},{9,... | collective-permute-start | bytes 98312 | tf_op jit(solution)/shard_map/ppermute | solution.py:235
  38.3 0.6 %collective-permute-done.11 = f32[64,128]{1,0:T(8,128)S(1)} collective-permute-done((f32[64,128]{1,0:T(8,128)S(1)}, f32[64,128]{1,0:T(8,128)S(1)}, u32[]{:S(2)}, u32[]{:S(2)}) %collective-permute-start.11) | collective-permute-done | bytes 32800 | tf_op jit(solution)/shard_map/ppermute | solution.py:235
  38.9 0.7 %slice_add_fusion = f32[128,128]{1,0:T(8,128)} fusion(f32[192,128]{1,0:T(8,128)S(1)} %select_add_fusion, f32[64,128]{1,0:T(8,128)S(1)} %collective-permute-done.11, pred[128]{0:T(512)(128)(4,1)S(1)} %compare_compare_fusion), kind=kLoop, calls=%fused_computation.1 | loop fusion | flops 49152 | bytes 163968 | tf_op jit(solution)/shard_map/add | solution.py:341
  39.9 0.8 %copy-done.7 = f32[8,128,128]{2,1,0:T(8,128)} copy-done((f32[8,128,128]{2,1,0:T(8,128)}, f32[8,128,128]{2,1,0:T(8,128)S(1)}, u32[]{:S(2)}) %copy-start.7) | copy-done | bytes 524312
  (57 shorter events, 4.1 us)
Async XLA Ops:
  0.6 6.1 %collective-permute-start = (bf16[128,128]{1,0:T(8,128)(2,1)}, bf16[128,128]{1,0:T(8,128)(2,1)S(1)}, u32[]{:S(2)}, u32[]{:S(2)}) collective-permute-start(bf16[128,128]{1,0:T(8,128)(2,1)} %own_ref.1), channel_id=1, source_target_pairs={{0,17},{1,16},{2,19},{3,18},{4,21},{5,20},{6,23},{7,22},{8,25},{9,... | collective-permute-start | bytes 98312 | tf_op jit(solution)/shard_map/ppermute | solution.py:235
  3.1 7.1 %collective-permute-start.2 = (bf16[128,128]{1,0:T(8,128)(2,1)}, bf16[128,128]{1,0:T(8,128)(2,1)S(1)}, u32[]{:S(2)}, u32[]{:S(2)}) collective-permute-start(bf16[128,128]{1,0:T(8,128)(2,1)} %own_ref.1), channel_id=1, source_target_pairs={{0,16},{1,18},{2,17},{3,20},{4,19},{5,22},{6,21},{7,24},{8,23},{9,... | collective-permute-start | bytes 98312 | tf_op jit(solution)/shard_map/ppermute | solution.py:235
  3.7 6.4 %collective-permute-start.3 = (bf16[128,128]{1,0:T(8,128)(2,1)}, bf16[128,128]{1,0:T(8,128)(2,1)S(1)}, u32[]{:S(2)}, u32[]{:S(2)}) collective-permute-start(bf16[128,128]{1,0:T(8,128)(2,1)} %own_ref.1), channel_id=1, source_target_pairs={{0,0},{1,2},{2,1},{3,4},{4,3},{5,6},{6,5},{7,8},{8,7},{9,10},{10,9... | collective-permute-start | bytes 98312 | tf_op jit(solution)/shard_map/ppermute | solution.py:235
  5.1 5.0 %collective-permute-start.4 = (bf16[128,128]{1,0:T(8,128)(2,1)}, bf16[128,128]{1,0:T(8,128)(2,1)S(1)}, u32[]{:S(2)}, u32[]{:S(2)}) collective-permute-start(bf16[128,128]{1,0:T(8,128)(2,1)} %own_ref.1), channel_id=1, source_target_pairs={{0,1},{1,0},{2,3},{3,2},{4,5},{5,4},{6,7},{7,6},{8,9},{9,8},{10,11... | collective-permute-start | bytes 98312 | tf_op jit(solution)/shard_map/ppermute | solution.py:235
  6.8 3.4 %collective-permute-start.1 = (bf16[128,128]{1,0:T(8,128)(2,1)S(1)}, bf16[128,128]{1,0:T(8,128)(2,1)S(1)}, u32[]{:S(2)}, u32[]{:S(2)}) collective-permute-start(bf16[128,128]{1,0:T(8,128)(2,1)S(1)} %collective-permute-done.rest_1_), channel_id=1, source_target_pairs={{0,1},{1,0},{2,3},{3,2},{4,5},{5,4},{6,7},{7,6},{8,9},{9,8},{10,11... | collective-permute-start | bytes 98312 | tf_op jit(solution)/shard_map/ppermute | solution.py:235
  12.0 1.7 %collective-permute-start.5 = (f32[4,128,128]{2,1,0:T(8,128)S(1)}, f32[4,128,128]{2,1,0:T(8,128)S(1)}, u32[]{:S(2)}, u32[]{:S(2)}) collective-permute-start(f32[4,128,128]{2,1,0:T(8,128)S(1)} %get-tuple-element.14), channel_id=1, source_target_pairs={{0,1},{1,0},{2,3},{3,2},{4,5},{5,4},{6,7},{7,6},{8,9},{9,8},{10,11... | collective-permute-start | bytes 786440 | tf_op jit(solution)/shard_map/ppermute | solution.py:235
  12.5 6.0 %copy-start.4 = (bf16[1024,256]{1,0:T(8,128)(2,1)S(1)}, bf16[1024,256]{1,0:T(8,128)(2,1)}, u32[]{:S(2)}) copy-start(bf16[1024,256]{1,0:T(8,128)(2,1)} %constant.30.clone.back_ref) | copy-start | bytes 1572868
  12.5 6.0 %copy-start.6 = (bf16[640,256]{1,0:T(8,128)(2,1)S(1)}, bf16[640,256]{1,0:T(8,128)(2,1)}, u32[]{:S(2)}) copy-start(bf16[640,256]{1,0:T(8,128)(2,1)} %constant.28.clone.table_ref) | copy-start | bytes 983044
  13.8 7.4 %collective-permute-start.6 = (f32[128,128]{1,0:T(8,128)S(1)}, f32[128,128]{1,0:T(8,128)S(1)}, u32[]{:S(2)}, u32[]{:S(2)}) collective-permute-start(f32[128,128]{1,0:T(8,128)S(1)} %get-tuple-element.16), channel_id=1, source_target_pairs={{0,18},{1,19},{2,16},{3,17},{4,22},{5,23},{6,20},{7,21},{8,26},{9,... | collective-permute-start | bytes 196616 | tf_op jit(solution)/shard_map/ppermute | solution.py:235
  17.8 4.3 %collective-permute-start.7 = (f32[128,128]{1,0:T(8,128)S(1)}, f32[128,128]{1,0:T(8,128)S(1)}, u32[]{:S(2)}, u32[]{:S(2)}) collective-permute-start(f32[128,128]{1,0:T(8,128)S(1)} %get-tuple-element.17), channel_id=1, source_target_pairs={{0,16},{1,17},{2,18},{3,19},{4,20},{5,21},{6,22},{7,23},{8,24},{9,... | collective-permute-start | bytes 196616 | tf_op jit(solution)/shard_map/ppermute | solution.py:235
  18.3 4.3 %collective-permute-start.8 = (f32[128,128]{1,0:T(8,128)S(1)}, f32[128,128]{1,0:T(8,128)S(1)}, u32[]{:S(2)}, u32[]{:S(2)}) collective-permute-start(f32[128,128]{1,0:T(8,128)S(1)} %get-tuple-element.18), channel_id=1, source_target_pairs={{0,2},{1,3},{2,0},{3,1},{4,6},{5,7},{6,4},{7,5},{8,10},{9,11},{10,... | collective-permute-start | bytes 196616 | tf_op jit(solution)/shard_map/ppermute | solution.py:235
  22.6 7.5 %collective-permute-start.12 = (f32[128,128]{1,0:T(8,128)S(1)}, f32[128,128]{1,0:T(8,128)S(1)}, u32[]{:S(2)}, u32[]{:S(2)}) collective-permute-start(f32[128,128]{1,0:T(8,128)S(1)} %add_add_fusion.1), channel_id=1, source_target_pairs={{0,12},{1,13},{2,14},{3,15},{4,8},{5,9},{6,10},{7,11},{8,4},{9,5},... | collective-permute-start | bytes 196616 | tf_op jit(solution)/shard_map/ppermute | solution.py:235
  25.3 5.9 %collective-permute-start.13 = (f32[128,128]{1,0:T(8,128)S(1)}, f32[128,128]{1,0:T(8,128)S(1)}, u32[]{:S(2)}, u32[]{:S(2)}) collective-permute-start(f32[128,128]{1,0:T(8,128)S(1)} %add_add_fusion.1), channel_id=1, source_target_pairs={{0,8},{1,9},{2,10},{3,11},{4,12},{5,13},{6,14},{7,15},{8,0},{9,1},... | collective-permute-start | bytes 196616 | tf_op jit(solution)/shard_map/ppermute | solution.py:235
  25.7 5.6 %collective-permute-start.14 = (f32[128,128]{1,0:T(8,128)S(1)}, f32[128,128]{1,0:T(8,128)S(1)}, u32[]{:S(2)}, u32[]{:S(2)}) collective-permute-start(f32[128,128]{1,0:T(8,128)S(1)} %add_add_fusion.1), channel_id=1, source_target_pairs={{0,4},{1,5},{2,6},{3,7},{4,0},{5,1},{6,2},{7,3},{8,12},{9,13},{10,... | collective-permute-start | bytes 196616 | tf_op jit(solution)/shard_map/ppermute | solution.py:235
  27.1 7.8 %collective-permute-start.10 = (f32[192,128]{1,0:T(8,128)S(1)}, f32[192,128]{1,0:T(8,128)S(1)}, u32[]{:S(2)}, u32[]{:S(2)}) collective-permute-start(f32[192,128]{1,0:T(8,128)S(1)} %get-tuple-element.20), channel_id=1, source_target_pairs={{0,0},{1,2},{2,1},{3,4},{4,3},{5,6},{6,5},{7,8},{8,7},{9,10},{10,9... | collective-permute-start | bytes 294920 | tf_op jit(solution)/shard_map/ppermute | solution.py:235
  27.8 7.1 %collective-permute-start.9 = (f32[192,128]{1,0:T(8,128)S(1)}, f32[192,128]{1,0:T(8,128)S(1)}, u32[]{:S(2)}, u32[]{:S(2)}) collective-permute-start(f32[192,128]{1,0:T(8,128)S(1)} %get-tuple-element.20), channel_id=1, source_target_pairs={{0,1},{1,0},{2,3},{3,2},{4,5},{5,4},{6,7},{7,6},{8,9},{9,8},{10,11... | collective-permute-start | bytes 294920 | tf_op jit(solution)/shard_map/ppermute | solution.py:235
  31.3 5.9 %collective-permute-start.15 = (f32[128,128]{1,0:T(8,128)S(1)}, f32[128,128]{1,0:T(8,128)S(1)}, u32[]{:S(2)}, u32[]{:S(2)}) collective-permute-start(f32[128,128]{1,0:T(8,128)S(1)} %add_add_fusion), channel_id=1, source_target_pairs={{0,18},{1,19},{2,16},{3,17},{4,22},{5,23},{6,20},{7,21},{8,26},{9,... | collective-permute-start | bytes 196616 | tf_op jit(solution)/shard_map/ppermute | solution.py:235
  33.0 4.8 %collective-permute-start.17 = (f32[128,128]{1,0:T(8,128)S(1)}, f32[128,128]{1,0:T(8,128)S(1)}, u32[]{:S(2)}, u32[]{:S(2)}) collective-permute-start(f32[128,128]{1,0:T(8,128)S(1)} %add_add_fusion), channel_id=1, source_target_pairs={{0,16},{1,17},{2,18},{3,19},{4,20},{5,21},{6,22},{7,23},{8,24},{9,... | collective-permute-start | bytes 196616 | tf_op jit(solution)/shard_map/ppermute | solution.py:235
  34.1 4.3 %collective-permute-start.19 = (f32[128,128]{1,0:T(8,128)S(1)}, f32[128,128]{1,0:T(8,128)S(1)}, u32[]{:S(2)}, u32[]{:S(2)}) collective-permute-start(f32[128,128]{1,0:T(8,128)S(1)} %add_add_fusion), channel_id=1, source_target_pairs={{0,2},{1,3},{2,0},{3,1},{4,6},{5,7},{6,4},{7,5},{8,10},{9,11},{10,... | collective-permute-start | bytes 196616 | tf_op jit(solution)/shard_map/ppermute | solution.py:235
  34.9 4.0 %collective-permute-start.11 = (f32[64,128]{1,0:T(8,128)S(1)}, f32[64,128]{1,0:T(8,128)S(1)}, u32[]{:S(2)}, u32[]{:S(2)}) collective-permute-start(f32[64,128]{1,0:T(8,128)S(1)} %slice.49), channel_id=1, source_target_pairs={{0,16},{1,17},{2,18},{3,19},{4,20},{5,21},{6,22},{7,23},{8,24},{9,... | collective-permute-start | bytes 98312 | tf_op jit(solution)/shard_map/ppermute | solution.py:235
  36.7 2.9 %collective-permute-start.21 = (f32[128,128]{1,0:T(8,128)S(1)}, f32[128,128]{1,0:T(8,128)S(1)}, u32[]{:S(2)}, u32[]{:S(2)}) collective-permute-start(f32[128,128]{1,0:T(8,128)S(1)} %add_add_fusion), channel_id=1, source_target_pairs={{0,1},{1,0},{2,3},{3,2},{4,5},{5,4},{6,7},{7,6},{8,9},{9,8},{10,11... | collective-permute-start | bytes 196616 | tf_op jit(solution)/shard_map/ppermute | solution.py:235
  37.2 2.4 %collective-permute-start.16 = (f32[128,128]{1,0:T(8,128)S(1)}, f32[128,128]{1,0:T(8,128)S(1)}, u32[]{:S(2)}, u32[]{:S(2)}) collective-permute-start(f32[128,128]{1,0:T(8,128)S(1)} %collective-permute-done.15), channel_id=1, source_target_pairs={{0,1},{1,0},{2,3},{3,2},{4,5},{5,4},{6,7},{7,6},{8,9},{9,8},{10,11... | collective-permute-start | bytes 196616 | tf_op jit(solution)/shard_map/ppermute | solution.py:235
  37.8 1.8 %collective-permute-start.18 = (f32[128,128]{1,0:T(8,128)S(1)}, f32[128,128]{1,0:T(8,128)S(1)}, u32[]{:S(2)}, u32[]{:S(2)}) collective-permute-start(f32[128,128]{1,0:T(8,128)S(1)} %collective-permute-done.17), channel_id=1, source_target_pairs={{0,1},{1,0},{2,3},{3,2},{4,5},{5,4},{6,7},{7,6},{8,9},{9,8},{10,11... | collective-permute-start | bytes 196616 | tf_op jit(solution)/shard_map/ppermute | solution.py:235
  38.3 1.3 %collective-permute-start.20 = (f32[128,128]{1,0:T(8,128)S(1)}, f32[128,128]{1,0:T(8,128)S(1)}, u32[]{:S(2)}, u32[]{:S(2)}) collective-permute-start(f32[128,128]{1,0:T(8,128)S(1)} %collective-permute-done.19), channel_id=1, source_target_pairs={{0,1},{1,0},{2,3},{3,2},{4,5},{5,4},{6,7},{7,6},{8,9},{9,8},{10,11... | collective-permute-start | bytes 196616 | tf_op jit(solution)/shard_map/ppermute | solution.py:235
  (6 other events, 11.6 us)

commit v5 on v4

--- a/solution.py
+++ b/solution.py
@@ -36,9 +36,6 @@
     cos_n, sin_n = turn(near)
     cos_w, sin_w = turn(wide)
     scale = 2.0 / period**2
-    rows_near = np.concatenate(halves(stack(cos_n, sin_n)), axis=1)
-    hi, lo = halves(stack(cos_n, -sin_n).T)
-    cols_near = stack(hi, hi, lo)
     rows_wide = stack(*halves(stack(cos_w, sin_w)))
     hi, lo = halves(stack(cos_w, -sin_w).T)
     cols_wide = stack(hi, hi, lo)
@@ -47,7 +44,6 @@
     back_rows_wide = stack(*halves(stack(cos_w, sin_w).T))
     back_cols_wide = stack(*halves(stack(cos_w, -sin_w) * scale))
     return (
-        stack(rows_near, cols_near),
         stack(rows_wide, cols_wide, back_rows_near, back_cols_near),
         stack(back_rows_wide, back_cols_wide),
     )
@@ -102,6 +98,33 @@
     hi, lo = split(part)
     upper, lower = cols[: cols.shape[0] // 2], cols[cols.shape[0] // 2 :]
     return dot(hi, upper) + dot(hi, lower) + dot(lo, upper)
+
+
+def table_kernel(out_ref):
+    radius = out_ref.shape[1] // 2
+    shape = (radius, radius)
+    first = lax.broadcasted_iota(jnp.int32, shape, 0)
+    second = lax.broadcasted_iota(jnp.int32, shape, 1)
+
+    def turn(freq, position):
+        steps = lax.rem((2 * freq + 1) * position, 4 * radius) - 2 * radius
+        half = steps.astype(f32) * (math.pi / (4 * radius))
+        square = half * half
+        cosine, sine = jnp.ones(shape, f32), jnp.ones(shape, f32)
+        for n in range(7, 0, -1):
+            cosine = 1.0 - cosine * square * (1.0 / (2 * n * (2 * n - 1)))
+            sine = 1.0 - sine * square * (1.0 / (2 * n * (2 * n + 1)))
+        sine = sine * half
+        return 2.0 * sine * sine - 1.0, -2.0 * sine * cosine
+
+    for n, part in enumerate(turn(first, second)):
+        hi, lo = split(part)
+        out_ref[n * radius : (n + 1) * radius, :radius] = hi
+        out_ref[n * radius : (n + 1) * radius, radius:] = lo
+    for n, part in enumerate(turn(second, first)):
+        hi, lo = split(part if n == 0 else -part)
+        for place, value in zip((2, 3, 4), (hi, hi, lo)):
+            out_ref[place * radius : (place + 1) * radius, n * radius : (n + 1) * radius] = value
 
 
 def cotangent_kernel(cot_ref, table_ref, out_ref):
@@ -171,7 +194,7 @@
     pieces, (table_ref, out_ref, window_ref) = rest[:-3], rest[-3:]
     radius = own_ref.shape[0]
     side = 2 * radius
-    window = window_of(own_ref[...], pieces, place_ref)
+    window = window_of(own_ref[...], pieces[::-1], place_ref)
     mixed = dot(table_ref[:side], window) + dot(table_ref[side : 2 * side], window)
     hi, lo = split(mixed)
     mixed = dot(jnp.concatenate([hi, lo, hi], axis=1), table_ref[2 * side : 5 * side])
@@ -253,10 +276,10 @@
     for corner in corners:
         pieces += [move(corner[0], to(stay, near)), *corner]
     pieces += [move(retard, to(stay, col)) for col in (far, near)]
-    near_table, filter_table, input_table = table
+    filter_table, input_table = table
 
     def call(kernel, outs, name, work, *operands):
-        scalars = operands[0] is place
+        scalars = bool(operands) and operands[0] is place
         return pl.pallas_call(
             kernel,
             out_shape=outs,
@@ -274,6 +297,12 @@
     def arrays(*shape):
         return jax.ShapeDtypeStruct(shape, f32)
 
+    near_table = call(
+        table_kernel,
+        jax.ShapeDtypeStruct((5 * radius, 2 * radius), bf16),
+        "near_table",
+        20,
+    )
     spectra = call(
         cotangent_kernel,
         arrays(count, 4, radius, radius),
@@ -291,7 +320,7 @@
         place,
         spectra,
         retard,
-        *pieces,
+        *pieces[::-1],
         filter_table,
     )
     keep = call(keep_kernel, half, "filters_keep", 800, place, spectra, window, filter_table)
@@ -321,7 +350,7 @@
             value, side = lax.optimization_barrier((value, side))
             beside = [move(side, to(stay, col)) for col in (near, far)]
         value = value + sum(
-            move(value, lambda a, b, m=m: (a ^ m[0], b ^ m[1])) for m in masks[::-1]
+            move(value, lambda a, b, m=m: (a ^ m[0], b ^ m[1])) for m in masks
         )
     low_col = lax.broadcasted_iota(jnp.int32, tall.shape, 1) < radius // 2
     other = jnp.where((col_index == 0) | (col_index == along - 1), 0.0, beside[1])
@@ -330,8 +359,8 @@
     parts = [value] + [move(value, flips[n]) for n in range(1, 4)]
     parts += [move(part, lambda a, b: (a, b ^ 1)) for part in parts]
     for bit, flag in enumerate((col_index >> 1, row_index, col_index)):
-        swap = flag & 1 == 1
-        parts = [jnp.where(swap, parts[n ^ (1 << bit)], parts[n]) for n in range(8)]
+        stay = flag & 1 == 0
+        parts = [jnp.where(stay, parts[n], parts[n ^ (1 << bit)]) for n in range(8)]
     grad_filters = jnp.stack(parts)
     low_row = lax.broadcasted_iota(jnp.int32, (radius, radius), 0) < radius // 2
     near_strip = jnp.concatenate([strips[0]] * 2, axis=0) if two else strips[0]

time: 40.9 us -> 40.5 us (level)
  local copies, waits for them, and re-layouts: 2.82 us -> 1.84 us
    unnamed x16 -> x12, local copies, waits for them, and re-layouts: 2.73 us -> 1.75 us
    pallas_call x4 -> x5, Pallas kernels: 6.88 us -> 7.18 us  [call(): pl.pallas_call(kernel, out_shape=outs, in_specs=[SMEM] * scalars + [VMEM]...]
  transfers between devices with their start and end apart: 22 -> 22, of which waited for: 7 -> 8; matrix products, arithmetic and copies ran while one was open for 2% -> 2% of each run, Pallas kernels for 13% -> 13%
where the time goes in v5:
time: 40.5 us; the launch traced here: 40.2 us
  starting transfers between devices  24.4 us (60%)
  Pallas kernels  7.18 us (18%)
  waiting for transfers between devices  4.91 us (12%)
  local copies, waits for them, and re-layouts  1.84 us (5%)
  other arithmetic  1 us (2%)
  between operations  0.86 us (2%)
    ppermute x22, starting transfers between devices, move(): return lax.ppermute(value, AXES, pairs)  24.4 us
    pallas_call x5, Pallas kernels, call(): pl.pallas_call(kernel, out_shape=outs, in_specs=[SMEM] * scalars + [VMEM]...  7.18 us
    ppermute x22, waiting for transfers between devices, move(): return lax.ppermute(value, AXES, pairs)  4.91 us
    unnamed x12, local copies, waits for them, and re-layouts  1.75 us
  transfers between devices with their start and end apart: 22, of which 8 were waited for; matrix products, arithmetic and copies ran while one was open for 2% of the time, Pallas kernels for 13%

profile of v5, /device:TPU:0, one launch (start us, length us, event | category | flops | bytes accessed | tf_op | source)
XLA Modules:
  0.0 40.2 jit_solution(5955847688248396525)
XLA Ops:
  0.6 2.5 %collective-permute-start.3 = (bf16[128,128]{1,0:T(8,128)(2,1)}, bf16[128,128]{1,0:T(8,128)(2,1)S(1)}, u32[]{:S(2)}, u32[]{:S(2)}) collective-permute-start(bf16[128,128]{1,0:T(8,128)(2,1)} %own_ref.1), channel_id=1, source_target_pairs={{0,17},{1,16},{2,19},{3,18},{4,21},{5,20},{6,23},{7,22},{8,25},{9,... | collective-permute-start | bytes 98312 | tf_op jit(solution)/shard_map/ppermute | solution.py:258
  3.1 0.6 %collective-permute-start.2 = (bf16[128,128]{1,0:T(8,128)(2,1)}, bf16[128,128]{1,0:T(8,128)(2,1)S(1)}, u32[]{:S(2)}, u32[]{:S(2)}) collective-permute-start(bf16[128,128]{1,0:T(8,128)(2,1)} %own_ref.1), channel_id=1, source_target_pairs={{0,16},{1,18},{2,17},{3,20},{4,19},{5,22},{6,21},{7,24},{8,23},{9,... | collective-permute-start | bytes 98312 | tf_op jit(solution)/shard_map/ppermute | solution.py:258
  3.7 1.4 %collective-permute-start.1 = (bf16[128,128]{1,0:T(8,128)(2,1)}, bf16[128,128]{1,0:T(8,128)(2,1)S(1)}, u32[]{:S(2)}, u32[]{:S(2)}) collective-permute-start(bf16[128,128]{1,0:T(8,128)(2,1)} %own_ref.1), channel_id=1, source_target_pairs={{0,0},{1,2},{2,1},{3,4},{4,3},{5,6},{6,5},{7,8},{8,7},{9,10},{10,9... | collective-permute-start | bytes 98312 | tf_op jit(solution)/shard_map/ppermute | solution.py:258
  5.1 1.6 %collective-permute-start = (bf16[128,128]{1,0:T(8,128)(2,1)}, bf16[128,128]{1,0:T(8,128)(2,1)S(1)}, u32[]{:S(2)}, u32[]{:S(2)}) collective-permute-start(bf16[128,128]{1,0:T(8,128)(2,1)} %own_ref.1), channel_id=1, source_target_pairs={{0,1},{1,0},{2,3},{3,2},{4,5},{5,4},{6,7},{7,6},{8,9},{9,8},{10,11... | collective-permute-start | bytes 98312 | tf_op jit(solution)/shard_map/ppermute | solution.py:258
  7.2 0.9 %copy-done = bf16[8,128,128]{2,1,0:T(8,128)(2,1)S(1)} copy-done((bf16[8,128,128]{2,1,0:T(8,128)(2,1)S(1)}, bf16[8,128,128]{2,1,0:T(8,128)(2,1)}, u32[]{:S(2)}) %copy-start) | copy-done | bytes 262168
  8.1 1.3 %cotangent_spectra.1.spec_ref = f32[8,4,128,128]{3,2,1,0:T(8,128)S(1)} custom-call(bf16[8,128,128]{2,1,0:T(8,128)(2,1)S(1)} %copy-done, bf16[640,256]{1,0:T(8,128)(2,1)S(1)} %near_table.1.table_ref), custom_call_target="tpu_custom_call" | custom-call | flops 1468006400 | bytes 589824 | tf_op jit(solution)/shard_map/cotangent_spectra/pallas_call | solution.py:283
  9.6 1.8 %filters_send.1 = (f32[4,128,128]{2,1,0:T(8,128)S(1)}, f32[4,128,128]{2,1,0:T(8,128)S(1)}) custom-call(s32[6]{0:T(128)S(1)} %stack.59.place_ref, f32[8,4,128,128]{3,2,1,0:T(8,128)S(1)} %cotangent_spectra.1.spec_ref, bf16[128,128]{1,0:T(8,128)(2,1)S(1)} %copy-done.2, bf16[128,128]{1,0:T(8,128)(2,1)S(1)} %collective-permute-done.rest_0_, ...), custom_call_target="tpu_custom_call" | custom-call | flops 2306867200 | bytes 3211288 | tf_op jit(solution)/shard_map/filters_send/pallas_call | solution.py:283
  11.3 0.7 %collective-permute-start.5 = (f32[4,128,128]{2,1,0:T(8,128)S(1)}, f32[4,128,128]{2,1,0:T(8,128)S(1)}, u32[]{:S(2)}, u32[]{:S(2)}) collective-permute-start(f32[4,128,128]{2,1,0:T(8,128)S(1)} %get-tuple-element.14), channel_id=1, source_target_pairs={{0,1},{1,0},{2,3},{3,2},{4,5},{5,4},{6,7},{7,6},{8,9},{9,8},{10,11... | collective-permute-start | bytes 786440 | tf_op jit(solution)/shard_map/ppermute | solution.py:258
  12.1 1.2 %filters_keep.1 = f32[4,128,128]{2,1,0:T(8,128)S(1)} custom-call(s32[6]{0:T(128)S(1)} %stack.59.place_ref, f32[8,4,128,128]{3,2,1,0:T(8,128)S(1)} %cotangent_spectra.1.spec_ref, f32[4,128,128]{2,1,0:T(8,128)S(1)} %get-tuple-element.13.window_ref, bf16[1792,256]{1,0:T(8,128)(2,1)S(1)} %copy-done.3), custom_call_target="tpu_custom_call" | custom-call | flops 1677721600 | bytes 3276824 | tf_op jit(solution)/shard_map/filters_keep/pallas_call | solution.py:283
  13.3 3.9 %collective-permute-start.6 = (f32[128,128]{1,0:T(8,128)S(1)}, f32[128,128]{1,0:T(8,128)S(1)}, u32[]{:S(2)}, u32[]{:S(2)}) collective-permute-start(f32[128,128]{1,0:T(8,128)S(1)} %get-tuple-element.16), channel_id=1, source_target_pairs={{0,18},{1,19},{2,16},{3,17},{4,22},{5,23},{6,20},{7,21},{8,26},{9,... | collective-permute-start | bytes 196616 | tf_op jit(solution)/shard_map/ppermute | solution.py:258
  17.9 2.6 %grad_input.1 = (f32[192,128]{1,0:T(8,128)S(1)}, f32[192,128]{1,0:T(8,128)S(1)}) custom-call(s32[6]{0:T(128)S(1)} %stack.59.place_ref, f32[8,4,128,128]{3,2,1,0:T(8,128)S(1)} %cotangent_spectra.1.spec_ref, bf16[8,128,128]{2,1,0:T(8,128)(2,1)S(1)} %copy-done.1, bf16[640,256]{1,0:T(8,128)(2,1)S(1)} %near_table.1.table_ref, bf16[1024,256]{1,0:T(8,128)(2,1)S(1)} %copy-done.4), custom_call_target="tpu_custom_call" | custom-call | flops 2726297600 | bytes 3211288 | tf_op jit(solution)/shard_map/grad_input/pallas_call | solution.py:283
  20.5 1.0 %collective-permute-done.7 = f32[128,128]{1,0:T(8,128)S(1)} collective-permute-done((f32[128,128]{1,0:T(8,128)S(1)}, f32[128,128]{1,0:T(8,128)S(1)}, u32[]{:S(2)}, u32[]{:S(2)}) %collective-permute-start.7) | collective-permute-done | bytes 65568 | tf_op jit(solution)/shard_map/ppermute | solution.py:258
  22.0 2.7 %collective-permute-start.14 = (f32[128,128]{1,0:T(8,128)S(1)}, f32[128,128]{1,0:T(8,128)S(1)}, u32[]{:S(2)}, u32[]{:S(2)}) collective-permute-start(f32[128,128]{1,0:T(8,128)S(1)} %add_add_fusion.1), channel_id=1, source_target_pairs={{0,12},{1,13},{2,14},{3,15},{4,8},{5,9},{6,10},{7,11},{8,4},{9,5},... | collective-permute-start | bytes 196616 | tf_op jit(solution)/shard_map/ppermute | solution.py:258
  25.1 1.3 %collective-permute-start.12 = (f32[128,128]{1,0:T(8,128)S(1)}, f32[128,128]{1,0:T(8,128)S(1)}, u32[]{:S(2)}, u32[]{:S(2)}) collective-permute-start(f32[128,128]{1,0:T(8,128)S(1)} %add_add_fusion.1), channel_id=1, source_target_pairs={{0,4},{1,5},{2,6},{3,7},{4,0},{5,1},{6,2},{7,3},{8,12},{9,13},{10,... | collective-permute-start | bytes 196616 | tf_op jit(solution)/shard_map/ppermute | solution.py:258
  26.5 0.7 %collective-permute-start.10 = (f32[192,128]{1,0:T(8,128)S(1)}, f32[192,128]{1,0:T(8,128)S(1)}, u32[]{:S(2)}, u32[]{:S(2)}) collective-permute-start(f32[192,128]{1,0:T(8,128)S(1)} %get-tuple-element.20), channel_id=1, source_target_pairs={{0,0},{1,2},{2,1},{3,4},{4,3},{5,6},{6,5},{7,8},{8,7},{9,10},{10,9... | collective-permute-start | bytes 294920 | tf_op jit(solution)/shard_map/ppermute | solution.py:258
  27.2 2.3 %collective-permute-start.9 = (f32[192,128]{1,0:T(8,128)S(1)}, f32[192,128]{1,0:T(8,128)S(1)}, u32[]{:S(2)}, u32[]{:S(2)}) collective-permute-start(f32[192,128]{1,0:T(8,128)S(1)} %get-tuple-element.20), channel_id=1, source_target_pairs={{0,1},{1,0},{2,3},{3,2},{4,5},{5,4},{6,7},{7,6},{8,9},{9,8},{10,11... | collective-permute-start | bytes 294920 | tf_op jit(solution)/shard_map/ppermute | solution.py:258
  29.5 1.2 %collective-permute-done.13 = f32[128,128]{1,0:T(8,128)S(1)} collective-permute-done((f32[128,128]{1,0:T(8,128)S(1)}, f32[128,128]{1,0:T(8,128)S(1)}, u32[]{:S(2)}, u32[]{:S(2)}) %collective-permute-start.13) | collective-permute-done | bytes 65568 | tf_op jit(solution)/shard_map/ppermute | solution.py:258
  30.7 1.7 %collective-permute-start.17 = (f32[128,128]{1,0:T(8,128)S(1)}, f32[128,128]{1,0:T(8,128)S(1)}, u32[]{:S(2)}, u32[]{:S(2)}) collective-permute-start(f32[128,128]{1,0:T(8,128)S(1)} %add_add_fusion), channel_id=1, source_target_pairs={{0,18},{1,19},{2,16},{3,17},{4,22},{5,23},{6,20},{7,21},{8,26},{9,... | collective-permute-start | bytes 196616 | tf_op jit(solution)/shard_map/ppermute | solution.py:258
  32.5 1.2 %collective-permute-start.16 = (f32[128,128]{1,0:T(8,128)S(1)}, f32[128,128]{1,0:T(8,128)S(1)}, u32[]{:S(2)}, u32[]{:S(2)}) collective-permute-start(f32[128,128]{1,0:T(8,128)S(1)} %add_add_fusion), channel_id=1, source_target_pairs={{0,16},{1,17},{2,18},{3,19},{4,20},{5,21},{6,22},{7,23},{8,24},{9,... | collective-permute-start | bytes 196616 | tf_op jit(solution)/shard_map/ppermute | solution.py:258
  33.7 0.6 %collective-permute-start.15 = (f32[128,128]{1,0:T(8,128)S(1)}, f32[128,128]{1,0:T(8,128)S(1)}, u32[]{:S(2)}, u32[]{:S(2)}) collective-permute-start(f32[128,128]{1,0:T(8,128)S(1)} %add_add_fusion), channel_id=1, source_target_pairs={{0,2},{1,3},{2,0},{3,1},{4,6},{5,7},{6,4},{7,5},{8,10},{9,11},{10,... | collective-permute-start | bytes 196616 | tf_op jit(solution)/shard_map/ppermute | solution.py:258
  34.3 1.8 %collective-permute-start.11 = (f32[64,128]{1,0:T(8,128)S(1)}, f32[64,128]{1,0:T(8,128)S(1)}, u32[]{:S(2)}, u32[]{:S(2)}) collective-permute-start(f32[64,128]{1,0:T(8,128)S(1)} %slice.49), channel_id=1, source_target_pairs={{0,16},{1,17},{2,18},{3,19},{4,20},{5,21},{6,22},{7,23},{8,24},{9,... | collective-permute-start | bytes 98312 | tf_op jit(solution)/shard_map/ppermute | solution.py:258
  37.2 0.7 %collective-permute-done.15 = f32[128,128]{1,0:T(8,128)S(1)} collective-permute-done((f32[128,128]{1,0:T(8,128)S(1)}, f32[128,128]{1,0:T(8,128)S(1)}, u32[]{:S(2)}, u32[]{:S(2)}) %collective-permute-start.15) | collective-permute-done | bytes 65568 | tf_op jit(solution)/shard_map/ppermute | solution.py:258
  38.3 0.7 %slice_add_fusion = f32[128,128]{1,0:T(8,128)} fusion(f32[192,128]{1,0:T(8,128)S(1)} %select_add_fusion, f32[64,128]{1,0:T(8,128)S(1)} %collective-permute-done.11, pred[128]{0:T(512)(128)(4,1)S(1)} %compare_compare_fusion), kind=kLoop, calls=%fused_computation.1 | loop fusion | flops 49152 | bytes 163968 | tf_op jit(solution)/shard_map/add | solution.py:370
  39.5 0.8 %copy-done.5 = f32[8,128,128]{2,1,0:T(8,128)} copy-done((f32[8,128,128]{2,1,0:T(8,128)}, f32[8,128,128]{2,1,0:T(8,128)S(1)}, u32[]{:S(2)}) %copy-start.5) | copy-done | bytes 524312
  (54 shorter events, 3.9 us)
Async XLA Ops:
  0.6 6.4 %collective-permute-start.3 = (bf16[128,128]{1,0:T(8,128)(2,1)}, bf16[128,128]{1,0:T(8,128)(2,1)S(1)}, u32[]{:S(2)}, u32[]{:S(2)}) collective-permute-start(bf16[128,128]{1,0:T(8,128)(2,1)} %own_ref.1), channel_id=1, source_target_pairs={{0,17},{1,16},{2,19},{3,18},{4,21},{5,20},{6,23},{7,22},{8,25},{9,... | collective-permute-start | bytes 98312 | tf_op jit(solution)/shard_map/ppermute | solution.py:258
  3.1 6.4 %collective-permute-start.2 = (bf16[128,128]{1,0:T(8,128)(2,1)}, bf16[128,128]{1,0:T(8,128)(2,1)S(1)}, u32[]{:S(2)}, u32[]{:S(2)}) collective-permute-start(bf16[128,128]{1,0:T(8,128)(2,1)} %own_ref.1), channel_id=1, source_target_pairs={{0,16},{1,18},{2,17},{3,20},{4,19},{5,22},{6,21},{7,24},{8,23},{9,... | collective-permute-start | bytes 98312 | tf_op jit(solution)/shard_map/ppermute | solution.py:258
  3.7 5.8 %collective-permute-start.1 = (bf16[128,128]{1,0:T(8,128)(2,1)}, bf16[128,128]{1,0:T(8,128)(2,1)S(1)}, u32[]{:S(2)}, u32[]{:S(2)}) collective-permute-start(bf16[128,128]{1,0:T(8,128)(2,1)} %own_ref.1), channel_id=1, source_target_pairs={{0,0},{1,2},{2,1},{3,4},{4,3},{5,6},{6,5},{7,8},{8,7},{9,10},{10,9... | collective-permute-start | bytes 98312 | tf_op jit(solution)/shard_map/ppermute | solution.py:258
  5.1 4.4 %collective-permute-start = (bf16[128,128]{1,0:T(8,128)(2,1)}, bf16[128,128]{1,0:T(8,128)(2,1)S(1)}, u32[]{:S(2)}, u32[]{:S(2)}) collective-permute-start(bf16[128,128]{1,0:T(8,128)(2,1)} %own_ref.1), channel_id=1, source_target_pairs={{0,1},{1,0},{2,3},{3,2},{4,5},{5,4},{6,7},{7,6},{8,9},{9,8},{10,11... | collective-permute-start | bytes 98312 | tf_op jit(solution)/shard_map/ppermute | solution.py:258
  7.1 2.4 %collective-permute-start.4 = (bf16[128,128]{1,0:T(8,128)(2,1)S(1)}, bf16[128,128]{1,0:T(8,128)(2,1)S(1)}, u32[]{:S(2)}, u32[]{:S(2)}) collective-permute-start(bf16[128,128]{1,0:T(8,128)(2,1)S(1)} %collective-permute-done.3.rest_3_), channel_id=1, source_target_pairs={{0,1},{1,0},{2,3},{3,2},{4,5},{5,4},{6,7},{7,6},{8,9},{9,8},{10,11... | collective-permute-start | bytes 98312 | tf_op jit(solution)/shard_map/ppermute | solution.py:258
  11.3 2.0 %collective-permute-start.5 = (f32[4,128,128]{2,1,0:T(8,128)S(1)}, f32[4,128,128]{2,1,0:T(8,128)S(1)}, u32[]{:S(2)}, u32[]{:S(2)}) collective-permute-start(f32[4,128,128]{2,1,0:T(8,128)S(1)} %get-tuple-element.14), channel_id=1, source_target_pairs={{0,1},{1,0},{2,3},{3,2},{4,5},{5,4},{6,7},{7,6},{8,9},{9,8},{10,11... | collective-permute-start | bytes 786440 | tf_op jit(solution)/shard_map/ppermute | solution.py:258
  12.1 5.8 %copy-start.1 = (bf16[8,128,128]{2,1,0:T(8,128)(2,1)S(1)}, bf16[8,128,128]{2,1,0:T(8,128)(2,1)}, u32[]{:S(2)}) copy-start(bf16[8,128,128]{2,1,0:T(8,128)(2,1)} %filt_ref.1) | copy-start | bytes 786436
  12.1 5.8 %copy-start.4 = (bf16[1024,256]{1,0:T(8,128)(2,1)S(1)}, bf16[1024,256]{1,0:T(8,128)(2,1)}, u32[]{:S(2)}) copy-start(bf16[1024,256]{1,0:T(8,128)(2,1)} %constant.27.clone.back_ref) | copy-start | bytes 1572868
  13.3 7.2 %collective-permute-start.6 = (f32[128,128]{1,0:T(8,128)S(1)}, f32[128,128]{1,0:T(8,128)S(1)}, u32[]{:S(2)}, u32[]{:S(2)}) collective-permute-start(f32[128,128]{1,0:T(8,128)S(1)} %get-tuple-element.16), channel_id=1, source_target_pairs={{0,18},{1,19},{2,16},{3,17},{4,22},{5,23},{6,20},{7,21},{8,26},{9,... | collective-permute-start | bytes 196616 | tf_op jit(solution)/shard_map/ppermute | solution.py:258
  17.2 4.3 %collective-permute-start.7 = (f32[128,128]{1,0:T(8,128)S(1)}, f32[128,128]{1,0:T(8,128)S(1)}, u32[]{:S(2)}, u32[]{:S(2)}) collective-permute-start(f32[128,128]{1,0:T(8,128)S(1)} %get-tuple-element.17), channel_id=1, source_target_pairs={{0,16},{1,17},{2,18},{3,19},{4,20},{5,21},{6,22},{7,23},{8,24},{9,... | collective-permute-start | bytes 196616 | tf_op jit(solution)/shard_map/ppermute | solution.py:258
  17.7 4.3 %collective-permute-start.8 = (f32[128,128]{1,0:T(8,128)S(1)}, f32[128,128]{1,0:T(8,128)S(1)}, u32[]{:S(2)}, u32[]{:S(2)}) collective-permute-start(f32[128,128]{1,0:T(8,128)S(1)} %get-tuple-element.18), channel_id=1, source_target_pairs={{0,2},{1,3},{2,0},{3,1},{4,6},{5,7},{6,4},{7,5},{8,10},{9,11},{10,... | collective-permute-start | bytes 196616 | tf_op jit(solution)/shard_map/ppermute | solution.py:258
  22.0 7.5 %collective-permute-start.14 = (f32[128,128]{1,0:T(8,128)S(1)}, f32[128,128]{1,0:T(8,128)S(1)}, u32[]{:S(2)}, u32[]{:S(2)}) collective-permute-start(f32[128,128]{1,0:T(8,128)S(1)} %add_add_fusion.1), channel_id=1, source_target_pairs={{0,12},{1,13},{2,14},{3,15},{4,8},{5,9},{6,10},{7,11},{8,4},{9,5},... | collective-permute-start | bytes 196616 | tf_op jit(solution)/shard_map/ppermute | solution.py:258
  24.8 5.9 %collective-permute-start.13 = (f32[128,128]{1,0:T(8,128)S(1)}, f32[128,128]{1,0:T(8,128)S(1)}, u32[]{:S(2)}, u32[]{:S(2)}) collective-permute-start(f32[128,128]{1,0:T(8,128)S(1)} %add_add_fusion.1), channel_id=1, source_target_pairs={{0,8},{1,9},{2,10},{3,11},{4,12},{5,13},{6,14},{7,15},{8,0},{9,1},... | collective-permute-start | bytes 196616 | tf_op jit(solution)/shard_map/ppermute | solution.py:258
  25.1 5.6 %collective-permute-start.12 = (f32[128,128]{1,0:T(8,128)S(1)}, f32[128,128]{1,0:T(8,128)S(1)}, u32[]{:S(2)}, u32[]{:S(2)}) collective-permute-start(f32[128,128]{1,0:T(8,128)S(1)} %add_add_fusion.1), channel_id=1, source_target_pairs={{0,4},{1,5},{2,6},{3,7},{4,0},{5,1},{6,2},{7,3},{8,12},{9,13},{10,... | collective-permute-start | bytes 196616 | tf_op jit(solution)/shard_map/ppermute | solution.py:258
  26.5 7.8 %collective-permute-start.10 = (f32[192,128]{1,0:T(8,128)S(1)}, f32[192,128]{1,0:T(8,128)S(1)}, u32[]{:S(2)}, u32[]{:S(2)}) collective-permute-start(f32[192,128]{1,0:T(8,128)S(1)} %get-tuple-element.20), channel_id=1, source_target_pairs={{0,0},{1,2},{2,1},{3,4},{4,3},{5,6},{6,5},{7,8},{8,7},{9,10},{10,9... | collective-permute-start | bytes 294920 | tf_op jit(solution)/shard_map/ppermute | solution.py:258
  27.2 7.1 %collective-permute-start.9 = (f32[192,128]{1,0:T(8,128)S(1)}, f32[192,128]{1,0:T(8,128)S(1)}, u32[]{:S(2)}, u32[]{:S(2)}) collective-permute-start(f32[192,128]{1,0:T(8,128)S(1)} %get-tuple-element.20), channel_id=1, source_target_pairs={{0,1},{1,0},{2,3},{3,2},{4,5},{5,4},{6,7},{7,6},{8,9},{9,8},{10,11... | collective-permute-start | bytes 294920 | tf_op jit(solution)/shard_map/ppermute | solution.py:258
  30.7 5.8 %collective-permute-start.17 = (f32[128,128]{1,0:T(8,128)S(1)}, f32[128,128]{1,0:T(8,128)S(1)}, u32[]{:S(2)}, u32[]{:S(2)}) collective-permute-start(f32[128,128]{1,0:T(8,128)S(1)} %add_add_fusion), channel_id=1, source_target_pairs={{0,18},{1,19},{2,16},{3,17},{4,22},{5,23},{6,20},{7,21},{8,26},{9,... | collective-permute-start | bytes 196616 | tf_op jit(solution)/shard_map/ppermute | solution.py:258
  32.5 4.8 %collective-permute-start.16 = (f32[128,128]{1,0:T(8,128)S(1)}, f32[128,128]{1,0:T(8,128)S(1)}, u32[]{:S(2)}, u32[]{:S(2)}) collective-permute-start(f32[128,128]{1,0:T(8,128)S(1)} %add_add_fusion), channel_id=1, source_target_pairs={{0,16},{1,17},{2,18},{3,19},{4,20},{5,21},{6,22},{7,23},{8,24},{9,... | collective-permute-start | bytes 196616 | tf_op jit(solution)/shard_map/ppermute | solution.py:258
  33.7 4.3 %collective-permute-start.15 = (f32[128,128]{1,0:T(8,128)S(1)}, f32[128,128]{1,0:T(8,128)S(1)}, u32[]{:S(2)}, u32[]{:S(2)}) collective-permute-start(f32[128,128]{1,0:T(8,128)S(1)} %add_add_fusion), channel_id=1, source_target_pairs={{0,2},{1,3},{2,0},{3,1},{4,6},{5,7},{6,4},{7,5},{8,10},{9,11},{10,... | collective-permute-start | bytes 196616 | tf_op jit(solution)/shard_map/ppermute | solution.py:258
  34.3 4.0 %collective-permute-start.11 = (f32[64,128]{1,0:T(8,128)S(1)}, f32[64,128]{1,0:T(8,128)S(1)}, u32[]{:S(2)}, u32[]{:S(2)}) collective-permute-start(f32[64,128]{1,0:T(8,128)S(1)} %slice.49), channel_id=1, source_target_pairs={{0,16},{1,17},{2,18},{3,19},{4,20},{5,21},{6,22},{7,23},{8,24},{9,... | collective-permute-start | bytes 98312 | tf_op jit(solution)/shard_map/ppermute | solution.py:258
  36.1 2.9 %collective-permute-start.18 = (f32[128,128]{1,0:T(8,128)S(1)}, f32[128,128]{1,0:T(8,128)S(1)}, u32[]{:S(2)}, u32[]{:S(2)}) collective-permute-start(f32[128,128]{1,0:T(8,128)S(1)} %add_add_fusion), channel_id=1, source_target_pairs={{0,1},{1,0},{2,3},{3,2},{4,5},{5,4},{6,7},{7,6},{8,9},{9,8},{10,11... | collective-permute-start | bytes 196616 | tf_op jit(solution)/shard_map/ppermute | solution.py:258
  36.5 2.5 %collective-permute-start.21 = (f32[128,128]{1,0:T(8,128)S(1)}, f32[128,128]{1,0:T(8,128)S(1)}, u32[]{:S(2)}, u32[]{:S(2)}) collective-permute-start(f32[128,128]{1,0:T(8,128)S(1)} %collective-permute-done.17), channel_id=1, source_target_pairs={{0,1},{1,0},{2,3},{3,2},{4,5},{5,4},{6,7},{7,6},{8,9},{9,8},{10,11... | collective-permute-start | bytes 196616 | tf_op jit(solution)/shard_map/ppermute | solution.py:258
  37.2 1.8 %collective-permute-start.20 = (f32[128,128]{1,0:T(8,128)S(1)}, f32[128,128]{1,0:T(8,128)S(1)}, u32[]{:S(2)}, u32[]{:S(2)}) collective-permute-start(f32[128,128]{1,0:T(8,128)S(1)} %collective-permute-done.16), channel_id=1, source_target_pairs={{0,1},{1,0},{2,3},{3,2},{4,5},{5,4},{6,7},{7,6},{8,9},{9,8},{10,11... | collective-permute-start | bytes 196616 | tf_op jit(solution)/shard_map/ppermute | solution.py:258
  38.0 1.3 %collective-permute-start.19 = (f32[128,128]{1,0:T(8,128)S(1)}, f32[128,128]{1,0:T(8,128)S(1)}, u32[]{:S(2)}, u32[]{:S(2)}) collective-permute-start(f32[128,128]{1,0:T(8,128)S(1)} %collective-permute-done.15), channel_id=1, source_target_pairs={{0,1},{1,0},{2,3},{3,2},{4,5},{5,4},{6,7},{7,6},{8,9},{9,8},{10,11... | collective-permute-start | bytes 196616 | tf_op jit(solution)/shard_map/ppermute | solution.py:258
  (4 other events, 6.0 us)

commit v6 on v5

--- a/solution.py
+++ b/solution.py
@@ -130,13 +130,19 @@
 def cotangent_kernel(cot_ref, table_ref, out_ref):
     count, radius = cot_ref.shape[0], cot_ref.shape[1]
     table = table_ref[...]
+    rows, cols = table[: 2 * radius], table[2 * radius :]
+    parts = []
     for f in range(0, count, 2):
-        spectra = near_spectra(cot_ref[f], cot_ref[f + 1], table, radius)
-        for g, (plus, minus) in enumerate(spectra):
-            out_ref[f + g, 0] = plus[0]
-            out_ref[f + g, 1] = plus[1]
-            out_ref[f + g, 2] = minus[0]
-            out_ref[f + g, 3] = minus[1]
+        pair = jnp.concatenate([cot_ref[f], cot_ref[f + 1]], axis=1)
+        hi, lo = split(dot(rows, jnp.concatenate([pair, pair], axis=0)))
+        for place in (slice(0, radius), slice(radius, 2 * radius)):
+            parts.append(jnp.concatenate([hi[:, place], lo[:, place], hi[:, place]], axis=1))
+    spectra = [butterfly(dot(part, cols), radius) for part in parts]
+    for f, (plus, minus) in enumerate(spectra):
+        out_ref[f, 0] = plus[0]
+        out_ref[f, 1] = plus[1]
+        out_ref[f, 2] = minus[0]
+        out_ref[f, 3] = minus[1]
 
 
 def window_of(own, pieces, place_ref):
@@ -199,9 +205,9 @@
     hi, lo = split(mixed)
     mixed = dot(jnp.concatenate([hi, lo, hi], axis=1), table_ref[2 * side : 5 * side])
     plus, minus = butterfly(mixed, radius)
+    filter_gradients(place_ref, spec_ref, plus + minus, table_ref, 5 * side, True, out_ref)
     for n, part in enumerate(plus + minus):
         window_ref[n] = part
-    filter_gradients(place_ref, spec_ref, plus + minus, table_ref, 5 * side, True, out_ref)
 
 
 def keep_kernel(place_ref, spec_ref, window_ref, table_ref, out_ref):
@@ -354,7 +360,7 @@
         )
     low_col = lax.broadcasted_iota(jnp.int32, tall.shape, 1) < radius // 2
     other = jnp.where((col_index == 0) | (col_index == along - 1), 0.0, beside[1])
-    own = own + jnp.where(low_col == (col_index & 1 == 1), beside[0], other)
+    own = own + jnp.where(low_col != (col_index & 1 == 1), other, beside[0])
     strips = [move(own[radius:], to(row, stay)) for row in row_moves]
     parts = [value] + [move(value, flips[n]) for n in range(1, 4)]
     parts += [move(part, lambda a, b: (a, b ^ 1)) for part in parts]

time: 40.5 us -> 40.3 us (level)
  waiting for transfers between devices: 4.91 us -> 7.59 us
  starting transfers between devices: 24.4 us -> 21.8 us
  Pallas kernels: 7.18 us -> 6.76 us
    ppermute x22, waiting for transfers between devices: 4.91 us -> 7.59 us  [move(): return lax.ppermute(value, AXES, pairs)]
    ppermute x22, starting transfers between devices: 24.4 us -> 21.8 us  [move(): return lax.ppermute(value, AXES, pairs)]
    pallas_call x5, Pallas kernels: 7.18 us -> 6.76 us  [call(): pl.pallas_call(kernel, out_shape=outs, in_specs=[SMEM] * scalars + [VMEM]...]
  transfers between devices with their start and end apart: 22 -> 22, of which waited for: 8 -> 9; matrix products, arithmetic and copies ran while one was open for 2% -> 2% of each run, Pallas kernels for 13% -> 12%
where the time goes in v6:
time: 40.3 us; the launch traced here: 40.1 us
  starting transfers between devices  21.8 us (54%)
  waiting for transfers between devices  7.59 us (19%)
  Pallas kernels  6.76 us (17%)
  local copies, waits for them, and re-layouts  2.02 us (5%)
  other arithmetic  1 us (2%)
  between operations  0.85 us (2%)
    ppermute x22, starting transfers between devices, move(): return lax.ppermute(value, AXES, pairs)  21.8 us
    ppermute x22, waiting for transfers between devices, move(): return lax.ppermute(value, AXES, pairs)  7.59 us
    pallas_call x5, Pallas kernels, call(): pl.pallas_call(kernel, out_shape=outs, in_specs=[SMEM] * scalars + [VMEM]...  6.76 us
    unnamed x12, local copies, waits for them, and re-layouts  1.93 us
  transfers between devices with their start and end apart: 22, of which 9 were waited for; matrix products, arithmetic and copies ran while one was open for 2% of the time, Pallas kernels for 12%

profile of v6, /device:TPU:0, one launch (start us, length us, event | category | flops | bytes accessed | tf_op | source)
XLA Modules:
  0.0 40.1 jit_solution(11166000861435910993)
XLA Ops:
  0.6 2.5 %collective-permute-start.3 = (bf16[128,128]{1,0:T(8,128)(2,1)}, bf16[128,128]{1,0:T(8,128)(2,1)S(1)}, u32[]{:S(2)}, u32[]{:S(2)}) collective-permute-start(bf16[128,128]{1,0:T(8,128)(2,1)} %own_ref.1), channel_id=1, source_target_pairs={{0,17},{1,16},{2,19},{3,18},{4,21},{5,20},{6,23},{7,22},{8,25},{9,... | collective-permute-start | bytes 98312 | tf_op jit(solution)/shard_map/ppermute | solution.py:264
  3.7 1.4 %collective-permute-start.1 = (bf16[128,128]{1,0:T(8,128)(2,1)}, bf16[128,128]{1,0:T(8,128)(2,1)S(1)}, u32[]{:S(2)}, u32[]{:S(2)}) collective-permute-start(bf16[128,128]{1,0:T(8,128)(2,1)} %own_ref.1), channel_id=1, source_target_pairs={{0,0},{1,2},{2,1},{3,4},{4,3},{5,6},{6,5},{7,8},{8,7},{9,10},{10,9... | collective-permute-start | bytes 98312 | tf_op jit(solution)/shard_map/ppermute | solution.py:264
  5.1 1.6 %collective-permute-start = (bf16[128,128]{1,0:T(8,128)(2,1)}, bf16[128,128]{1,0:T(8,128)(2,1)S(1)}, u32[]{:S(2)}, u32[]{:S(2)}) collective-permute-start(bf16[128,128]{1,0:T(8,128)(2,1)} %own_ref.1), channel_id=1, source_target_pairs={{0,1},{1,0},{2,3},{3,2},{4,5},{5,4},{6,7},{7,6},{8,9},{9,8},{10,11... | collective-permute-start | bytes 98312 | tf_op jit(solution)/shard_map/ppermute | solution.py:264
  7.2 0.9 %copy-done = bf16[8,128,128]{2,1,0:T(8,128)(2,1)S(1)} copy-done((bf16[8,128,128]{2,1,0:T(8,128)(2,1)S(1)}, bf16[8,128,128]{2,1,0:T(8,128)(2,1)}, u32[]{:S(2)}) %copy-start) | copy-done | bytes 262168
  8.1 0.8 %cotangent_spectra.1.spec_ref = f32[8,4,128,128]{3,2,1,0:T(8,128)S(1)} custom-call(bf16[8,128,128]{2,1,0:T(8,128)(2,1)S(1)} %copy-done, bf16[640,256]{1,0:T(8,128)(2,1)S(1)} %near_table.1.table_ref), custom_call_target="tpu_custom_call" | custom-call | flops 1468006400 | bytes 589824 | tf_op jit(solution)/shard_map/cotangent_spectra/pallas_call | solution.py:289
  9.3 1.8 %filters_send.1 = (f32[4,128,128]{2,1,0:T(8,128)S(1)}, f32[4,128,128]{2,1,0:T(8,128)S(1)}) custom-call(s32[6]{0:T(128)S(1)} %stack.59.place_ref, f32[8,4,128,128]{3,2,1,0:T(8,128)S(1)} %cotangent_spectra.1.spec_ref, bf16[128,128]{1,0:T(8,128)(2,1)S(1)} %copy-done.2, bf16[128,128]{1,0:T(8,128)(2,1)S(1)} %collective-permute-done.rest_0_, ...), custom_call_target="tpu_custom_call" | custom-call | flops 2306867200 | bytes 3211288 | tf_op jit(solution)/shard_map/filters_send/pallas_call | solution.py:289
  11.1 1.0 %collective-permute-start.5 = (f32[4,128,128]{2,1,0:T(8,128)S(1)}, f32[4,128,128]{2,1,0:T(8,128)S(1)}, u32[]{:S(2)}, u32[]{:S(2)}) collective-permute-start(f32[4,128,128]{2,1,0:T(8,128)S(1)} %get-tuple-element.14), channel_id=1, source_target_pairs={{0,1},{1,0},{2,3},{3,2},{4,5},{5,4},{6,7},{7,6},{8,9},{9,8},{10,11... | collective-permute-start | bytes 786440 | tf_op jit(solution)/shard_map/ppermute | solution.py:264
  12.1 1.2 %filters_keep.1 = f32[4,128,128]{2,1,0:T(8,128)S(1)} custom-call(s32[6]{0:T(128)S(1)} %stack.59.place_ref, f32[8,4,128,128]{3,2,1,0:T(8,128)S(1)} %cotangent_spectra.1.spec_ref, f32[4,128,128]{2,1,0:T(8,128)S(1)} %get-tuple-element.13.window_ref, bf16[1792,256]{1,0:T(8,128)(2,1)S(1)} %copy-done.3), custom_call_target="tpu_custom_call" | custom-call | flops 1677721600 | bytes 3276824 | tf_op jit(solution)/shard_map/filters_keep/pallas_call | solution.py:289
  13.3 3.6 %collective-permute-start.6 = (f32[128,128]{1,0:T(8,128)S(1)}, f32[128,128]{1,0:T(8,128)S(1)}, u32[]{:S(2)}, u32[]{:S(2)}) collective-permute-start(f32[128,128]{1,0:T(8,128)S(1)} %get-tuple-element.16), channel_id=1, source_target_pairs={{0,18},{1,19},{2,16},{3,17},{4,22},{5,23},{6,20},{7,21},{8,26},{9,... | collective-permute-start | bytes 196616 | tf_op jit(solution)/shard_map/ppermute | solution.py:264
  17.6 2.6 %grad_input.1 = (f32[192,128]{1,0:T(8,128)S(1)}, f32[192,128]{1,0:T(8,128)S(1)}) custom-call(s32[6]{0:T(128)S(1)} %stack.59.place_ref, f32[8,4,128,128]{3,2,1,0:T(8,128)S(1)} %cotangent_spectra.1.spec_ref, bf16[8,128,128]{2,1,0:T(8,128)(2,1)S(1)} %copy-done.1, bf16[640,256]{1,0:T(8,128)(2,1)S(1)} %near_table.1.table_ref, bf16[1024,256]{1,0:T(8,128)(2,1)S(1)} %copy-done.4), custom_call_target="tpu_custom_call" | custom-call | flops 2726297600 | bytes 3211288 | tf_op jit(solution)/shard_map/grad_input/pallas_call | solution.py:289
  20.3 1.0 %collective-permute-done.7 = f32[128,128]{1,0:T(8,128)S(1)} collective-permute-done((f32[128,128]{1,0:T(8,128)S(1)}, f32[128,128]{1,0:T(8,128)S(1)}, u32[]{:S(2)}, u32[]{:S(2)}) %collective-permute-start.7) | collective-permute-done | bytes 65568 | tf_op jit(solution)/shard_map/ppermute | solution.py:264
  21.8 3.0 %collective-permute-start.14 = (f32[128,128]{1,0:T(8,128)S(1)}, f32[128,128]{1,0:T(8,128)S(1)}, u32[]{:S(2)}, u32[]{:S(2)}) collective-permute-start(f32[128,128]{1,0:T(8,128)S(1)} %add_add_fusion.1), channel_id=1, source_target_pairs={{0,12},{1,13},{2,14},{3,15},{4,8},{5,9},{6,10},{7,11},{8,4},{9,5},... | collective-permute-start | bytes 196616 | tf_op jit(solution)/shard_map/ppermute | solution.py:264
  24.9 1.3 %collective-permute-start.12 = (f32[128,128]{1,0:T(8,128)S(1)}, f32[128,128]{1,0:T(8,128)S(1)}, u32[]{:S(2)}, u32[]{:S(2)}) collective-permute-start(f32[128,128]{1,0:T(8,128)S(1)} %add_add_fusion.1), channel_id=1, source_target_pairs={{0,4},{1,5},{2,6},{3,7},{4,0},{5,1},{6,2},{7,3},{8,12},{9,13},{10,... | collective-permute-start | bytes 196616 | tf_op jit(solution)/shard_map/ppermute | solution.py:264
  26.2 0.7 %collective-permute-start.9 = (f32[192,128]{1,0:T(8,128)S(1)}, f32[192,128]{1,0:T(8,128)S(1)}, u32[]{:S(2)}, u32[]{:S(2)}) collective-permute-start(f32[192,128]{1,0:T(8,128)S(1)} %get-tuple-element.20), channel_id=1, source_target_pairs={{0,0},{1,2},{2,1},{3,4},{4,3},{5,6},{6,5},{7,8},{8,7},{9,10},{10,9... | collective-permute-start | bytes 294920 | tf_op jit(solution)/shard_map/ppermute | solution.py:264
  26.9 1.1 %collective-permute-done.14 = f32[128,128]{1,0:T(8,128)S(1)} collective-permute-done((f32[128,128]{1,0:T(8,128)S(1)}, f32[128,128]{1,0:T(8,128)S(1)}, u32[]{:S(2)}, u32[]{:S(2)}) %collective-permute-start.14) | collective-permute-done | bytes 65568 | tf_op jit(solution)/shard_map/ppermute | solution.py:264
  28.0 2.5 %collective-permute-done.13 = f32[128,128]{1,0:T(8,128)S(1)} collective-permute-done((f32[128,128]{1,0:T(8,128)S(1)}, f32[128,128]{1,0:T(8,128)S(1)}, u32[]{:S(2)}, u32[]{:S(2)}) %collective-permute-start.13) | collective-permute-done | bytes 65568 | tf_op jit(solution)/shard_map/ppermute | solution.py:264
  30.6 1.8 %collective-permute-start.17 = (f32[128,128]{1,0:T(8,128)S(1)}, f32[128,128]{1,0:T(8,128)S(1)}, u32[]{:S(2)}, u32[]{:S(2)}) collective-permute-start(f32[128,128]{1,0:T(8,128)S(1)} %add_add_fusion), channel_id=1, source_target_pairs={{0,18},{1,19},{2,16},{3,17},{4,22},{5,23},{6,20},{7,21},{8,26},{9,... | collective-permute-start | bytes 196616 | tf_op jit(solution)/shard_map/ppermute | solution.py:264
  32.4 1.1 %collective-permute-start.16 = (f32[128,128]{1,0:T(8,128)S(1)}, f32[128,128]{1,0:T(8,128)S(1)}, u32[]{:S(2)}, u32[]{:S(2)}) collective-permute-start(f32[128,128]{1,0:T(8,128)S(1)} %add_add_fusion), channel_id=1, source_target_pairs={{0,16},{1,17},{2,18},{3,19},{4,20},{5,21},{6,22},{7,23},{8,24},{9,... | collective-permute-start | bytes 196616 | tf_op jit(solution)/shard_map/ppermute | solution.py:264
  33.5 0.6 %collective-permute-start.15 = (f32[128,128]{1,0:T(8,128)S(1)}, f32[128,128]{1,0:T(8,128)S(1)}, u32[]{:S(2)}, u32[]{:S(2)}) collective-permute-start(f32[128,128]{1,0:T(8,128)S(1)} %add_add_fusion), channel_id=1, source_target_pairs={{0,2},{1,3},{2,0},{3,1},{4,6},{5,7},{6,4},{7,5},{8,10},{9,11},{10,... | collective-permute-start | bytes 196616 | tf_op jit(solution)/shard_map/ppermute | solution.py:264
  34.2 1.7 %collective-permute-start.11 = (f32[64,128]{1,0:T(8,128)S(1)}, f32[64,128]{1,0:T(8,128)S(1)}, u32[]{:S(2)}, u32[]{:S(2)}) collective-permute-start(f32[64,128]{1,0:T(8,128)S(1)} %slice.49), channel_id=1, source_target_pairs={{0,16},{1,17},{2,18},{3,19},{4,20},{5,21},{6,22},{7,23},{8,24},{9,... | collective-permute-start | bytes 98312 | tf_op jit(solution)/shard_map/ppermute | solution.py:264
  36.4 0.7 %collective-permute-done.16 = f32[128,128]{1,0:T(8,128)S(1)} collective-permute-done((f32[128,128]{1,0:T(8,128)S(1)}, f32[128,128]{1,0:T(8,128)S(1)}, u32[]{:S(2)}, u32[]{:S(2)}) %collective-permute-start.16) | collective-permute-done | bytes 65568 | tf_op jit(solution)/shard_map/ppermute | solution.py:264
  37.1 0.7 %collective-permute-done.15 = f32[128,128]{1,0:T(8,128)S(1)} collective-permute-done((f32[128,128]{1,0:T(8,128)S(1)}, f32[128,128]{1,0:T(8,128)S(1)}, u32[]{:S(2)}, u32[]{:S(2)}) %collective-permute-start.15) | collective-permute-done | bytes 65568 | tf_op jit(solution)/shard_map/ppermute | solution.py:264
  38.2 0.7 %slice_add_fusion = f32[128,128]{1,0:T(8,128)} fusion(f32[192,128]{1,0:T(8,128)S(1)} %select_add_fusion, f32[64,128]{1,0:T(8,128)S(1)} %collective-permute-done.11, pred[128]{0:T(512)(128)(4,1)S(1)} %compare_compare_fusion), kind=kLoop, calls=%fused_computation.1 | loop fusion | flops 49152 | bytes 163968 | tf_op jit(solution)/shard_map/add | solution.py:376
  39.3 0.8 %copy-done.5 = f32[8,128,128]{2,1,0:T(8,128)} copy-done((f32[8,128,128]{2,1,0:T(8,128)}, f32[8,128,128]{2,1,0:T(8,128)S(1)}, u32[]{:S(2)}) %copy-start.5) | copy-done | bytes 524312
  (54 shorter events, 4.0 us)
Async XLA Ops:
  0.6 6.4 %collective-permute-start.3 = (bf16[128,128]{1,0:T(8,128)(2,1)}, bf16[128,128]{1,0:T(8,128)(2,1)S(1)}, u32[]{:S(2)}, u32[]{:S(2)}) collective-permute-start(bf16[128,128]{1,0:T(8,128)(2,1)} %own_ref.1), channel_id=1, source_target_pairs={{0,17},{1,16},{2,19},{3,18},{4,21},{5,20},{6,23},{7,22},{8,25},{9,... | collective-permute-start | bytes 98312 | tf_op jit(solution)/shard_map/ppermute | solution.py:264
  3.1 6.0 %collective-permute-start.2 = (bf16[128,128]{1,0:T(8,128)(2,1)}, bf16[128,128]{1,0:T(8,128)(2,1)S(1)}, u32[]{:S(2)}, u32[]{:S(2)}) collective-permute-start(bf16[128,128]{1,0:T(8,128)(2,1)} %own_ref.1), channel_id=1, source_target_pairs={{0,16},{1,18},{2,17},{3,20},{4,19},{5,22},{6,21},{7,24},{8,23},{9,... | collective-permute-start | bytes 98312 | tf_op jit(solution)/shard_map/ppermute | solution.py:264
  3.7 5.4 %collective-permute-start.1 = (bf16[128,128]{1,0:T(8,128)(2,1)}, bf16[128,128]{1,0:T(8,128)(2,1)S(1)}, u32[]{:S(2)}, u32[]{:S(2)}) collective-permute-start(bf16[128,128]{1,0:T(8,128)(2,1)} %own_ref.1), channel_id=1, source_target_pairs={{0,0},{1,2},{2,1},{3,4},{4,3},{5,6},{6,5},{7,8},{8,7},{9,10},{10,9... | collective-permute-start | bytes 98312 | tf_op jit(solution)/shard_map/ppermute | solution.py:264
  5.1 4.0 %collective-permute-start = (bf16[128,128]{1,0:T(8,128)(2,1)}, bf16[128,128]{1,0:T(8,128)(2,1)S(1)}, u32[]{:S(2)}, u32[]{:S(2)}) collective-permute-start(bf16[128,128]{1,0:T(8,128)(2,1)} %own_ref.1), channel_id=1, source_target_pairs={{0,1},{1,0},{2,3},{3,2},{4,5},{5,4},{6,7},{7,6},{8,9},{9,8},{10,11... | collective-permute-start | bytes 98312 | tf_op jit(solution)/shard_map/ppermute | solution.py:264
  7.1 2.0 %collective-permute-start.4 = (bf16[128,128]{1,0:T(8,128)(2,1)S(1)}, bf16[128,128]{1,0:T(8,128)(2,1)S(1)}, u32[]{:S(2)}, u32[]{:S(2)}) collective-permute-start(bf16[128,128]{1,0:T(8,128)(2,1)S(1)} %collective-permute-done.3.rest_3_), channel_id=1, source_target_pairs={{0,1},{1,0},{2,3},{3,2},{4,5},{5,4},{6,7},{7,6},{8,9},{9,8},{10,11... | collective-permute-start | bytes 98312 | tf_op jit(solution)/shard_map/ppermute | solution.py:264
  11.1 2.2 %collective-permute-start.5 = (f32[4,128,128]{2,1,0:T(8,128)S(1)}, f32[4,128,128]{2,1,0:T(8,128)S(1)}, u32[]{:S(2)}, u32[]{:S(2)}) collective-permute-start(f32[4,128,128]{2,1,0:T(8,128)S(1)} %get-tuple-element.14), channel_id=1, source_target_pairs={{0,1},{1,0},{2,3},{3,2},{4,5},{5,4},{6,7},{7,6},{8,9},{9,8},{10,11... | collective-permute-start | bytes 786440 | tf_op jit(solution)/shard_map/ppermute | solution.py:264
  12.1 5.6 %copy-start.1 = (bf16[8,128,128]{2,1,0:T(8,128)(2,1)S(1)}, bf16[8,128,128]{2,1,0:T(8,128)(2,1)}, u32[]{:S(2)}) copy-start(bf16[8,128,128]{2,1,0:T(8,128)(2,1)} %filt_ref.1) | copy-start | bytes 786436
  12.1 5.6 %copy-start.4 = (bf16[1024,256]{1,0:T(8,128)(2,1)S(1)}, bf16[1024,256]{1,0:T(8,128)(2,1)}, u32[]{:S(2)}) copy-start(bf16[1024,256]{1,0:T(8,128)(2,1)} %constant.27.clone.back_ref) | copy-start | bytes 1572868
  13.3 6.9 %collective-permute-start.6 = (f32[128,128]{1,0:T(8,128)S(1)}, f32[128,128]{1,0:T(8,128)S(1)}, u32[]{:S(2)}, u32[]{:S(2)}) collective-permute-start(f32[128,128]{1,0:T(8,128)S(1)} %get-tuple-element.16), channel_id=1, source_target_pairs={{0,18},{1,19},{2,16},{3,17},{4,22},{5,23},{6,20},{7,21},{8,26},{9,... | collective-permute-start | bytes 196616 | tf_op jit(solution)/shard_map/ppermute | solution.py:264
  17.0 4.3 %collective-permute-start.7 = (f32[128,128]{1,0:T(8,128)S(1)}, f32[128,128]{1,0:T(8,128)S(1)}, u32[]{:S(2)}, u32[]{:S(2)}) collective-permute-start(f32[128,128]{1,0:T(8,128)S(1)} %get-tuple-element.17), channel_id=1, source_target_pairs={{0,16},{1,17},{2,18},{3,19},{4,20},{5,21},{6,22},{7,23},{8,24},{9,... | collective-permute-start | bytes 196616 | tf_op jit(solution)/shard_map/ppermute | solution.py:264
  17.5 4.3 %collective-permute-start.8 = (f32[128,128]{1,0:T(8,128)S(1)}, f32[128,128]{1,0:T(8,128)S(1)}, u32[]{:S(2)}, u32[]{:S(2)}) collective-permute-start(f32[128,128]{1,0:T(8,128)S(1)} %get-tuple-element.18), channel_id=1, source_target_pairs={{0,2},{1,3},{2,0},{3,1},{4,6},{5,7},{6,4},{7,5},{8,10},{9,11},{10,... | collective-permute-start | bytes 196616 | tf_op jit(solution)/shard_map/ppermute | solution.py:264
  21.8 6.2 %collective-permute-start.14 = (f32[128,128]{1,0:T(8,128)S(1)}, f32[128,128]{1,0:T(8,128)S(1)}, u32[]{:S(2)}, u32[]{:S(2)}) collective-permute-start(f32[128,128]{1,0:T(8,128)S(1)} %add_add_fusion.1), channel_id=1, source_target_pairs={{0,12},{1,13},{2,14},{3,15},{4,8},{5,9},{6,10},{7,11},{8,4},{9,5},... | collective-permute-start | bytes 196616 | tf_op jit(solution)/shard_map/ppermute | solution.py:264
  24.8 5.8 %collective-permute-start.13 = (f32[128,128]{1,0:T(8,128)S(1)}, f32[128,128]{1,0:T(8,128)S(1)}, u32[]{:S(2)}, u32[]{:S(2)}) collective-permute-start(f32[128,128]{1,0:T(8,128)S(1)} %add_add_fusion.1), channel_id=1, source_target_pairs={{0,8},{1,9},{2,10},{3,11},{4,12},{5,13},{6,14},{7,15},{8,0},{9,1},... | collective-permute-start | bytes 196616 | tf_op jit(solution)/shard_map/ppermute | solution.py:264
  24.9 5.7 %collective-permute-start.12 = (f32[128,128]{1,0:T(8,128)S(1)}, f32[128,128]{1,0:T(8,128)S(1)}, u32[]{:S(2)}, u32[]{:S(2)}) collective-permute-start(f32[128,128]{1,0:T(8,128)S(1)} %add_add_fusion.1), channel_id=1, source_target_pairs={{0,4},{1,5},{2,6},{3,7},{4,0},{5,1},{6,2},{7,3},{8,12},{9,13},{10,... | collective-permute-start | bytes 196616 | tf_op jit(solution)/shard_map/ppermute | solution.py:264
  26.2 7.9 %collective-permute-start.10 = (f32[192,128]{1,0:T(8,128)S(1)}, f32[192,128]{1,0:T(8,128)S(1)}, u32[]{:S(2)}, u32[]{:S(2)}) collective-permute-start(f32[192,128]{1,0:T(8,128)S(1)} %get-tuple-element.20), channel_id=1, source_target_pairs={{0,1},{1,0},{2,3},{3,2},{4,5},{5,4},{6,7},{7,6},{8,9},{9,8},{10,11... | collective-permute-start | bytes 294920 | tf_op jit(solution)/shard_map/ppermute | solution.py:264
  26.2 7.9 %collective-permute-start.9 = (f32[192,128]{1,0:T(8,128)S(1)}, f32[192,128]{1,0:T(8,128)S(1)}, u32[]{:S(2)}, u32[]{:S(2)}) collective-permute-start(f32[192,128]{1,0:T(8,128)S(1)} %get-tuple-element.20), channel_id=1, source_target_pairs={{0,0},{1,2},{2,1},{3,4},{4,3},{5,6},{6,5},{7,8},{8,7},{9,10},{10,9... | collective-permute-start | bytes 294920 | tf_op jit(solution)/shard_map/ppermute | solution.py:264
  30.6 5.8 %collective-permute-start.17 = (f32[128,128]{1,0:T(8,128)S(1)}, f32[128,128]{1,0:T(8,128)S(1)}, u32[]{:S(2)}, u32[]{:S(2)}) collective-permute-start(f32[128,128]{1,0:T(8,128)S(1)} %add_add_fusion), channel_id=1, source_target_pairs={{0,18},{1,19},{2,16},{3,17},{4,22},{5,23},{6,20},{7,21},{8,26},{9,... | collective-permute-start | bytes 196616 | tf_op jit(solution)/shard_map/ppermute | solution.py:264
  32.4 4.7 %collective-permute-start.16 = (f32[128,128]{1,0:T(8,128)S(1)}, f32[128,128]{1,0:T(8,128)S(1)}, u32[]{:S(2)}, u32[]{:S(2)}) collective-permute-start(f32[128,128]{1,0:T(8,128)S(1)} %add_add_fusion), channel_id=1, source_target_pairs={{0,16},{1,17},{2,18},{3,19},{4,20},{5,21},{6,22},{7,23},{8,24},{9,... | collective-permute-start | bytes 196616 | tf_op jit(solution)/shard_map/ppermute | solution.py:264
  33.5 4.3 %collective-permute-start.15 = (f32[128,128]{1,0:T(8,128)S(1)}, f32[128,128]{1,0:T(8,128)S(1)}, u32[]{:S(2)}, u32[]{:S(2)}) collective-permute-start(f32[128,128]{1,0:T(8,128)S(1)} %add_add_fusion), channel_id=1, source_target_pairs={{0,2},{1,3},{2,0},{3,1},{4,6},{5,7},{6,4},{7,5},{8,10},{9,11},{10,... | collective-permute-start | bytes 196616 | tf_op jit(solution)/shard_map/ppermute | solution.py:264
  34.2 4.0 %collective-permute-start.11 = (f32[64,128]{1,0:T(8,128)S(1)}, f32[64,128]{1,0:T(8,128)S(1)}, u32[]{:S(2)}, u32[]{:S(2)}) collective-permute-start(f32[64,128]{1,0:T(8,128)S(1)} %slice.49), channel_id=1, source_target_pairs={{0,16},{1,17},{2,18},{3,19},{4,20},{5,21},{6,22},{7,23},{8,24},{9,... | collective-permute-start | bytes 98312 | tf_op jit(solution)/shard_map/ppermute | solution.py:264
  35.8 3.0 %collective-permute-start.18 = (f32[128,128]{1,0:T(8,128)S(1)}, f32[128,128]{1,0:T(8,128)S(1)}, u32[]{:S(2)}, u32[]{:S(2)}) collective-permute-start(f32[128,128]{1,0:T(8,128)S(1)} %add_add_fusion), channel_id=1, source_target_pairs={{0,1},{1,0},{2,3},{3,2},{4,5},{5,4},{6,7},{7,6},{8,9},{9,8},{10,11... | collective-permute-start | bytes 196616 | tf_op jit(solution)/shard_map/ppermute | solution.py:264
  36.4 2.5 %collective-permute-start.21 = (f32[128,128]{1,0:T(8,128)S(1)}, f32[128,128]{1,0:T(8,128)S(1)}, u32[]{:S(2)}, u32[]{:S(2)}) collective-permute-start(f32[128,128]{1,0:T(8,128)S(1)} %collective-permute-done.17), channel_id=1, source_target_pairs={{0,1},{1,0},{2,3},{3,2},{4,5},{5,4},{6,7},{7,6},{8,9},{9,8},{10,11... | collective-permute-start | bytes 196616 | tf_op jit(solution)/shard_map/ppermute | solution.py:264
  37.1 1.8 %collective-permute-start.20 = (f32[128,128]{1,0:T(8,128)S(1)}, f32[128,128]{1,0:T(8,128)S(1)}, u32[]{:S(2)}, u32[]{:S(2)}) collective-permute-start(f32[128,128]{1,0:T(8,128)S(1)} %collective-permute-done.16), channel_id=1, source_target_pairs={{0,1},{1,0},{2,3},{3,2},{4,5},{5,4},{6,7},{7,6},{8,9},{9,8},{10,11... | collective-permute-start | bytes 196616 | tf_op jit(solution)/shard_map/ppermute | solution.py:264
  37.8 1.3 %collective-permute-start.19 = (f32[128,128]{1,0:T(8,128)S(1)}, f32[128,128]{1,0:T(8,128)S(1)}, u32[]{:S(2)}, u32[]{:S(2)}) collective-permute-start(f32[128,128]{1,0:T(8,128)S(1)} %collective-permute-done.15), channel_id=1, source_target_pairs={{0,1},{1,0},{2,3},{3,2},{4,5},{5,4},{6,7},{7,6},{8,9},{9,8},{10,11... | collective-permute-start | bytes 196616 | tf_op jit(solution)/shard_map/ppermute | solution.py:264
  (4 other events, 5.3 us)
